TPU v7x, 512 devices: a whole 4x4x16 slice. The times are simulated.
512 devices in a mesh: section: 32 (over z, core), tp: 16 (over y, x).
Axes of the slice: x: 4, y: 4, z: 16, core: 2. Of those that a mesh axis runs over, the one named last changes fastest.
Arguments:
- patches: bfloat16 [4, 64, 3200], P(None, None, 'tp'), may hold values from -6 to 6
- w_in: bfloat16 [32, 3200, 3200], P('section', 'tp'), may hold values from -0.109375 to 0.109375
- w_out: bfloat16 [32, 3200, 3200], P('section', 'tp'), may hold values from -0.078125 to 0.078125
- w_proj: bfloat16 [3200, 8192], P('tp', 'section'), may hold values from -0.109375 to 0.109375
Outputs:
- image_embeds: bfloat16 [256, 8192], P('tp', 'section')
All inputs are finite; a program needn't handle non-finite values.
Results may differ from a plain program's by a relative error of at most 0.035.
Values may be sent and summed in bfloat16 or wider, within the bound.
No kernel may reach another device: no remote copies, remote signals or barrier semaphores. Data moves between devices by JAX's collectives and lax.ppermute only.
A program may use at most 64 MiB of HBM per device.

v0:
```python
import jax
import jax.numpy as jnp
from jax import lax
from jax.sharding import PartitionSpec as P


def swapped(block, axis, distance):
    count = lax.axis_size(axis)
    route = []
    for low in range(count):
        high = low | 1 << distance
        if high != low and high < count:
            route += [(low, high), (high, low)]
    return lax.ppermute(block, axis, route)


def from_behind(array, axis, by):
    size = lax.axis_size(axis)
    pairs = [(i, i + by) for i in range(size) if 0 <= i + by < size]
    return lax.ppermute(array, axis, pairs)


def from_root(array, axis, root):
    mine = lax.axis_index(axis) == root
    return lax.psum(jnp.where(mine, array, jnp.zeros_like(array)), axis)


def contract_last(left, right):
    return lax.dot_general(
        left, right, (((1,), (1,)), ((), ())), preferred_element_type=jnp.float32
    )


def on_device(patches, w_in, w_out, w_proj):
    sections = lax.axis_size("section")
    layer_count = sections // 2
    section_index = lax.axis_index("section")
    pair_index = section_index // 2
    micro_count = patches.shape[0]
    row_count = patches.shape[1]
    columns = patches.shape[2]
    tick_count = micro_count + layer_count - 1
    up_local = w_in[0]
    down_local = w_out[0]

    def partial_of(current):
        whole = lax.all_gather(current, "tp", axis=1, tiled=True)
        values = whole.astype(jnp.float32)
        scale = lax.rsqrt(jnp.mean(values * values, axis=1, keepdims=True) + 1e-06)
        normed = (values * scale).astype(jnp.bfloat16)
        hidden = jax.nn.gelu(contract_last(normed, up_local)).astype(jnp.bfloat16)
        return contract_last(lax.all_gather(hidden, "tp", axis=1, tiled=True), down_local)

    def plan(tick):
        micro_index = tick - pair_index
        active = jnp.logical_and(micro_index >= 0, micro_index < micro_count)
        safe_index = jnp.clip(micro_index, 0, micro_count - 1)
        first_rows = lax.dynamic_index_in_dim(patches, safe_index, 0, keepdims=False)
        keep = jnp.logical_and(active, pair_index == layer_count - 1)
        return (safe_index, first_rows, keep)

    def one_tick(tick, carry):
        incoming, collected = carry
        safe_index, first_rows, keep = plan(tick)
        current = jnp.where(pair_index == 0, first_rows, incoming)
        partial_value = partial_of(current)
        branch = partial_value + swapped(partial_value, "section", 0)
        result = (current.astype(jnp.float32) + branch).astype(jnp.bfloat16)
        stored = lax.dynamic_update_index_in_dim(collected, result, safe_index, 0)
        collected = jnp.where(keep, stored, collected)
        passed = from_behind(result, "section", 2)
        return (passed, collected)

    begin = (jnp.zeros((row_count, columns), jnp.bfloat16), jnp.zeros(patches.shape, jnp.bfloat16))
    final_rows = lax.fori_loop(0, tick_count, one_tick, begin)[1]
    features = from_root(final_rows, "section", sections - 1)
    flat_rows = features.reshape(micro_count * row_count, columns)
    summed = lax.psum_scatter(
        jnp.dot(flat_rows, w_proj, preferred_element_type=jnp.float32),
        "tp",
        scatter_dimension=0,
        tiled=True,
    )
    return summed.astype(jnp.bfloat16)


def solution(mesh):
    return jax.shard_map(
        on_device,
        mesh=mesh,
        in_specs=(
            P(None, None, "tp"),
            P("section", "tp", None),
            P("section", "tp", None),
            P("tp", "section"),
        ),
        out_specs=P("tp", "section"),
        check_vma=False,
    )
```

profile of v0, /device:TPU:6, one launch (start us, length us, event | category | flops | bytes accessed | tf_op | source)
XLA Modules:
  0.0 1457.8 jit_solution(14999670827359744575)
XLA Ops:
  6.6 1150.2 %while.16 = (s32[]{:T(128)}, bf16[64,200]{1,0:T(8,128)(2,1)S(1)}, bf16[4,64,200]{2,1,0:T(8,128)(2,1)S(1)}, pred[]{:T(512)}, s32[]{:T(128)}, /*index=5*/bf16[4,64...) while((s32[]{:T(128)}, bf16[64,200]{1,0:T(8,128)(2,1)S(1)}, ...), condition=%wide.region_2.3_spmd, body=%wide.region_0.2_spmd.sunk | while | flops 164864064 | bytes 20973900 | solution.py:75
  7.4 26.7 %all-gather.4 = bf16[16,200,64]{1,2,0:T(8,128)(2,1)S(1)} all-gather(bf16[1,200,64]{1,2,0:T(8,128)(2,1)S(1)} %fusion.30), channel_id=1, replica_groups=mesh['section'=32,'tp'=16] {'tp'}, dimensions={0}, use_global_device_ids=true | all-gather | bytes 435200 | tf_op jit(solution)/shard_map/while/body/eval_jaxpr/all_gather | solution.py:47
  36.3 21.2 %all-gather.5 = bf16[16,200,64]{1,2,0:T(8,128)(2,1)S(1)} all-gather(bf16[1,200,64]{1,2,0:T(8,128)(2,1)S(1)} %fusion.31), channel_id=1, replica_groups=mesh['section'=32,'tp'=16] {'tp'}, dimensions={0}, use_global_device_ids=true | all-gather | bytes 435200 | tf_op jit(solution)/shard_map/while/body/eval_jaxpr/all_gather | solution.py:52
  59.0 2.0 collective-permute-start
  67.0 23.6 %all-gather.4 = bf16[16,200,64]{1,2,0:T(8,128)(2,1)S(1)} all-gather(bf16[1,200,64]{1,2,0:T(8,128)(2,1)S(1)} %fusion.30), channel_id=1, replica_groups=mesh['section'=32,'tp'=16] {'tp'}, dimensions={0}, use_global_device_ids=true | all-gather | bytes 435200 | tf_op jit(solution)/shard_map/while/body/eval_jaxpr/all_gather | solution.py:47
  92.9 21.6 %all-gather.5 = bf16[16,200,64]{1,2,0:T(8,128)(2,1)S(1)} all-gather(bf16[1,200,64]{1,2,0:T(8,128)(2,1)S(1)} %fusion.31), channel_id=1, replica_groups=mesh['section'=32,'tp'=16] {'tp'}, dimensions={0}, use_global_device_ids=true | all-gather | bytes 435200 | tf_op jit(solution)/shard_map/while/body/eval_jaxpr/all_gather | solution.py:52
  120.0 4.4 collective-permute-start.1
  126.8 23.4 %all-gather.4 = bf16[16,200,64]{1,2,0:T(8,128)(2,1)S(1)} all-gather(bf16[1,200,64]{1,2,0:T(8,128)(2,1)S(1)} %fusion.30), channel_id=1, replica_groups=mesh['section'=32,'tp'=16] {'tp'}, dimensions={0}, use_global_device_ids=true | all-gather | bytes 435200 | tf_op jit(solution)/shard_map/while/body/eval_jaxpr/all_gather | solution.py:47
  152.4 21.9 %all-gather.5 = bf16[16,200,64]{1,2,0:T(8,128)(2,1)S(1)} all-gather(bf16[1,200,64]{1,2,0:T(8,128)(2,1)S(1)} %fusion.31), channel_id=1, replica_groups=mesh['section'=32,'tp'=16] {'tp'}, dimensions={0}, use_global_device_ids=true | all-gather | bytes 435200 | tf_op jit(solution)/shard_map/while/body/eval_jaxpr/all_gather | solution.py:52
  179.8 4.4 collective-permute-start.1
  186.5 23.3 %all-gather.4 = bf16[16,200,64]{1,2,0:T(8,128)(2,1)S(1)} all-gather(bf16[1,200,64]{1,2,0:T(8,128)(2,1)S(1)} %fusion.30), channel_id=1, replica_groups=mesh['section'=32,'tp'=16] {'tp'}, dimensions={0}, use_global_device_ids=true | all-gather | bytes 435200 | tf_op jit(solution)/shard_map/while/body/eval_jaxpr/all_gather | solution.py:47
  212.0 21.9 %all-gather.5 = bf16[16,200,64]{1,2,0:T(8,128)(2,1)S(1)} all-gather(bf16[1,200,64]{1,2,0:T(8,128)(2,1)S(1)} %fusion.31), channel_id=1, replica_groups=mesh['section'=32,'tp'=16] {'tp'}, dimensions={0}, use_global_device_ids=true | all-gather | bytes 435200 | tf_op jit(solution)/shard_map/while/body/eval_jaxpr/all_gather | solution.py:52
  235.5 2.0 collective-permute-start
  239.5 4.2 collective-permute-start.1
  246.1 23.4 %all-gather.4 = bf16[16,200,64]{1,2,0:T(8,128)(2,1)S(1)} all-gather(bf16[1,200,64]{1,2,0:T(8,128)(2,1)S(1)} %fusion.30), channel_id=1, replica_groups=mesh['section'=32,'tp'=16] {'tp'}, dimensions={0}, use_global_device_ids=true | all-gather | bytes 435200 | tf_op jit(solution)/shard_map/while/body/eval_jaxpr/all_gather | solution.py:47
  271.7 21.9 %all-gather.5 = bf16[16,200,64]{1,2,0:T(8,128)(2,1)S(1)} all-gather(bf16[1,200,64]{1,2,0:T(8,128)(2,1)S(1)} %fusion.31), channel_id=1, replica_groups=mesh['section'=32,'tp'=16] {'tp'}, dimensions={0}, use_global_device_ids=true | all-gather | bytes 435200 | tf_op jit(solution)/shard_map/while/body/eval_jaxpr/all_gather | solution.py:52
  299.1 5.3 collective-permute-start.1
  306.7 23.2 %all-gather.4 = bf16[16,200,64]{1,2,0:T(8,128)(2,1)S(1)} all-gather(bf16[1,200,64]{1,2,0:T(8,128)(2,1)S(1)} %fusion.30), channel_id=1, replica_groups=mesh['section'=32,'tp'=16] {'tp'}, dimensions={0}, use_global_device_ids=true | all-gather | bytes 435200 | tf_op jit(solution)/shard_map/while/body/eval_jaxpr/all_gather | solution.py:47
  332.2 22.0 %all-gather.5 = bf16[16,200,64]{1,2,0:T(8,128)(2,1)S(1)} all-gather(bf16[1,200,64]{1,2,0:T(8,128)(2,1)S(1)} %fusion.31), channel_id=1, replica_groups=mesh['section'=32,'tp'=16] {'tp'}, dimensions={0}, use_global_device_ids=true | all-gather | bytes 435200 | tf_op jit(solution)/shard_map/while/body/eval_jaxpr/all_gather | solution.py:52
  359.7 5.4 collective-permute-start.1
  367.4 23.2 %all-gather.4 = bf16[16,200,64]{1,2,0:T(8,128)(2,1)S(1)} all-gather(bf16[1,200,64]{1,2,0:T(8,128)(2,1)S(1)} %fusion.30), channel_id=1, replica_groups=mesh['section'=32,'tp'=16] {'tp'}, dimensions={0}, use_global_device_ids=true | all-gather | bytes 435200 | tf_op jit(solution)/shard_map/while/body/eval_jaxpr/all_gather | solution.py:47
  392.9 22.0 %all-gather.5 = bf16[16,200,64]{1,2,0:T(8,128)(2,1)S(1)} all-gather(bf16[1,200,64]{1,2,0:T(8,128)(2,1)S(1)} %fusion.31), channel_id=1, replica_groups=mesh['section'=32,'tp'=16] {'tp'}, dimensions={0}, use_global_device_ids=true | all-gather | bytes 435200 | tf_op jit(solution)/shard_map/while/body/eval_jaxpr/all_gather | solution.py:52
  416.5 2.0 collective-permute-start
  420.4 5.5 collective-permute-start.1
  428.3 23.2 %all-gather.4 = bf16[16,200,64]{1,2,0:T(8,128)(2,1)S(1)} all-gather(bf16[1,200,64]{1,2,0:T(8,128)(2,1)S(1)} %fusion.30), channel_id=1, replica_groups=mesh['section'=32,'tp'=16] {'tp'}, dimensions={0}, use_global_device_ids=true | all-gather | bytes 435200 | tf_op jit(solution)/shard_map/while/body/eval_jaxpr/all_gather | solution.py:47
  453.8 22.0 %all-gather.5 = bf16[16,200,64]{1,2,0:T(8,128)(2,1)S(1)} all-gather(bf16[1,200,64]{1,2,0:T(8,128)(2,1)S(1)} %fusion.31), channel_id=1, replica_groups=mesh['section'=32,'tp'=16] {'tp'}, dimensions={0}, use_global_device_ids=true | all-gather | bytes 435200 | tf_op jit(solution)/shard_map/while/body/eval_jaxpr/all_gather | solution.py:52
  481.3 5.3 collective-permute-start.1
  489.0 23.2 %all-gather.4 = bf16[16,200,64]{1,2,0:T(8,128)(2,1)S(1)} all-gather(bf16[1,200,64]{1,2,0:T(8,128)(2,1)S(1)} %fusion.30), channel_id=1, replica_groups=mesh['section'=32,'tp'=16] {'tp'}, dimensions={0}, use_global_device_ids=true | all-gather | bytes 435200 | tf_op jit(solution)/shard_map/while/body/eval_jaxpr/all_gather | solution.py:47
  514.5 22.0 %all-gather.5 = bf16[16,200,64]{1,2,0:T(8,128)(2,1)S(1)} all-gather(bf16[1,200,64]{1,2,0:T(8,128)(2,1)S(1)} %fusion.31), channel_id=1, replica_groups=mesh['section'=32,'tp'=16] {'tp'}, dimensions={0}, use_global_device_ids=true | all-gather | bytes 435200 | tf_op jit(solution)/shard_map/while/body/eval_jaxpr/all_gather | solution.py:52
  542.0 5.3 collective-permute-start.1
  549.6 23.2 %all-gather.4 = bf16[16,200,64]{1,2,0:T(8,128)(2,1)S(1)} all-gather(bf16[1,200,64]{1,2,0:T(8,128)(2,1)S(1)} %fusion.30), channel_id=1, replica_groups=mesh['section'=32,'tp'=16] {'tp'}, dimensions={0}, use_global_device_ids=true | all-gather | bytes 435200 | tf_op jit(solution)/shard_map/while/body/eval_jaxpr/all_gather | solution.py:47
  575.1 22.0 %all-gather.5 = bf16[16,200,64]{1,2,0:T(8,128)(2,1)S(1)} all-gather(bf16[1,200,64]{1,2,0:T(8,128)(2,1)S(1)} %fusion.31), channel_id=1, replica_groups=mesh['section'=32,'tp'=16] {'tp'}, dimensions={0}, use_global_device_ids=true | all-gather | bytes 435200 | tf_op jit(solution)/shard_map/while/body/eval_jaxpr/all_gather | solution.py:52
  602.6 5.5 collective-permute-start.1
  610.5 23.1 %all-gather.4 = bf16[16,200,64]{1,2,0:T(8,128)(2,1)S(1)} all-gather(bf16[1,200,64]{1,2,0:T(8,128)(2,1)S(1)} %fusion.30), channel_id=1, replica_groups=mesh['section'=32,'tp'=16] {'tp'}, dimensions={0}, use_global_device_ids=true | all-gather | bytes 435200 | tf_op jit(solution)/shard_map/while/body/eval_jaxpr/all_gather | solution.py:47
  635.8 22.1 %all-gather.5 = bf16[16,200,64]{1,2,0:T(8,128)(2,1)S(1)} all-gather(bf16[1,200,64]{1,2,0:T(8,128)(2,1)S(1)} %fusion.31), channel_id=1, replica_groups=mesh['section'=32,'tp'=16] {'tp'}, dimensions={0}, use_global_device_ids=true | all-gather | bytes 435200 | tf_op jit(solution)/shard_map/while/body/eval_jaxpr/all_gather | solution.py:52
  659.5 2.0 collective-permute-start
  663.5 5.4 collective-permute-start.1
  671.2 23.0 %all-gather.4 = bf16[16,200,64]{1,2,0:T(8,128)(2,1)S(1)} all-gather(bf16[1,200,64]{1,2,0:T(8,128)(2,1)S(1)} %fusion.30), channel_id=1, replica_groups=mesh['section'=32,'tp'=16] {'tp'}, dimensions={0}, use_global_device_ids=true | all-gather | bytes 435200 | tf_op jit(solution)/shard_map/while/body/eval_jaxpr/all_gather | solution.py:47
  696.4 22.2 %all-gather.5 = bf16[16,200,64]{1,2,0:T(8,128)(2,1)S(1)} all-gather(bf16[1,200,64]{1,2,0:T(8,128)(2,1)S(1)} %fusion.31), channel_id=1, replica_groups=mesh['section'=32,'tp'=16] {'tp'}, dimensions={0}, use_global_device_ids=true | all-gather | bytes 435200 | tf_op jit(solution)/shard_map/while/body/eval_jaxpr/all_gather | solution.py:52
  720.2 2.0 collective-permute-start
  724.2 5.3 collective-permute-start.1
  731.9 23.0 %all-gather.4 = bf16[16,200,64]{1,2,0:T(8,128)(2,1)S(1)} all-gather(bf16[1,200,64]{1,2,0:T(8,128)(2,1)S(1)} %fusion.30), channel_id=1, replica_groups=mesh['section'=32,'tp'=16] {'tp'}, dimensions={0}, use_global_device_ids=true | all-gather | bytes 435200 | tf_op jit(solution)/shard_map/while/body/eval_jaxpr/all_gather | solution.py:47
  757.1 22.2 %all-gather.5 = bf16[16,200,64]{1,2,0:T(8,128)(2,1)S(1)} all-gather(bf16[1,200,64]{1,2,0:T(8,128)(2,1)S(1)} %fusion.31), channel_id=1, replica_groups=mesh['section'=32,'tp'=16] {'tp'}, dimensions={0}, use_global_device_ids=true | all-gather | bytes 435200 | tf_op jit(solution)/shard_map/while/body/eval_jaxpr/all_gather | solution.py:52
  784.8 5.4 collective-permute-start.1
  792.6 23.0 %all-gather.4 = bf16[16,200,64]{1,2,0:T(8,128)(2,1)S(1)} all-gather(bf16[1,200,64]{1,2,0:T(8,128)(2,1)S(1)} %fusion.30), channel_id=1, replica_groups=mesh['section'=32,'tp'=16] {'tp'}, dimensions={0}, use_global_device_ids=true | all-gather | bytes 435200 | tf_op jit(solution)/shard_map/while/body/eval_jaxpr/all_gather | solution.py:47
  817.8 22.3 %all-gather.5 = bf16[16,200,64]{1,2,0:T(8,128)(2,1)S(1)} all-gather(bf16[1,200,64]{1,2,0:T(8,128)(2,1)S(1)} %fusion.31), channel_id=1, replica_groups=mesh['section'=32,'tp'=16] {'tp'}, dimensions={0}, use_global_device_ids=true | all-gather | bytes 435200 | tf_op jit(solution)/shard_map/while/body/eval_jaxpr/all_gather | solution.py:52
  845.5 5.8 collective-permute-start.1
  853.7 22.7 %all-gather.4 = bf16[16,200,64]{1,2,0:T(8,128)(2,1)S(1)} all-gather(bf16[1,200,64]{1,2,0:T(8,128)(2,1)S(1)} %fusion.30), channel_id=1, replica_groups=mesh['section'=32,'tp'=16] {'tp'}, dimensions={0}, use_global_device_ids=true | all-gather | bytes 435200 | tf_op jit(solution)/shard_map/while/body/eval_jaxpr/all_gather | solution.py:47
  878.7 22.5 %all-gather.5 = bf16[16,200,64]{1,2,0:T(8,128)(2,1)S(1)} all-gather(bf16[1,200,64]{1,2,0:T(8,128)(2,1)S(1)} %fusion.31), channel_id=1, replica_groups=mesh['section'=32,'tp'=16] {'tp'}, dimensions={0}, use_global_device_ids=true | all-gather | bytes 435200 | tf_op jit(solution)/shard_map/while/body/eval_jaxpr/all_gather | solution.py:52
  906.7 5.3 collective-permute-start.1
  914.4 22.7 %all-gather.4 = bf16[16,200,64]{1,2,0:T(8,128)(2,1)S(1)} all-gather(bf16[1,200,64]{1,2,0:T(8,128)(2,1)S(1)} %fusion.30), channel_id=1, replica_groups=mesh['section'=32,'tp'=16] {'tp'}, dimensions={0}, use_global_device_ids=true | all-gather | bytes 435200 | tf_op jit(solution)/shard_map/while/body/eval_jaxpr/all_gather | solution.py:47
  939.4 22.5 %all-gather.5 = bf16[16,200,64]{1,2,0:T(8,128)(2,1)S(1)} all-gather(bf16[1,200,64]{1,2,0:T(8,128)(2,1)S(1)} %fusion.31), channel_id=1, replica_groups=mesh['section'=32,'tp'=16] {'tp'}, dimensions={0}, use_global_device_ids=true | all-gather | bytes 435200 | tf_op jit(solution)/shard_map/while/body/eval_jaxpr/all_gather | solution.py:52
  967.4 5.2 collective-permute-start.1
  975.0 22.9 %all-gather.4 = bf16[16,200,64]{1,2,0:T(8,128)(2,1)S(1)} all-gather(bf16[1,200,64]{1,2,0:T(8,128)(2,1)S(1)} %fusion.30), channel_id=1, replica_groups=mesh['section'=32,'tp'=16] {'tp'}, dimensions={0}, use_global_device_ids=true | all-gather | bytes 435200 | tf_op jit(solution)/shard_map/while/body/eval_jaxpr/all_gather | solution.py:47
  1000.2 22.3 %all-gather.5 = bf16[16,200,64]{1,2,0:T(8,128)(2,1)S(1)} all-gather(bf16[1,200,64]{1,2,0:T(8,128)(2,1)S(1)} %fusion.31), channel_id=1, replica_groups=mesh['section'=32,'tp'=16] {'tp'}, dimensions={0}, use_global_device_ids=true | all-gather | bytes 435200 | tf_op jit(solution)/shard_map/while/body/eval_jaxpr/all_gather | solution.py:52
  1027.9 5.6 collective-permute-start.1
  1035.8 23.2 %all-gather.4 = bf16[16,200,64]{1,2,0:T(8,128)(2,1)S(1)} all-gather(bf16[1,200,64]{1,2,0:T(8,128)(2,1)S(1)} %fusion.30), channel_id=1, replica_groups=mesh['section'=32,'tp'=16] {'tp'}, dimensions={0}, use_global_device_ids=true | all-gather | bytes 435200 | tf_op jit(solution)/shard_map/while/body/eval_jaxpr/all_gather | solution.py:47
  1061.3 22.0 %all-gather.5 = bf16[16,200,64]{1,2,0:T(8,128)(2,1)S(1)} all-gather(bf16[1,200,64]{1,2,0:T(8,128)(2,1)S(1)} %fusion.31), channel_id=1, replica_groups=mesh['section'=32,'tp'=16] {'tp'}, dimensions={0}, use_global_device_ids=true | all-gather | bytes 435200 | tf_op jit(solution)/shard_map/while/body/eval_jaxpr/all_gather | solution.py:52
  1088.8 5.7 collective-permute-start.1
  1096.8 22.9 %all-gather.4 = bf16[16,200,64]{1,2,0:T(8,128)(2,1)S(1)} all-gather(bf16[1,200,64]{1,2,0:T(8,128)(2,1)S(1)} %fusion.30), channel_id=1, replica_groups=mesh['section'=32,'tp'=16] {'tp'}, dimensions={0}, use_global_device_ids=true | all-gather | bytes 435200 | tf_op jit(solution)/shard_map/while/body/eval_jaxpr/all_gather | solution.py:47
  1122.0 22.3 %all-gather.5 = bf16[16,200,64]{1,2,0:T(8,128)(2,1)S(1)} all-gather(bf16[1,200,64]{1,2,0:T(8,128)(2,1)S(1)} %fusion.31), channel_id=1, replica_groups=mesh['section'=32,'tp'=16] {'tp'}, dimensions={0}, use_global_device_ids=true | all-gather | bytes 435200 | tf_op jit(solution)/shard_map/while/body/eval_jaxpr/all_gather | solution.py:52
  1149.8 5.4 collective-permute-start.1
  1157.5 204.7 %all-reduce.2.cloned.1.call-done = bf16[256,200]{1,0:T(8,128)(2,1)} async-done(((bf16[256,200]{1,0:T(8,128)(2,1)}), bf16[256,200]{1,0:T(8,128)(2,1)}) %all-reduce.2.cloned.1.call-update) | async-done | bytes 102416 | tf_op jit(solution)/shard_map/psum | solution.py:25
  1364.0 85.7 %reduce-scatter.2.cloned.1.call-done = f32[16,256]{1,0:T(8,128)} async-done(((f32[256,256]{1,0:T(8,128)}), f32[16,256]{1,0:T(8,128)}) %reduce-scatter.2.cloned.1.call-update) | async-done | bytes 16400 | tf_op jit(solution)/shard_map/reduce_scatter | solution.py:78
  (330 shorter events, 185.8 us)
Async XLA Ops:
  6.5 1355.7 %copy-start = (bf16[200,256]{1,0:T(8,128)(2,1)S(1)}, bf16[200,256]{1,0:T(8,128)(2,1)}, u32[]{:S(2)}) copy-start(bf16[200,256]{1,0:T(8,128)(2,1)} %param.9) | copy-start | bytes 307204
  6.5 1355.7 %all-reduce.2.cloned.1.call-start = ((), (), s32[]{:S(2)}) async-start(), calls=%async_computation.1 | async-start | bytes 262144 | tf_op jit(solution)/shard_map/psum | solution.py:25
  34.4 1.3 copy-start.1
  36.3 22.2 %copy-start.2 = (bf16[200,3200]{1,0:T(8,128)(2,1)S(1)}, bf16[200,3200]{1,0:T(8,128)(2,1)}, u32[]{:S(2)}) copy-start(bf16[200,3200]{1,0:T(8,128)(2,1)} %get-tuple-element.278) | copy-start | bytes 3840004 | tf_op jit(solution)/shard_map/while
  59.0 3.2 collective-permute-start
  63.0 3.3 collective-permute-start.1
  91.0 1.3 copy-start.1
  92.9 22.6 %copy-start.2 = (bf16[200,3200]{1,0:T(8,128)(2,1)S(1)}, bf16[200,3200]{1,0:T(8,128)(2,1)}, u32[]{:S(2)}) copy-start(bf16[200,3200]{1,0:T(8,128)(2,1)} %get-tuple-element.278) | copy-start | bytes 3840004 | tf_op jit(solution)/shard_map/while
  116.0 3.2 collective-permute-start
  120.0 6.0 collective-permute-start.1
  152.4 22.9 %copy-start.2 = (bf16[200,3200]{1,0:T(8,128)(2,1)S(1)}, bf16[200,3200]{1,0:T(8,128)(2,1)}, u32[]{:S(2)}) copy-start(bf16[200,3200]{1,0:T(8,128)(2,1)} %get-tuple-element.278) | copy-start | bytes 3840004 | tf_op jit(solution)/shard_map/while
  175.8 3.2 collective-permute-start
  179.8 6.0 collective-permute-start.1
  212.0 23.0 %copy-start.2 = (bf16[200,3200]{1,0:T(8,128)(2,1)S(1)}, bf16[200,3200]{1,0:T(8,128)(2,1)}, u32[]{:S(2)}) copy-start(bf16[200,3200]{1,0:T(8,128)(2,1)} %get-tuple-element.278) | copy-start | bytes 3840004 | tf_op jit(solution)/shard_map/while
  235.5 3.2 collective-permute-start
  239.5 5.8 collective-permute-start.1
  271.6 22.9 %copy-start.2 = (bf16[200,3200]{1,0:T(8,128)(2,1)S(1)}, bf16[200,3200]{1,0:T(8,128)(2,1)}, u32[]{:S(2)}) copy-start(bf16[200,3200]{1,0:T(8,128)(2,1)} %get-tuple-element.278) | copy-start | bytes 3840004 | tf_op jit(solution)/shard_map/while
  295.1 3.2 collective-permute-start
  299.1 6.8 collective-permute-start.1
  332.1 23.0 %copy-start.2 = (bf16[200,3200]{1,0:T(8,128)(2,1)S(1)}, bf16[200,3200]{1,0:T(8,128)(2,1)}, u32[]{:S(2)}) copy-start(bf16[200,3200]{1,0:T(8,128)(2,1)} %get-tuple-element.278) | copy-start | bytes 3840004 | tf_op jit(solution)/shard_map/while
  355.7 3.2 collective-permute-start
  359.7 7.0 collective-permute-start.1
  392.9 23.0 %copy-start.2 = (bf16[200,3200]{1,0:T(8,128)(2,1)S(1)}, bf16[200,3200]{1,0:T(8,128)(2,1)}, u32[]{:S(2)}) copy-start(bf16[200,3200]{1,0:T(8,128)(2,1)} %get-tuple-element.278) | copy-start | bytes 3840004 | tf_op jit(solution)/shard_map/while
  416.5 3.2 collective-permute-start
  420.4 7.1 collective-permute-start.1
  453.8 23.0 %copy-start.2 = (bf16[200,3200]{1,0:T(8,128)(2,1)S(1)}, bf16[200,3200]{1,0:T(8,128)(2,1)}, u32[]{:S(2)}) copy-start(bf16[200,3200]{1,0:T(8,128)(2,1)} %get-tuple-element.278) | copy-start | bytes 3840004 | tf_op jit(solution)/shard_map/while
  477.3 3.2 collective-permute-start
  481.3 6.9 collective-permute-start.1
  514.5 23.0 %copy-start.2 = (bf16[200,3200]{1,0:T(8,128)(2,1)S(1)}, bf16[200,3200]{1,0:T(8,128)(2,1)}, u32[]{:S(2)}) copy-start(bf16[200,3200]{1,0:T(8,128)(2,1)} %get-tuple-element.278) | copy-start | bytes 3840004 | tf_op jit(solution)/shard_map/while
  538.0 3.2 collective-permute-start
  542.0 6.9 collective-permute-start.1
  575.1 23.0 %copy-start.2 = (bf16[200,3200]{1,0:T(8,128)(2,1)S(1)}, bf16[200,3200]{1,0:T(8,128)(2,1)}, u32[]{:S(2)}) copy-start(bf16[200,3200]{1,0:T(8,128)(2,1)} %get-tuple-element.278) | copy-start | bytes 3840004 | tf_op jit(solution)/shard_map/while
  598.7 3.2 collective-permute-start
  602.6 7.1 collective-permute-start.1
  635.8 23.2 %copy-start.2 = (bf16[200,3200]{1,0:T(8,128)(2,1)S(1)}, bf16[200,3200]{1,0:T(8,128)(2,1)}, u32[]{:S(2)}) copy-start(bf16[200,3200]{1,0:T(8,128)(2,1)} %get-tuple-element.278) | copy-start | bytes 3840004 | tf_op jit(solution)/shard_map/while
  659.5 3.2 collective-permute-start
  663.5 7.0 collective-permute-start.1
  696.4 23.3 %copy-start.2 = (bf16[200,3200]{1,0:T(8,128)(2,1)S(1)}, bf16[200,3200]{1,0:T(8,128)(2,1)}, u32[]{:S(2)}) copy-start(bf16[200,3200]{1,0:T(8,128)(2,1)} %get-tuple-element.278) | copy-start | bytes 3840004 | tf_op jit(solution)/shard_map/while
  720.2 3.2 collective-permute-start
  724.2 6.9 collective-permute-start.1
  755.2 1.3 copy-start.1
  757.1 23.2 %copy-start.2 = (bf16[200,3200]{1,0:T(8,128)(2,1)S(1)}, bf16[200,3200]{1,0:T(8,128)(2,1)}, u32[]{:S(2)}) copy-start(bf16[200,3200]{1,0:T(8,128)(2,1)} %get-tuple-element.278) | copy-start | bytes 3840004 | tf_op jit(solution)/shard_map/while
  780.9 3.2 collective-permute-start
  784.8 7.0 collective-permute-start.1
  817.8 23.3 %copy-start.2 = (bf16[200,3200]{1,0:T(8,128)(2,1)S(1)}, bf16[200,3200]{1,0:T(8,128)(2,1)}, u32[]{:S(2)}) copy-start(bf16[200,3200]{1,0:T(8,128)(2,1)} %get-tuple-element.278) | copy-start | bytes 3840004 | tf_op jit(solution)/shard_map/while
  841.6 3.2 collective-permute-start
  845.5 7.4 collective-permute-start.1
  878.7 23.5 %copy-start.2 = (bf16[200,3200]{1,0:T(8,128)(2,1)S(1)}, bf16[200,3200]{1,0:T(8,128)(2,1)}, u32[]{:S(2)}) copy-start(bf16[200,3200]{1,0:T(8,128)(2,1)} %get-tuple-element.278) | copy-start | bytes 3840004 | tf_op jit(solution)/shard_map/while
  902.8 3.2 collective-permute-start
  906.7 6.9 collective-permute-start.1
  937.5 1.3 copy-start.1
  939.4 23.5 %copy-start.2 = (bf16[200,3200]{1,0:T(8,128)(2,1)S(1)}, bf16[200,3200]{1,0:T(8,128)(2,1)}, u32[]{:S(2)}) copy-start(bf16[200,3200]{1,0:T(8,128)(2,1)} %get-tuple-element.278) | copy-start | bytes 3840004 | tf_op jit(solution)/shard_map/while
  963.4 3.2 collective-permute-start
  967.4 6.8 collective-permute-start.1
  1000.2 23.3 %copy-start.2 = (bf16[200,3200]{1,0:T(8,128)(2,1)S(1)}, bf16[200,3200]{1,0:T(8,128)(2,1)}, u32[]{:S(2)}) copy-start(bf16[200,3200]{1,0:T(8,128)(2,1)} %get-tuple-element.278) | copy-start | bytes 3840004 | tf_op jit(solution)/shard_map/while
  1024.0 3.2 collective-permute-start
  1027.9 7.1 collective-permute-start.1
  1061.3 23.0 %copy-start.2 = (bf16[200,3200]{1,0:T(8,128)(2,1)S(1)}, bf16[200,3200]{1,0:T(8,128)(2,1)}, u32[]{:S(2)}) copy-start(bf16[200,3200]{1,0:T(8,128)(2,1)} %get-tuple-element.278) | copy-start | bytes 3840004 | tf_op jit(solution)/shard_map/while
  1084.8 3.2 collective-permute-start
  1088.8 7.3 collective-permute-start.1
  1122.0 23.3 %copy-start.2 = (bf16[200,3200]{1,0:T(8,128)(2,1)S(1)}, bf16[200,3200]{1,0:T(8,128)(2,1)}, u32[]{:S(2)}) copy-start(bf16[200,3200]{1,0:T(8,128)(2,1)} %get-tuple-element.278) | copy-start | bytes 3840004 | tf_op jit(solution)/shard_map/while
  1145.9 3.2 collective-permute-start
  1149.8 6.9 collective-permute-start.1
  1157.5 292.2 %reduce-scatter.2.cloned.1.call-start = ((), (), s32[]{:S(2)}) async-start(), calls=%async_computation.2 | async-start | bytes 278528 | tf_op jit(solution)/shard_map/reduce_scatter | solution.py:78
  (15 other events, 19.6 us)
Sparse Core Ops, SparseCore 0:
  1157.6 204.5 all-reduce.1
  1366.8 82.8 reduce-scatter.1
where the time goes:
time: 1460 us
  blocking collectives  862 us (59%)
  waiting for transfers between devices  343 us (23%)
  starting transfers between devices  133 us (9%)
  local copies, waits for them, and re-layouts  46.3 us (3%)
  other arithmetic  34.6 us (2%)
  matrix products  22.9 us (2%)
    all_gather x19, blocking collectives, partial_of(): whole = lax.all_gather(current, 'tp', axis=1, tiled=True)  443 us
    all_gather x19, blocking collectives, partial_of(): lax.all_gather(hidden, 'tp', axis=1, tiled=True)  419 us
    psum x1, waiting for transfers between devices, from_root(): return lax.psum(jnp.where(mine, array, jnp.zeros_like(array)), axis)  205 us
    ppermute x19, starting transfers between devices, from_behind(): return lax.ppermute(array, axis, pairs)  96.2 us
    reduce_scatter x1, waiting for transfers between devices, on_device(): lax.psum_scatter(jnp.dot(flat_rows, w_proj, preferred_element_type=jnp.fl...  85.7 us
    ppermute x19, starting transfers between devices, swapped(): return lax.ppermute(block, axis, route)  37.1 us
    ppermute x19, waiting for transfers between devices, from_behind(): return lax.ppermute(array, axis, pairs)  29.9 us
  transfers between devices with their start and end apart: 40, of which 40 were waited for; matrix products, arithmetic and copies ran while one was open for 0% of the time, Pallas kernels for 0%

commit v1 on v0

v1 whole, which is shorter than its diff:
```python
import functools

import jax
import jax.numpy as jnp
from jax import lax
from jax.experimental import pallas as pl
from jax.experimental.pallas import tpu as pltpu
from jax.sharding import Mesh, PartitionSpec as P

TILE = 640


def half_layer(first_ref, pair_ref, up_ref, down_ref, out_ref, hidden_ref):
    rows = pair_ref[0].astype(jnp.float32) + pair_ref[1].astype(jnp.float32)
    scale = lax.rsqrt(jnp.mean(rows * rows, axis=1, keepdims=True) + 1e-06)
    normed = (rows * scale).astype(jnp.bfloat16)
    units, width = up_ref.shape
    for start in range(0, units, TILE):
        part = lax.dot_general(
            normed,
            up_ref[start : start + TILE, :],
            (((1,), (1,)), ((), ())),
            preferred_element_type=jnp.float32,
        )
        hidden_ref[:, start : start + TILE] = jax.nn.gelu(part).astype(jnp.bfloat16)
    hidden = hidden_ref[...]
    keep = first_ref[0] == 1
    for start in range(0, width, TILE):
        part = lax.dot_general(
            hidden,
            down_ref[start : start + TILE, :],
            (((1,), (1,)), ((), ())),
            preferred_element_type=jnp.float32,
        )
        base = jnp.where(keep, rows[:, start : start + TILE], 0.0)
        out_ref[:, start : start + TILE] = (base + part).astype(jnp.bfloat16)


def apply_half(first, pair, up, down):
    _, row_count, width = pair.shape
    units = up.shape[0]
    return pl.pallas_call(
        half_layer,
        out_shape=jax.ShapeDtypeStruct((row_count, width), jnp.bfloat16),
        in_specs=[
            pl.BlockSpec(memory_space=pltpu.SMEM),
            pl.BlockSpec(memory_space=pltpu.VMEM),
            pl.BlockSpec(memory_space=pltpu.VMEM),
            pl.BlockSpec(memory_space=pltpu.VMEM),
        ],
        out_specs=pl.BlockSpec(memory_space=pltpu.VMEM),
        scratch_shapes=[pltpu.VMEM((row_count, units), jnp.bfloat16)],
        compiler_params=pltpu.CompilerParams(vmem_limit_bytes=10 * 2**20),
        cost_estimate=pl.CostEstimate(
            flops=4 * row_count * units * width,
            bytes_accessed=4 * units * width,
            transcendentals=row_count * units,
        ),
    )(first, pair, up, down)


def on_device(layers, patches, w_in, w_out, w_proj):
    plane = lax.axis_index("z")
    core = lax.axis_index("c")
    tp = ("y", "x")
    first = (core == 0).astype(jnp.int32).reshape(1)

    up = lax.all_gather(w_in[0], tp, axis=0, tiled=True)
    down = lax.all_gather(w_out[0], tp, axis=0, tiled=True)
    columns = lax.all_gather(w_proj, tp, axis=0, tiled=True)
    up = pltpu.with_memory_space_constraint(up, pltpu.VMEM)
    down = pltpu.with_memory_space_constraint(down, pltpu.VMEM)

    flat = patches.reshape(-1, patches.shape[2])
    mine = lax.all_to_all(flat, tp, split_axis=0, concat_axis=1, tiled=True)
    pair = jnp.stack([mine, jnp.zeros_like(mine)])
    for layer in range(layers):
        part = apply_half(first, pair, up, down)
        if layer < layers - 1:
            part = lax.ppermute(part, "z", [(layer, layer + 1)])
        pair = lax.all_gather(part, "c", axis=0, tiled=False)

    total = pair[0].astype(jnp.float32) + pair[1].astype(jnp.float32)
    rows = jnp.where(plane == layers - 1, total, 0.0).astype(jnp.bfloat16)
    holders = [layers - 1]
    step = layers // 2
    while step:
        route = [(held, (held + step) % layers) for held in holders]
        rows = rows + lax.ppermute(rows, "z", route)
        holders += [target for _, target in route]
        step //= 2
    return jnp.dot(rows, columns, preferred_element_type=jnp.float32).astype(jnp.bfloat16)


def solution(mesh):
    sections = mesh.shape["section"]
    grid = Mesh(mesh.devices.reshape(sections // 2, 2, 4, 4), ("z", "c", "y", "x"))
    section, tp = ("z", "c"), ("y", "x")
    return jax.shard_map(
        functools.partial(on_device, sections // 2),
        mesh=grid,
        in_specs=(
            P(None, None, tp),
            P(section, tp, None),
            P(section, tp, None),
            P(tp, section),
        ),
        out_specs=P(tp, section),
        check_vma=False,
    )
```

time: 1460 us -> 693 us (0.47)
  the two profiles are of different devices: /device:TPU:6 before, /device:TPU:448 now
where the time goes in v1:
time: 693 us; the launch traced here: 684 us
  waiting for transfers between devices  385 us (56%)
  Pallas kernels  173 us (25%)
  local copies, waits for them, and re-layouts  54.8 us (8%)
  blocking collectives  33 us (5%)
  starting transfers between devices  21.8 us (3%)
  between operations  13.7 us (2%)
    pallas_call x16, Pallas kernels, apply_half(): pl.pallas_call(half_layer, out_shape=jax.ShapeDtypeStruct((row_count, wid...  173 us
    all_gather x1, waiting for transfers between devices, on_device(): down = lax.all_gather(w_out[0], tp, axis=0, tiled=True)  148 us
    all_gather x1, waiting for transfers between devices, on_device(): up = lax.all_gather(w_in[0], tp, axis=0, tiled=True)  132 us
    ppermute x15, waiting for transfers between devices, on_device(): part = lax.ppermute(part, 'z', [(layer, layer + 1)])  69.9 us
    unnamed x16, local copies, waits for them, and re-layouts  54.6 us
    all_gather x16, blocking collectives, on_device(): pair = lax.all_gather(part, 'c', axis=0, tiled=False)  33 us
    ppermute x4, waiting for transfers between devices, on_device(): rows = rows + lax.ppermute(rows, 'z', route)  25.8 us
  transfers between devices with their start and end apart: 23, of which 6 were waited for; matrix products, arithmetic and copies ran while one was open for 0% of the time, Pallas kernels for 6%

profile of v1, /device:TPU:448, one launch (start us, length us, event | category | flops | bytes accessed | tf_op | source)
XLA Modules:
  0.0 684.3 jit_solution(5731170527247871545)
XLA Ops:
  6.5 0.7 all-gather.24.cloned.1.call-update
  7.3 0.7 all-gather.26.cloned.1.call-update
  8.0 7.0 %all-to-all-start = ((bf16[16,16,200]{2,1,0:T(8,128)(2,1)}), bf16[16,16,200]{2,1,0:T(8,128)(2,1)S(1)}, u32[]{:S(2)}, u32[]{:S(2)}) async-start(bf16[16,16,200]{2,1,0:T(8,128)(2,1)} %bitcast.1), calls=%async_computation | async-start | bytes 262144 | tf_op jit(solution)/shard_map/all_to_all | solution.py:75
  15.1 7.9 %all-to-all-done = bf16[16,16,200]{2,1,0:T(8,128)(2,1)S(1)} async-done(((bf16[16,16,200]{2,1,0:T(8,128)(2,1)}), bf16[16,16,200]{2,1,0:T(8,128)(2,1)S(1)}, u32[]{:S(2)}, u32[]{:S(2)}) %all-to-all-start) | async-done | bytes 102432 | tf_op jit(solution)/shard_map/all_to_all | solution.py:75
  23.3 132.0 %all-gather.24.cloned.1.call-done = bf16[1,3200,3200]{2,1,0:T(8,128)(2,1)} async-done(((bf16[1,200,3200]{2,1,0:T(8,128)(2,1)}), bf16[1,3200,3200]{2,1,0:T(8,128)(2,1)}) %all-gather.24.cloned.1.call-update) | async-done | bytes 20480016 | tf_op jit(solution)/shard_map/all_gather | solution.py:68
  155.3 148.4 %all-gather.26.cloned.1.call-done = bf16[1,3200,3200]{2,1,0:T(8,128)(2,1)} async-done(((bf16[1,200,3200]{2,1,0:T(8,128)(2,1)}), bf16[1,3200,3200]{2,1,0:T(8,128)(2,1)}) %all-gather.26.cloned.1.call-update) | async-done | bytes 20480016 | tf_op jit(solution)/shard_map/all_gather | solution.py:69
  303.7 6.8 copy-done
  310.6 6.8 copy-done.4
  317.4 10.8 %shard_map.46 = bf16[16,3200]{1,0:T(8,128)(2,1)S(1)} custom-call(s32[1]{0:T(128)} %bitcast.first_ref, bf16[2,16,3200]{2,1,0:T(8,128)(2,1)S(1)} %stack.7.pair_ref, bf16[3200,3200]{1,0:T(8,128)(2,1)S(1)} %bitcast.21, bf16[3200,3200]{1,0:T(8,128)(2,1)S(1)} %bitcast.37), custom_call_target="tpu_custom_call" | custom-call | flops 655360000 | bytes 40960000 | tf_op jit(solution)/shard_map/pallas_call | solution.py:42
  328.9 2.0 all-gather.2
  330.8 6.8 copy-done.1
  337.7 6.8 copy-done.5
  344.5 10.8 %shard_map.47 = bf16[16,3200]{1,0:T(8,128)(2,1)S(1)} custom-call(s32[1]{0:T(128)} %bitcast.first_ref, bf16[2,16,3200]{2,1,0:T(8,128)(2,1)S(1)} %bitcast.54, bf16[3200,3200]{1,0:T(8,128)(2,1)S(1)} %bitcast.22, bf16[3200,3200]{1,0:T(8,128)(2,1)S(1)} %bitcast.38), custom_call_target="tpu_custom_call" | custom-call | flops 655360000 | bytes 40960000 | tf_op jit(solution)/shard_map/pallas_call | solution.py:42
  355.3 0.7 collective-permute-start.1
  356.0 2.1 all-gather.3
  358.1 10.8 %shard_map.48 = bf16[16,3200]{1,0:T(8,128)(2,1)S(1)} custom-call(s32[1]{0:T(128)} %bitcast.first_ref, bf16[2,16,3200]{2,1,0:T(8,128)(2,1)S(1)} %bitcast.55, bf16[3200,3200]{1,0:T(8,128)(2,1)S(1)} %bitcast.23, bf16[3200,3200]{1,0:T(8,128)(2,1)S(1)} %bitcast.39), custom_call_target="tpu_custom_call" | custom-call | flops 655360000 | bytes 40960000 | tf_op jit(solution)/shard_map/pallas_call | solution.py:42
  368.9 0.7 collective-permute-start.2
  369.6 2.0 all-gather.4
  371.6 10.8 %shard_map.49 = bf16[16,3200]{1,0:T(8,128)(2,1)S(1)} custom-call(s32[1]{0:T(128)} %bitcast.first_ref, bf16[2,16,3200]{2,1,0:T(8,128)(2,1)S(1)} %bitcast.56, bf16[3200,3200]{1,0:T(8,128)(2,1)S(1)} %bitcast.24, bf16[3200,3200]{1,0:T(8,128)(2,1)S(1)} %bitcast.40), custom_call_target="tpu_custom_call" | custom-call | flops 655360000 | bytes 40960000 | tf_op jit(solution)/shard_map/pallas_call | solution.py:42
  382.4 0.7 collective-permute-start.3
  383.1 2.2 all-gather.5
  385.3 10.8 %shard_map.50 = bf16[16,3200]{1,0:T(8,128)(2,1)S(1)} custom-call(s32[1]{0:T(128)} %bitcast.first_ref, bf16[2,16,3200]{2,1,0:T(8,128)(2,1)S(1)} %bitcast.57, bf16[3200,3200]{1,0:T(8,128)(2,1)S(1)} %bitcast.25, bf16[3200,3200]{1,0:T(8,128)(2,1)S(1)} %bitcast.41), custom_call_target="tpu_custom_call" | custom-call | flops 655360000 | bytes 40960000 | tf_op jit(solution)/shard_map/pallas_call | solution.py:42
  396.1 0.7 collective-permute-start.4
  396.8 2.0 all-gather.6
  398.7 10.8 %shard_map.51 = bf16[16,3200]{1,0:T(8,128)(2,1)S(1)} custom-call(s32[1]{0:T(128)} %bitcast.first_ref, bf16[2,16,3200]{2,1,0:T(8,128)(2,1)S(1)} %bitcast.58, bf16[3200,3200]{1,0:T(8,128)(2,1)S(1)} %bitcast.26, bf16[3200,3200]{1,0:T(8,128)(2,1)S(1)} %bitcast.42), custom_call_target="tpu_custom_call" | custom-call | flops 655360000 | bytes 40960000 | tf_op jit(solution)/shard_map/pallas_call | solution.py:42
  409.5 0.7 collective-permute-start.5
  410.2 2.4 all-gather.7
  412.6 10.8 %shard_map.52 = bf16[16,3200]{1,0:T(8,128)(2,1)S(1)} custom-call(s32[1]{0:T(128)} %bitcast.first_ref, bf16[2,16,3200]{2,1,0:T(8,128)(2,1)S(1)} %bitcast.59, bf16[3200,3200]{1,0:T(8,128)(2,1)S(1)} %bitcast.27, bf16[3200,3200]{1,0:T(8,128)(2,1)S(1)} %bitcast.43), custom_call_target="tpu_custom_call" | custom-call | flops 655360000 | bytes 40960000 | tf_op jit(solution)/shard_map/pallas_call | solution.py:42
  423.4 0.7 collective-permute-start.6
  424.1 2.0 all-gather.8
  426.1 10.8 %shard_map.53 = bf16[16,3200]{1,0:T(8,128)(2,1)S(1)} custom-call(s32[1]{0:T(128)} %bitcast.first_ref, bf16[2,16,3200]{2,1,0:T(8,128)(2,1)S(1)} %bitcast.60, bf16[3200,3200]{1,0:T(8,128)(2,1)S(1)} %bitcast.28, bf16[3200,3200]{1,0:T(8,128)(2,1)S(1)} %bitcast.44), custom_call_target="tpu_custom_call" | custom-call | flops 655360000 | bytes 40960000 | tf_op jit(solution)/shard_map/pallas_call | solution.py:42
  436.9 0.7 collective-permute-start.7
  437.6 2.1 all-gather.9
  439.7 10.8 %shard_map.54 = bf16[16,3200]{1,0:T(8,128)(2,1)S(1)} custom-call(s32[1]{0:T(128)} %bitcast.first_ref, bf16[2,16,3200]{2,1,0:T(8,128)(2,1)S(1)} %bitcast.61, bf16[3200,3200]{1,0:T(8,128)(2,1)S(1)} %bitcast.29, bf16[3200,3200]{1,0:T(8,128)(2,1)S(1)} %bitcast.45), custom_call_target="tpu_custom_call" | custom-call | flops 655360000 | bytes 40960000 | tf_op jit(solution)/shard_map/pallas_call | solution.py:42
  450.5 0.7 collective-permute-start.8
  451.2 2.0 all-gather.10
  453.2 10.8 %shard_map.55 = bf16[16,3200]{1,0:T(8,128)(2,1)S(1)} custom-call(s32[1]{0:T(128)} %bitcast.first_ref, bf16[2,16,3200]{2,1,0:T(8,128)(2,1)S(1)} %bitcast.62, bf16[3200,3200]{1,0:T(8,128)(2,1)S(1)} %bitcast.30, bf16[3200,3200]{1,0:T(8,128)(2,1)S(1)} %bitcast.46), custom_call_target="tpu_custom_call" | custom-call | flops 655360000 | bytes 40960000 | tf_op jit(solution)/shard_map/pallas_call | solution.py:42
  464.0 0.7 collective-permute-start.9
  464.7 2.2 all-gather.11
  466.8 10.8 %shard_map.56 = bf16[16,3200]{1,0:T(8,128)(2,1)S(1)} custom-call(s32[1]{0:T(128)} %bitcast.first_ref, bf16[2,16,3200]{2,1,0:T(8,128)(2,1)S(1)} %bitcast.63, bf16[3200,3200]{1,0:T(8,128)(2,1)S(1)} %bitcast.31, bf16[3200,3200]{1,0:T(8,128)(2,1)S(1)} %bitcast.47), custom_call_target="tpu_custom_call" | custom-call | flops 655360000 | bytes 40960000 | tf_op jit(solution)/shard_map/pallas_call | solution.py:42
  477.6 0.7 collective-permute-start.10
  478.3 2.0 all-gather.12
  480.3 10.8 %shard_map.57 = bf16[16,3200]{1,0:T(8,128)(2,1)S(1)} custom-call(s32[1]{0:T(128)} %bitcast.first_ref, bf16[2,16,3200]{2,1,0:T(8,128)(2,1)S(1)} %bitcast.64, bf16[3200,3200]{1,0:T(8,128)(2,1)S(1)} %bitcast.32, bf16[3200,3200]{1,0:T(8,128)(2,1)S(1)} %bitcast.48), custom_call_target="tpu_custom_call" | custom-call | flops 655360000 | bytes 40960000 | tf_op jit(solution)/shard_map/pallas_call | solution.py:42
  491.1 0.7 collective-permute-start.11
  491.8 2.4 all-gather.13
  494.2 6.8 copy-done.2
  501.0 6.8 copy-done.6
  507.8 10.8 %shard_map.58 = bf16[16,3200]{1,0:T(8,128)(2,1)S(1)} custom-call(s32[1]{0:T(128)} %bitcast.first_ref, bf16[2,16,3200]{2,1,0:T(8,128)(2,1)S(1)} %bitcast.65, bf16[3200,3200]{1,0:T(8,128)(2,1)S(1)} %bitcast.33, bf16[3200,3200]{1,0:T(8,128)(2,1)S(1)} %bitcast.49), custom_call_target="tpu_custom_call" | custom-call | flops 655360000 | bytes 40960000 | tf_op jit(solution)/shard_map/pallas_call | solution.py:42
  519.3 2.0 all-gather.14
  521.3 10.8 %shard_map.59 = bf16[16,3200]{1,0:T(8,128)(2,1)S(1)} custom-call(s32[1]{0:T(128)} %bitcast.first_ref, bf16[2,16,3200]{2,1,0:T(8,128)(2,1)S(1)} %bitcast.66, bf16[3200,3200]{1,0:T(8,128)(2,1)S(1)} %bitcast.34, bf16[3200,3200]{1,0:T(8,128)(2,1)S(1)} %bitcast.50), custom_call_target="tpu_custom_call" | custom-call | flops 655360000 | bytes 40960000 | tf_op jit(solution)/shard_map/pallas_call | solution.py:42
  532.1 1.3 collective-permute-start.13
  533.4 67.1 %collective-permute-done.13 = bf16[16,3200]{1,0:T(8,128)(2,1)S(1)} collective-permute-done((bf16[16,3200]{1,0:T(8,128)(2,1)S(1)}, bf16[16,3200]{1,0:T(8,128)(2,1)S(1)}, u32[]{:S(2)}, u32[]{:S(2)}) %collective-permute-start.13) | collective-permute-done | bytes 102432 | tf_op jit(solution)/shard_map/ppermute | solution.py:80
  600.6 2.1 all-gather.15
  602.7 10.8 %shard_map.60 = bf16[16,3200]{1,0:T(8,128)(2,1)S(1)} custom-call(s32[1]{0:T(128)} %bitcast.first_ref, bf16[2,16,3200]{2,1,0:T(8,128)(2,1)S(1)} %bitcast.67, bf16[3200,3200]{1,0:T(8,128)(2,1)S(1)} %bitcast.35, bf16[3200,3200]{1,0:T(8,128)(2,1)S(1)} %bitcast.51), custom_call_target="tpu_custom_call" | custom-call | flops 655360000 | bytes 40960000 | tf_op jit(solution)/shard_map/pallas_call | solution.py:42
  613.5 1.3 collective-permute-start.14
  614.8 2.7 collective-permute-done.14
  617.5 1.9 all-gather.16
  619.5 6.8 copy-done.3
  626.3 6.8 copy-done.7
  633.1 10.8 %shard_map.61 = bf16[16,3200]{1,0:T(8,128)(2,1)S(1)} custom-call(s32[1]{0:T(128)} %bitcast.first_ref, bf16[2,16,3200]{2,1,0:T(8,128)(2,1)S(1)} %bitcast.53, bf16[3200,3200]{1,0:T(8,128)(2,1)S(1)} %bitcast.36, bf16[3200,3200]{1,0:T(8,128)(2,1)S(1)} %bitcast.52), custom_call_target="tpu_custom_call" | custom-call | flops 655360000 | bytes 40960000 | tf_op jit(solution)/shard_map/pallas_call | solution.py:42
  643.9 2.0 all-gather.17
  648.1 1.3 collective-permute-start.18
  649.4 25.7 %collective-permute-done.18 = bf16[16,3200]{1,0:T(8,128)(2,1)S(1)} collective-permute-done((bf16[16,3200]{1,0:T(8,128)(2,1)S(1)}, bf16[16,3200]{1,0:T(8,128)(2,1)S(1)}, u32[]{:S(2)}, u32[]{:S(2)}) %collective-permute-start.18) | collective-permute-done | bytes 102432 | tf_op jit(solution)/shard_map/ppermute | solution.py:89
  675.2 2.4 convolution_convert_fusion
  (41 shorter events, 3.9 us)
Async XLA Ops:
  6.5 148.8 %all-gather.24.cloned.1.call-start = ((), (), s32[]{:S(2)}) async-start(), calls=%async_computation.2 | async-start | bytes 21760000 | tf_op jit(solution)/shard_map/all_gather | solution.py:68
  7.3 296.5 %all-gather.26.cloned.1.call-start = ((), (), s32[]{:S(2)}) async-start(), calls=%async_computation.3 | async-start | bytes 21760000 | tf_op jit(solution)/shard_map/all_gather | solution.py:69
  8.0 15.0 %all-to-all-start = ((bf16[16,16,200]{2,1,0:T(8,128)(2,1)}), bf16[16,16,200]{2,1,0:T(8,128)(2,1)S(1)}, u32[]{:S(2)}, u32[]{:S(2)}) async-start(bf16[16,16,200]{2,1,0:T(8,128)(2,1)} %bitcast.1), calls=%async_computation | async-start | bytes 262144 | tf_op jit(solution)/shard_map/all_to_all | solution.py:75
  15.1 634.4 %all-gather.22.cloned.1.call-start = ((), (), s32[]{:S(2)}) async-start(), calls=%async_computation.1 | async-start | bytes 1740800 | tf_op jit(solution)/shard_map/all_gather | solution.py:70
  303.7 6.8 copy-start
  310.6 6.8 copy-start.4
  328.2 0.7 collective-permute-start
  330.8 6.8 copy-start.1
  337.7 6.8 copy-start.5
  355.3 0.7 collective-permute-start.1
  368.9 0.7 collective-permute-start.2
  382.4 0.7 collective-permute-start.3
  396.1 0.7 collective-permute-start.4
  409.5 0.7 collective-permute-start.5
  423.4 0.7 collective-permute-start.6
  436.9 0.7 collective-permute-start.7
  450.5 0.7 collective-permute-start.8
  464.0 0.7 collective-permute-start.9
  477.6 0.7 collective-permute-start.10
  491.1 0.7 collective-permute-start.11
  494.2 6.8 copy-start.2
  501.0 6.8 copy-start.6
  518.6 0.7 collective-permute-start.12
  532.1 68.5 %collective-permute-start.13 = (bf16[16,3200]{1,0:T(8,128)(2,1)S(1)}, bf16[16,3200]{1,0:T(8,128)(2,1)S(1)}, u32[]{:S(2)}, u32[]{:S(2)}) collective-permute-start(bf16[16,3200]{1,0:T(8,128)(2,1)S(1)} %shard_map.59), channel_id=1, source_target_pairs={{416,448},{417,449},{418,450},{419,451},{420,452},{421,453},{422,4... | collective-permute-start | bytes 307208 | tf_op jit(solution)/shard_map/ppermute | solution.py:80
  613.5 4.0 collective-permute-start.14
  619.5 6.8 copy-start.3
  626.3 6.8 copy-start.7
  645.9 0.7 collective-permute-start.15
  646.7 0.7 collective-permute-start.16
  647.4 0.7 collective-permute-start.17
  648.1 27.1 %collective-permute-start.18 = (bf16[16,3200]{1,0:T(8,128)(2,1)S(1)}, bf16[16,3200]{1,0:T(8,128)(2,1)S(1)}, u32[]{:S(2)}, u32[]{:S(2)}) collective-permute-start(bf16[16,3200]{1,0:T(8,128)(2,1)S(1)} %add.21), channel_id=1, source_target_pairs={{480,0},{224,256},{96,128},{352,384},{32,64},{288,320},{160,192},{... | collective-permute-start | bytes 307208 | tf_op jit(solution)/shard_map/ppermute | solution.py:89
Sparse Core Ops, SparseCore 0:
  10.4 144.9 all-gather.23
  158.3 145.3 all-gather.25
  491.9 108.5 all-gather.21

commit v2 on v1

v2 whole, which is shorter than its diff:
```python
import functools

import jax
import jax.numpy as jnp
from jax import lax
from jax.experimental import pallas as pl
from jax.experimental.pallas import tpu as pltpu
from jax.sharding import Mesh, PartitionSpec as P

SIDE = 4
OFFSETS = (0, 3, 1, 2)


def moved(block, axis, by):
    route = [(i, (i + by) % SIDE) for i in range(SIDE)]
    return lax.ppermute(block, axis, route)


def ring(top, bottom, axis):
    below_top = moved(top, axis, 1)
    above_bottom = moved(bottom, axis, -1)
    below_bottom = moved(bottom, axis, 1)
    above_top = moved(top, axis, -1)
    far_top = moved(below_top, axis, 1)
    far_bottom = moved(above_bottom, axis, -1)
    return (
        (top, below_top, above_top, far_top),
        (bottom, below_bottom, above_bottom, far_bottom),
    )


def in_order(parts, axis):
    place = lax.axis_index(axis)
    rows, width = parts[0].shape
    whole = jnp.zeros((SIDE, rows, width), parts[0].dtype)
    for part, offset in zip(parts, OFFSETS):
        at = lax.rem(place + offset, SIDE)
        whole = lax.dynamic_update_slice(whole, part[None], (at, 0, 0))
    return whole.reshape(SIDE * rows, width)


def product(left, right):
    return lax.dot_general(
        left, right, (((1,), (1,)), ((), ())), preferred_element_type=jnp.float32
    )


def half_layer(state_ref, pair_ref, *refs):
    sources, (out_ref, tops_ref, bottoms_ref, hidden_top, hidden_bottom, sems) = (
        refs[:16],
        refs[16:],
    )
    row_count, width = out_ref.shape
    high = tops_ref.shape[1] // SIDE
    low = bottoms_ref.shape[1] // SIDE
    block = high + low

    @pl.when(state_ref[0] == 0)
    def _():
        out_ref[...] = jnp.zeros_like(out_ref)

    @pl.when(state_ref[0] == 1)
    def _():
        copies = []
        for which in range(2):
            for index in range(1, SIDE):
                slot = 3 * which + index - 1
                for half, target in enumerate((tops_ref, bottoms_ref)):
                    copies.append(
                        pltpu.make_async_copy(
                            sources[8 * which + 4 * half + index],
                            target.at[slot],
                            sems.at[2 * slot + half],
                        )
                    )
        for copy in copies:
            copy.start()

        rows = pair_ref[0].astype(jnp.float32) + pair_ref[1].astype(jnp.float32)
        scale = lax.rsqrt(jnp.mean(rows * rows, axis=1, keepdims=True) + 1e-06)
        normed = (rows * scale).astype(jnp.bfloat16)

        def joined():
            tops = [hidden_top[i] for i in range(SIDE)]
            bottoms = [hidden_bottom[i] for i in range(SIDE)]
            return tops, bottoms

        def stage(which, left, finish):
            for index, offset in enumerate(OFFSETS):
                at = lax.rem(state_ref[2 + which] + offset, SIDE)
                for half, (target, store) in enumerate(
                    ((tops_ref, hidden_top), (bottoms_ref, hidden_bottom))
                ):
                    if index == 0:
                        right = sources[8 * which + 4 * half][...]
                    else:
                        slot = 3 * which + index - 1
                        copies[2 * slot + half].wait()
                        right = target[slot]
                    store[at] = finish(product(left, right))

        stage(0, normed, jax.nn.gelu)
        tops, bottoms = joined()
        pieces = []
        for y in range(SIDE):
            for x in range(SIDE):
                pieces.append(tops[y][:, x * high : (x + 1) * high])
                pieces.append(bottoms[y][:, x * low : (x + 1) * low])
        hidden = jnp.concatenate(pieces, axis=1).astype(jnp.bfloat16)
        stage(1, hidden, lambda part: part)
        tops, bottoms = joined()
        pieces = []
        for y in range(SIDE):
            for x in range(SIDE):
                pieces.append(tops[x][:, y * high : (y + 1) * high])
                pieces.append(bottoms[x][:, y * low : (y + 1) * low])
        total = jnp.concatenate(pieces, axis=1)
        base = jnp.where(state_ref[1] == 1, rows, 0.0)
        out_ref[...] = (base + total).astype(jnp.bfloat16)


def apply_half(state, pair, up, down):
    _, row_count, width = pair.shape
    (up_tops, up_bottoms), (down_tops, down_bottoms) = up, down
    sources = (*up_tops, *up_bottoms, *down_tops, *down_bottoms)
    own = (0, 4, 8, 12)
    sources = [
        pltpu.with_memory_space_constraint(s, pltpu.VMEM) if i in own else s
        for i, s in enumerate(sources)
    ]
    resident = pl.BlockSpec(memory_space=pltpu.VMEM)
    anywhere = pl.BlockSpec(memory_space=pl.ANY)
    high, low = up_tops[0].shape[0], up_bottoms[0].shape[0]
    return pl.pallas_call(
        half_layer,
        out_shape=jax.ShapeDtypeStruct((row_count, width), jnp.bfloat16),
        in_specs=[pl.BlockSpec(memory_space=pltpu.SMEM), resident]
        + [resident if i in own else anywhere for i in range(16)],
        out_specs=resident,
        scratch_shapes=[
            pltpu.VMEM((6, high, width), jnp.bfloat16),
            pltpu.VMEM((6, low, width), jnp.bfloat16),
            pltpu.VMEM((SIDE, row_count, high), jnp.float32),
            pltpu.VMEM((SIDE, row_count, low), jnp.float32),
            pltpu.SemaphoreType.DMA((12,)),
        ],
        compiler_params=pltpu.CompilerParams(vmem_limit_bytes=40 * 2**20),
        cost_estimate=pl.CostEstimate(
            flops=4 * row_count * width * width,
            bytes_accessed=3 * width * width,
            transcendentals=row_count * width,
        ),
        name="half_layer",
    )(state, pair, *sources)


def on_device(layers, patches, w_in, w_out, w_proj):
    plane = lax.axis_index("z")
    core = lax.axis_index("c")
    tp = ("y", "x")
    cut = w_in.shape[1] // 16 * 8 + 8

    flat = patches.reshape(-1, patches.shape[2])
    mine = lax.all_to_all(flat, tp, split_axis=0, concat_axis=1, tiled=True)
    pair = jnp.stack([mine, jnp.zeros_like(mine)])

    up_tops, up_bottoms = ring(w_in[0, :cut], w_in[0, cut:], "x")
    down_tops, down_bottoms = ring(w_out[0, :cut], w_out[0, cut:], "y")
    up_top, up_bottom = in_order(up_tops, "x"), in_order(up_bottoms, "x")
    down_top, down_bottom = in_order(down_tops, "y"), in_order(down_bottoms, "y")
    up_top, pair = lax.optimization_barrier((up_top, pair))
    up = ring(up_top, up_bottom, "y")
    down = ring(down_top, down_bottom, "x")
    columns = lax.all_gather(w_proj, tp, axis=0, tiled=True)

    places = [core == 0, lax.axis_index("y"), lax.axis_index("x")]
    for layer in range(layers):
        state = jnp.stack([plane == layer] + places).astype(jnp.int32)
        part = apply_half(state, pair, up, down)
        if layer < layers - 1:
            part = lax.ppermute(part, "z", [(layer, layer + 1)])
        pair = lax.all_gather(part, "c", axis=0, tiled=False)

    total = pair[0].astype(jnp.float32) + pair[1].astype(jnp.float32)
    rows = jnp.where(plane == layers - 1, total, 0.0).astype(jnp.bfloat16)
    holders = [layers - 1]
    step = layers // 2
    while step:
        route = [(held, (held + step) % layers) for held in holders]
        rows = rows + lax.ppermute(rows, "z", route)
        holders += [target for _, target in route]
        step //= 2
    return jnp.dot(rows, columns, preferred_element_type=jnp.float32).astype(jnp.bfloat16)


def solution(mesh):
    sections = mesh.shape["section"]
    grid = Mesh(
        mesh.devices.reshape(sections // 2, 2, SIDE, SIDE), ("z", "c", "y", "x")
    )
    section, tp = ("z", "c"), ("y", "x")
    return jax.shard_map(
        functools.partial(on_device, sections // 2),
        mesh=grid,
        in_specs=(
            P(None, None, tp),
            P(section, tp, None),
            P(section, tp, None),
            P(tp, section),
        ),
        out_specs=P(tp, section),
        check_vma=False,
    )
```

time: 693 us -> 793 us (1.14)
  waiting for transfers between devices: 385 us -> 532 us
  Pallas kernels: 173 us -> 71.7 us
  starting transfers between devices: 21.8 us -> 96.6 us
  local copies, waits for them, and re-layouts: 54.8 us -> 32.4 us
    all_gather x2 -> x0, waiting for transfers between devices: 280 us -> none  [the longest x1 148 us: on_device(): down = lax.all_gather(w_out[0], tp, axis=0, tiled=True)]
    ppermute x15, waiting for transfers between devices: 69.9 us -> 280 us  [on_device(): part = lax.ppermute(part, 'z', [(layer, layer + 1)])]
    ppermute x0 -> x24, waiting for transfers between devices: none -> 201 us  [moved(): return lax.ppermute(block, axis, route)]
    pallas_call x16, Pallas kernels: 173 us -> 71.7 us  [apply_half(): pl.pallas_call(half_layer, out_shape=jax.ShapeDtypeStruct((row_count, wid...]
    ppermute x0 -> x24, starting transfers between devices: none -> 77.8 us  [moved(): return lax.ppermute(block, axis, route)]
    unnamed x16, local copies, waits for them, and re-layouts: 54.6 us -> 5.54 us
    ppermute x4, waiting for transfers between devices: 25.8 us -> 41.4 us  [on_device(): rows = rows + lax.ppermute(rows, 'z', route)]
    dynamic_update_slice x0 -> x12, local copies, waits for them, and re-layouts: none -> 12.5 us  [in_order(): whole = lax.dynamic_update_slice(whole, part[None], (at, 0, 0))]
  transfers between devices with their start and end apart: 23 -> 45, of which waited for: 6 -> 10; matrix products, arithmetic and copies ran while one was open for 0% -> 3% of each run, Pallas kernels for 6% -> 9%
where the time goes in v2:
time: 793 us; the launch traced here: 783 us
  waiting for transfers between devices  532 us (67%)
  starting transfers between devices  96.6 us (12%)
  Pallas kernels  71.7 us (9%)
  local copies, waits for them, and re-layouts  32.4 us (4%)
  blocking collectives  31.1 us (4%)
  between operations  14.6 us (2%)
    ppermute x15, waiting for transfers between devices, on_device(): part = lax.ppermute(part, 'z', [(layer, layer + 1)])  280 us
    ppermute x24, waiting for transfers between devices, moved(): return lax.ppermute(block, axis, route)  201 us
    ppermute x24, starting transfers between devices, moved(): return lax.ppermute(block, axis, route)  77.8 us
    pallas_call x16, Pallas kernels, apply_half(): pl.pallas_call(half_layer, out_shape=jax.ShapeDtypeStruct((row_count, wid...  71.7 us
    ppermute x4, waiting for transfers between devices, on_device(): rows = rows + lax.ppermute(rows, 'z', route)  41.4 us
    all_gather x16, blocking collectives, on_device(): pair = lax.all_gather(part, 'c', axis=0, tiled=False)  31.1 us
  transfers between devices with their start and end apart: 45, of which 10 were waited for; matrix products, arithmetic and copies ran while one was open for 3% of the time, Pallas kernels for 9%

profile of v2, /device:TPU:448, one launch (start us, length us, event | category | flops | bytes accessed | tf_op | source)
XLA Modules:
  0.0 782.6 jit_solution(6213631515437095274)
XLA Ops:
  9.5 3.4 collective-permute-start.12
  12.9 3.6 collective-permute-start.13
  19.3 2.3 collective-permute-start.18
  21.5 4.8 collective-permute-start.19
  27.9 2.2 slice_bitcast_fusion.3
  30.1 3.4 collective-permute-start.6
  33.6 4.2 all-to-all-start
  38.1 2.0 slice_bitcast_fusion.1
  40.1 10.2 %all-to-all-done = bf16[16,16,200]{2,1,0:T(8,128)(2,1)S(1)} async-done(((bf16[16,16,200]{2,1,0:T(8,128)(2,1)}), bf16[16,16,200]{2,1,0:T(8,128)(2,1)S(1)}, u32[]{:S(2)}, u32[]{:S(2)}) %all-to-all-start) | async-done | bytes 102432 | tf_op jit(solution)/shard_map/all_to_all | solution.py:164
  53.7 2.5 collective-permute-start.7
  58.2 3.3 collective-permute-start
  61.5 2.0 bitcast_dynamic-update-slice_fusion.7
  63.5 3.7 collective-permute-start.1
  69.1 3.5 collective-permute-done.7
  72.6 4.1 collective-permute-start.20
  77.6 3.7 collective-permute-start.8
  84.3 2.1 collective-permute-start.2
  86.4 2.0 bitcast_dynamic-update-slice_fusion.1
  89.3 5.0 collective-permute-start.22
  94.2 5.8 collective-permute-done.8
  100.9 4.1 collective-permute-start.10
  110.0 2.8 collective-permute-start.21
  112.8 36.5 %collective-permute-done.22.refs_14_ = bf16[384,3200]{1,0:T(8,128)(2,1)} collective-permute-done((bf16[384,3200]{1,0:T(8,128)(2,1)}, bf16[384,3200]{1,0:T(8,128)(2,1)}, u32[]{:S(2)}, u32[]{:S(2)}) %collective-permute-start.22) | collective-permute-done | bytes 2457632 | tf_op jit(solution)/shard_map/ppermute | solution.py:16
  149.3 3.5 collective-permute-start.16
  152.8 3.4 collective-permute-start.9
  156.2 58.5 %collective-permute-done.21.refs_13_ = bf16[384,3200]{1,0:T(8,128)(2,1)S(1)} collective-permute-done((bf16[384,3200]{1,0:T(8,128)(2,1)}, bf16[384,3200]{1,0:T(8,128)(2,1)S(1)}, u32[]{:S(2)}, u32[]{:S(2)}) %collective-permute-start.21) | collective-permute-done | bytes 2457632 | tf_op jit(solution)/shard_map/ppermute | solution.py:16
  214.7 2.2 collective-permute-start.4
  218.9 3.6 collective-permute-start.5
  223.9 5.1 collective-permute-start.23
  229.1 3.4 collective-permute-start.11
  232.7 50.1 %collective-permute-done.4.refs_2_ = bf16[416,3200]{1,0:T(8,128)(2,1)} collective-permute-done((bf16[416,3200]{1,0:T(8,128)(2,1)S(1)}, bf16[416,3200]{1,0:T(8,128)(2,1)}, u32[]{:S(2)}, u32[]{:S(2)}) %collective-permute-start.4) | collective-permute-done | bytes 2662432 | tf_op jit(solution)/shard_map/ppermute | solution.py:16
  282.8 46.4 %collective-permute-done.11.refs_7_ = bf16[384,3200]{1,0:T(8,128)(2,1)} collective-permute-done((bf16[384,3200]{1,0:T(8,128)(2,1)}, bf16[384,3200]{1,0:T(8,128)(2,1)}, u32[]{:S(2)}, u32[]{:S(2)}) %collective-permute-start.11) | collective-permute-done | bytes 2457632 | tf_op jit(solution)/shard_map/ppermute | solution.py:16
  330.9 3.5 half_layer.16
  335.2 1.9 all-gather
  337.1 3.6 half_layer.17
  341.5 1.9 all-gather.1
  343.4 3.4 half_layer.18
  349.5 3.8 half_layer.19
  354.0 1.9 all-gather.3
  356.0 3.4 half_layer.20
  360.1 1.9 all-gather.4
  362.1 3.5 half_layer.21
  366.4 1.9 all-gather.5
  368.3 3.4 half_layer.22
  372.4 1.9 all-gather.6
  374.4 3.6 half_layer.23
  378.7 1.9 all-gather.7
  380.7 3.4 half_layer.24
  384.8 1.9 all-gather.8
  386.8 3.8 half_layer.25
  393.3 3.4 half_layer.26
  397.4 1.9 all-gather.10
  399.3 3.5 half_layer.27
  403.6 1.9 all-gather.11
  407.3 3.4 half_layer.28
  411.4 1.9 all-gather.12
  413.4 3.6 half_layer.29
  418.3 277.3 %collective-permute-done.37 = bf16[16,3200]{1,0:T(8,128)(2,1)S(1)} collective-permute-done((bf16[16,3200]{1,0:T(8,128)(2,1)S(1)}, bf16[16,3200]{1,0:T(8,128)(2,1)S(1)}, u32[]{:S(2)}, u32[]{:S(2)}) %collective-permute-start.37) | collective-permute-done | bytes 102432 | tf_op jit(solution)/shard_map/ppermute | solution.py:181
  697.6 19.0 %half_layer.30 = bf16[16,3200]{1,0:T(8,128)(2,1)S(1)} custom-call(s32[4]{0:T(128)S(1)} %add_add_fusion.1.state_ref, bf16[2,16,3200]{2,1,0:T(8,128)(2,1)S(1)} %bitcast.105, bf16[416,3200]{1,0:T(8,128)(2,1)S(1)} %bitcast.89, bf16[416,3200]{1,0:T(8,128)(2,1)} %collective-permute-done.3.refs_1_, bf16[416,3200]{1,0:T(8,128)(2,1)} %collective-permute-done.4.refs_2_, ...), custom_call_target="tpu_custom_call" | custom-call | flops 655360000 | bytes 30720000 | tf_op jit(solution)/shard_map/half_layer/pallas_call | solution.py:134
  717.9 2.6 collective-permute-done.38
  722.5 3.6 half_layer.31
  726.1 2.0 all-gather.15
  731.6 41.3 %collective-permute-done.42 = bf16[16,3200]{1,0:T(8,128)(2,1)S(1)} collective-permute-done((bf16[16,3200]{1,0:T(8,128)(2,1)S(1)}, bf16[16,3200]{1,0:T(8,128)(2,1)S(1)}, u32[]{:S(2)}, u32[]{:S(2)}) %collective-permute-start.42) | collective-permute-done | bytes 102432 | tf_op jit(solution)/shard_map/ppermute | solution.py:190
  773.0 2.4 convolution_convert_fusion
  (119 shorter events, 55.8 us)
Async XLA Ops:
  6.5 1.8 copy-start.5
  9.5 68.2 %collective-permute-start.12 = (bf16[104,3200]{1,0:T(8,128)(2,1)}, bf16[104,3200]{1,0:T(8,128)(2,1)S(1)}, u32[]{:S(2)}, u32[]{:S(2)}) collective-permute-start(bf16[104,3200]{1,0:T(8,128)(2,1)} %get-tuple-element.11), channel_id=1, source_target_pairs={{0,4},{4,8},{8,12},{12,0},{1,5},{5,9},{9,13},{13,1},{2,6},{6,10},{... | collective-permute-start | bytes 1996808 | tf_op jit(solution)/shard_map/ppermute | solution.py:16
  12.9 71.4 %collective-permute-start.13 = (bf16[104,3200]{1,0:T(8,128)(2,1)}, bf16[104,3200]{1,0:T(8,128)(2,1)}, u32[]{:S(2)}, u32[]{:S(2)}) collective-permute-start(bf16[104,3200]{1,0:T(8,128)(2,1)} %get-tuple-element.11), channel_id=1, source_target_pairs={{0,12},{4,0},{8,4},{12,8},{1,13},{5,1},{9,5},{13,9},{2,14},{6,2},{... | collective-permute-start | bytes 1996808 | tf_op jit(solution)/shard_map/ppermute | solution.py:16
  19.3 34.5 %collective-permute-start.18 = (bf16[96,3200]{1,0:T(8,128)(2,1)}, bf16[96,3200]{1,0:T(8,128)(2,1)}, u32[]{:S(2)}, u32[]{:S(2)}) collective-permute-start(bf16[96,3200]{1,0:T(8,128)(2,1)} %get-tuple-element.9), channel_id=1, source_target_pairs={{0,4},{4,8},{8,12},{12,0},{1,5},{5,9},{9,13},{13,1},{2,6},{6,10},{... | collective-permute-start | bytes 1843208 | tf_op jit(solution)/shard_map/ppermute | solution.py:16
  21.5 36.6 %collective-permute-start.19 = (bf16[96,3200]{1,0:T(8,128)(2,1)}, bf16[96,3200]{1,0:T(8,128)(2,1)}, u32[]{:S(2)}, u32[]{:S(2)}) collective-permute-start(bf16[96,3200]{1,0:T(8,128)(2,1)} %get-tuple-element.9), channel_id=1, source_target_pairs={{0,12},{4,0},{8,4},{12,8},{1,13},{5,1},{9,5},{13,9},{2,14},{6,2},{... | collective-permute-start | bytes 1843208 | tf_op jit(solution)/shard_map/ppermute | solution.py:16
  30.1 33.3 %collective-permute-start.6 = (bf16[96,3200]{1,0:T(8,128)(2,1)}, bf16[96,3200]{1,0:T(8,128)(2,1)}, u32[]{:S(2)}, u32[]{:S(2)}) collective-permute-start(bf16[96,3200]{1,0:T(8,128)(2,1)} %get-tuple-element.13), channel_id=1, source_target_pairs={{0,1},{1,2},{2,3},{3,0},{4,5},{5,6},{6,7},{7,4},{8,9},{9,10},{10,1... | collective-permute-start | bytes 1843208 | tf_op jit(solution)/shard_map/ppermute | solution.py:16
  33.6 16.7 %all-to-all-start = ((bf16[16,16,200]{2,1,0:T(8,128)(2,1)}), bf16[16,16,200]{2,1,0:T(8,128)(2,1)S(1)}, u32[]{:S(2)}, u32[]{:S(2)}) async-start(bf16[16,16,200]{2,1,0:T(8,128)(2,1)} %bitcast.24), calls=%async_computation | async-start | bytes 262144 | tf_op jit(solution)/shard_map/all_to_all | solution.py:164
  37.9 693.8 %all-gather.18.cloned.1.call-start = ((), (), s32[]{:S(2)}) async-start(), calls=%async_computation.1 | async-start | bytes 1740800 | tf_op jit(solution)/shard_map/all_gather | solution.py:174
  50.3 0.7 copy-start.7
  52.7 10.7 %copy-start.6 = (bf16[104,3200]{1,0:T(8,128)(2,1)S(1)}, bf16[104,3200]{1,0:T(8,128)(2,1)}, u32[]{:S(2)}) copy-start(bf16[104,3200]{1,0:T(8,128)(2,1)} %get-tuple-element.15) | copy-start | bytes 1996804
  53.7 18.9 %collective-permute-start.7 = (bf16[96,3200]{1,0:T(8,128)(2,1)}, bf16[96,3200]{1,0:T(8,128)(2,1)S(1)}, u32[]{:S(2)}, u32[]{:S(2)}) collective-permute-start(bf16[96,3200]{1,0:T(8,128)(2,1)} %get-tuple-element.13), channel_id=1, source_target_pairs={{0,3},{1,0},{2,1},{3,2},{4,7},{5,4},{6,5},{7,6},{8,11},{9,8},{10,9... | collective-permute-start | bytes 1843208 | tf_op jit(solution)/shard_map/ppermute | solution.py:16
  58.2 24.1 %collective-permute-start = (bf16[104,3200]{1,0:T(8,128)(2,1)}, bf16[104,3200]{1,0:T(8,128)(2,1)S(1)}, u32[]{:S(2)}, u32[]{:S(2)}) collective-permute-start(bf16[104,3200]{1,0:T(8,128)(2,1)} %get-tuple-element.15), channel_id=1, source_target_pairs={{0,1},{1,2},{2,3},{3,0},{4,5},{5,6},{6,7},{7,4},{8,9},{9,10},{10,1... | collective-permute-start | bytes 1996808 | tf_op jit(solution)/shard_map/ppermute | solution.py:16
  63.5 41.6 %collective-permute-start.1 = (bf16[104,3200]{1,0:T(8,128)(2,1)S(1)}, bf16[104,3200]{1,0:T(8,128)(2,1)S(1)}, u32[]{:S(2)}, u32[]{:S(2)}) collective-permute-start(bf16[104,3200]{1,0:T(8,128)(2,1)S(1)} %copy-done.6), channel_id=1, source_target_pairs={{0,3},{1,0},{2,1},{3,2},{4,7},{5,4},{6,5},{7,6},{8,11},{9,8},{10,9... | collective-permute-start | bytes 1996808 | tf_op jit(solution)/shard_map/ppermute | solution.py:16
  72.6 15.8 %collective-permute-start.20 = (bf16[96,3200]{1,0:T(8,128)(2,1)}, bf16[96,3200]{1,0:T(8,128)(2,1)S(1)}, u32[]{:S(2)}, u32[]{:S(2)}) collective-permute-start(bf16[96,3200]{1,0:T(8,128)(2,1)} %collective-permute-done.19), channel_id=1, source_target_pairs={{0,12},{4,0},{8,4},{12,8},{1,13},{5,1},{9,5},{13,9},{2,14},{6,2},{... | collective-permute-start | bytes 1843208 | tf_op jit(solution)/shard_map/ppermute | solution.py:16
  77.6 22.4 %collective-permute-start.8 = (bf16[96,3200]{1,0:T(8,128)(2,1)S(1)}, bf16[96,3200]{1,0:T(8,128)(2,1)S(1)}, u32[]{:S(2)}, u32[]{:S(2)}) collective-permute-start(bf16[96,3200]{1,0:T(8,128)(2,1)S(1)} %collective-permute-done.7), channel_id=1, source_target_pairs={{0,3},{1,0},{2,1},{3,2},{4,7},{5,4},{6,5},{7,6},{8,11},{9,8},{10,9... | collective-permute-start | bytes 1843208 | tf_op jit(solution)/shard_map/ppermute | solution.py:16
  82.3 22.8 %collective-permute-start.14 = (bf16[104,3200]{1,0:T(8,128)(2,1)S(1)}, bf16[104,3200]{1,0:T(8,128)(2,1)S(1)}, u32[]{:S(2)}, u32[]{:S(2)}) collective-permute-start(bf16[104,3200]{1,0:T(8,128)(2,1)S(1)} %collective-permute-done.12), channel_id=1, source_target_pairs={{0,4},{4,8},{8,12},{12,0},{1,5},{5,9},{9,13},{13,1},{2,6},{6,10},{... | collective-permute-start | bytes 1996808 | tf_op jit(solution)/shard_map/ppermute | solution.py:16
  84.3 23.7 %collective-permute-start.2 = (bf16[104,3200]{1,0:T(8,128)(2,1)S(1)}, bf16[104,3200]{1,0:T(8,128)(2,1)S(1)}, u32[]{:S(2)}, u32[]{:S(2)}) collective-permute-start(bf16[104,3200]{1,0:T(8,128)(2,1)S(1)} %collective-permute-done), channel_id=1, source_target_pairs={{0,1},{1,2},{2,3},{3,0},{4,5},{5,6},{6,7},{7,4},{8,9},{9,10},{10,1... | collective-permute-start | bytes 1996808 | tf_op jit(solution)/shard_map/ppermute | solution.py:16
  89.3 60.0 %collective-permute-start.22 = (bf16[384,3200]{1,0:T(8,128)(2,1)}, bf16[384,3200]{1,0:T(8,128)(2,1)}, u32[]{:S(2)}, u32[]{:S(2)}) collective-permute-start(bf16[384,3200]{1,0:T(8,128)(2,1)} %bitcast.40.refs_12_), channel_id=1, source_target_pairs={{0,3},{1,0},{2,1},{3,2},{4,7},{5,4},{6,5},{7,6},{8,11},{9,8},{10,9... | collective-permute-start | bytes 7372808 | tf_op jit(solution)/shard_map/ppermute | solution.py:16
  100.9 51.9 %collective-permute-start.10 = (bf16[384,3200]{1,0:T(8,128)(2,1)}, bf16[384,3200]{1,0:T(8,128)(2,1)}, u32[]{:S(2)}, u32[]{:S(2)}) collective-permute-start(bf16[384,3200]{1,0:T(8,128)(2,1)} %bitcast.30.refs_4_), channel_id=1, source_target_pairs={{0,12},{4,0},{8,4},{12,8},{1,13},{5,1},{9,5},{13,9},{2,14},{6,2},{... | collective-permute-start | bytes 7372808 | tf_op jit(solution)/shard_map/ppermute | solution.py:16
  106.1 110.8 %collective-permute-start.15 = (bf16[416,3200]{1,0:T(8,128)(2,1)}, bf16[416,3200]{1,0:T(8,128)(2,1)}, u32[]{:S(2)}, u32[]{:S(2)}) collective-permute-start(bf16[416,3200]{1,0:T(8,128)(2,1)} %bitcast.35.refs_8_), channel_id=1, source_target_pairs={{0,1},{1,2},{2,3},{3,0},{4,5},{5,6},{6,7},{7,4},{8,9},{9,10},{10,1... | collective-permute-start | bytes 7987208 | tf_op jit(solution)/shard_map/ppermute | solution.py:16
  108.1 110.8 %collective-permute-start.3 = (bf16[416,3200]{1,0:T(8,128)(2,1)S(1)}, bf16[416,3200]{1,0:T(8,128)(2,1)}, u32[]{:S(2)}, u32[]{:S(2)}) collective-permute-start(bf16[416,3200]{1,0:T(8,128)(2,1)S(1)} %bitcast.73), channel_id=1, source_target_pairs={{0,4},{4,8},{8,12},{12,0},{1,5},{5,9},{9,13},{13,1},{2,6},{6,10},{... | collective-permute-start | bytes 7987208 | tf_op jit(solution)/shard_map/ppermute | solution.py:16
  110.0 104.7 %collective-permute-start.21 = (bf16[384,3200]{1,0:T(8,128)(2,1)}, bf16[384,3200]{1,0:T(8,128)(2,1)S(1)}, u32[]{:S(2)}, u32[]{:S(2)}) collective-permute-start(bf16[384,3200]{1,0:T(8,128)(2,1)} %bitcast.40.refs_12_), channel_id=1, source_target_pairs={{0,1},{1,2},{2,3},{3,0},{4,5},{5,6},{6,7},{7,4},{8,9},{9,10},{10,1... | collective-permute-start | bytes 7372808 | tf_op jit(solution)/shard_map/ppermute | solution.py:16
  149.3 79.8 %collective-permute-start.16 = (bf16[416,3200]{1,0:T(8,128)(2,1)}, bf16[416,3200]{1,0:T(8,128)(2,1)}, u32[]{:S(2)}, u32[]{:S(2)}) collective-permute-start(bf16[416,3200]{1,0:T(8,128)(2,1)} %bitcast.35.refs_8_), channel_id=1, source_target_pairs={{0,3},{1,0},{2,1},{3,2},{4,7},{5,4},{6,5},{7,6},{8,11},{9,8},{10,9... | collective-permute-start | bytes 7987208 | tf_op jit(solution)/shard_map/ppermute | solution.py:16
  152.8 69.6 %collective-permute-start.9 = (bf16[384,3200]{1,0:T(8,128)(2,1)}, bf16[384,3200]{1,0:T(8,128)(2,1)S(1)}, u32[]{:S(2)}, u32[]{:S(2)}) collective-permute-start(bf16[384,3200]{1,0:T(8,128)(2,1)} %bitcast.30.refs_4_), channel_id=1, source_target_pairs={{0,4},{4,8},{8,12},{12,0},{1,5},{5,9},{9,13},{13,1},{2,6},{6,10},{... | collective-permute-start | bytes 7372808 | tf_op jit(solution)/shard_map/ppermute | solution.py:16
  214.7 7.8 copy-start.4
  214.7 68.1 %collective-permute-start.4 = (bf16[416,3200]{1,0:T(8,128)(2,1)S(1)}, bf16[416,3200]{1,0:T(8,128)(2,1)}, u32[]{:S(2)}, u32[]{:S(2)}) collective-permute-start(bf16[416,3200]{1,0:T(8,128)(2,1)S(1)} %bitcast.74), channel_id=1, source_target_pairs={{0,12},{4,0},{8,4},{12,8},{1,13},{5,1},{9,5},{13,9},{2,14},{6,2},{... | collective-permute-start | bytes 7987208 | tf_op jit(solution)/shard_map/ppermute | solution.py:16
  216.9 112.3 %collective-permute-start.17 = (bf16[416,3200]{1,0:T(8,128)(2,1)}, bf16[416,3200]{1,0:T(8,128)(2,1)}, u32[]{:S(2)}, u32[]{:S(2)}) collective-permute-start(bf16[416,3200]{1,0:T(8,128)(2,1)} %collective-permute-done.15.refs_9_), channel_id=1, source_target_pairs={{0,1},{1,2},{2,3},{3,0},{4,5},{5,6},{6,7},{7,4},{8,9},{9,10},{10,1... | collective-permute-start | bytes 7987208 | tf_op jit(solution)/shard_map/ppermute | solution.py:16
  218.9 110.3 %collective-permute-start.5 = (bf16[416,3200]{1,0:T(8,128)(2,1)}, bf16[416,3200]{1,0:T(8,128)(2,1)}, u32[]{:S(2)}, u32[]{:S(2)}) collective-permute-start(bf16[416,3200]{1,0:T(8,128)(2,1)} %collective-permute-done.3.refs_1_), channel_id=1, source_target_pairs={{0,4},{4,8},{8,12},{12,0},{1,5},{5,9},{9,13},{13,1},{2,6},{6,10},{... | collective-permute-start | bytes 7987208 | tf_op jit(solution)/shard_map/ppermute | solution.py:16
  222.5 1.4 copy-start
  223.9 58.9 %collective-permute-start.23 = (bf16[384,3200]{1,0:T(8,128)(2,1)}, bf16[384,3200]{1,0:T(8,128)(2,1)}, u32[]{:S(2)}, u32[]{:S(2)}) collective-permute-start(bf16[384,3200]{1,0:T(8,128)(2,1)} %collective-permute-done.22.refs_14_), channel_id=1, source_target_pairs={{0,3},{1,0},{2,1},{3,2},{4,7},{5,4},{6,5},{7,6},{8,11},{9,8},{10,9... | collective-permute-start | bytes 7372808 | tf_op jit(solution)/shard_map/ppermute | solution.py:16
  229.1 100.1 %collective-permute-start.11 = (bf16[384,3200]{1,0:T(8,128)(2,1)}, bf16[384,3200]{1,0:T(8,128)(2,1)}, u32[]{:S(2)}, u32[]{:S(2)}) collective-permute-start(bf16[384,3200]{1,0:T(8,128)(2,1)} %collective-permute-done.10.refs_6_), channel_id=1, source_target_pairs={{0,12},{4,0},{8,4},{12,8},{1,13},{5,1},{9,5},{13,9},{2,14},{6,2},{... | collective-permute-start | bytes 7372808 | tf_op jit(solution)/shard_map/ppermute | solution.py:16
  329.2 1.7 copy-start.1
  330.9 6.2 copy-start.2
  334.4 0.8 collective-permute-start.24
  340.7 0.8 collective-permute-start.25
  346.8 0.8 collective-permute-start.26
  353.3 0.8 collective-permute-start.27
  359.3 0.8 collective-permute-start.28
  365.6 0.8 collective-permute-start.29
  371.7 0.8 collective-permute-start.30
  378.0 0.8 collective-permute-start.31
  384.1 0.8 collective-permute-start.32
  390.5 0.8 collective-permute-start.33
  396.6 0.8 collective-permute-start.34
  402.9 0.8 collective-permute-start.35
  405.6 1.7 copy-start.3
  410.7 0.8 collective-permute-start.36
  417.0 278.7 %collective-permute-start.37 = (bf16[16,3200]{1,0:T(8,128)(2,1)S(1)}, bf16[16,3200]{1,0:T(8,128)(2,1)S(1)}, u32[]{:S(2)}, u32[]{:S(2)}) collective-permute-start(bf16[16,3200]{1,0:T(8,128)(2,1)S(1)} %half_layer.29), channel_id=1, source_target_pairs={{416,448},{417,449},{418,450},{419,451},{420,452},{421,453},{422,4... | collective-permute-start | bytes 307208 | tf_op jit(solution)/shard_map/ppermute | solution.py:181
  716.6 4.0 collective-permute-start.38
  728.1 0.7 collective-permute-start.39
  728.9 0.7 collective-permute-start.40
  729.6 0.7 collective-permute-start.41
  730.3 42.7 %collective-permute-start.42 = (bf16[16,3200]{1,0:T(8,128)(2,1)S(1)}, bf16[16,3200]{1,0:T(8,128)(2,1)S(1)}, u32[]{:S(2)}, u32[]{:S(2)}) collective-permute-start(bf16[16,3200]{1,0:T(8,128)(2,1)S(1)} %add.91), channel_id=1, source_target_pairs={{480,0},{224,256},{96,128},{352,384},{32,64},{288,320},{160,192},{... | collective-permute-start | bytes 307208 | tf_op jit(solution)/shard_map/ppermute | solution.py:190
Sparse Core Ops, SparseCore 0:
  232.7 56.5 all-gather.17

commit v3 on v1

v3 whole, which is shorter than its diff:
```python
import functools

import jax
import jax.numpy as jnp
from jax import lax
from jax.experimental import pallas as pl
from jax.experimental.pallas import tpu as pltpu
from jax.sharding import Mesh, PartitionSpec as P

SIDE = 4
OFFSETS = (0, 3, 1, 2)
INTRA = [(0, 1), (1, 0), (2, 3), (3, 2)]
INTER = [(0, 3), (3, 0), (1, 2), (2, 1)]


def moved(block, axis, by):
    route = [(i, (i + by) % SIDE) for i in range(SIDE)]
    return lax.ppermute(block, axis, route)


def ring(block, axis, halves):
    below = moved(block, axis, 1)
    above = moved(block, axis, -1)
    head = moved(halves(below)[0], axis, 1)
    tail = moved(halves(above)[1], axis, -1)
    return below, above, head, tail


def in_order(parts, place):
    rows, width = parts[0].shape
    whole = jnp.zeros((SIDE, rows, width), parts[0].dtype)
    for part, offset in zip(parts, OFFSETS):
        at = lax.rem(place + offset, SIDE)
        whole = lax.dynamic_update_slice(whole, part[None], (at, 0, 0))
    return whole.reshape(SIDE * rows, width)


def product(left, right):
    return lax.dot_general(
        left, right, (((1,), (1,)), ((), ())), preferred_element_type=jnp.float32
    )


def quarter_layer(state_ref, pair_ref, *refs):
    up_refs, down_refs = refs[:5], refs[5:9]
    out_ref, near_ref, far_ref, held_ref, hidden_ref, total_ref, sems = refs[9:]
    width = out_ref.shape[1]
    block = width // SIDE // SIDE

    @pl.when(state_ref[0] == 0)
    def _():
        out_ref[...] = jnp.zeros_like(out_ref)

    @pl.when(state_ref[0] == 1)
    def _():
        ups = [
            pltpu.make_async_copy(up_refs[i], near_ref.at[i], sems.at[SIDE + i])
            for i in range(3)
        ]
        ups += [
            pltpu.make_async_copy(up_refs[3 + i], far_ref.at[i], sems.at[SIDE + 3 + i])
            for i in range(2)
        ]
        for copy in ups:
            copy.start()
        copies = [
            pltpu.make_async_copy(down_refs[i], held_ref.at[i], sems.at[i])
            for i in range(SIDE)
        ]
        for copy in copies:
            copy.start()
        rows = pair_ref[0].astype(jnp.float32) + pair_ref[1].astype(jnp.float32)
        scale = lax.rsqrt(jnp.mean(rows * rows, axis=1, keepdims=True) + 1e-06)
        normed = (rows * scale).astype(jnp.bfloat16)
        y, x = state_ref[2], state_ref[3]
        for index, offset in enumerate(OFFSETS[:3]):
            ups[index].wait()
            part = product(normed, near_ref[index])
            hidden_ref[lax.rem(y + offset, SIDE)] = jax.nn.gelu(part)
        far = lax.rem(y + 2, SIDE)
        ups[3].wait()
        hidden_ref[far, :, :block] = jax.nn.gelu(product(normed, far_ref[0]))
        ups[4].wait()
        hidden_ref[far, :, block:] = jax.nn.gelu(product(normed, far_ref[1]))
        hidden = jnp.concatenate([hidden_ref[i] for i in range(SIDE)], axis=1)
        hidden = hidden.astype(jnp.bfloat16)

        mate = x + 1 - 2 * lax.rem(x, 2)
        for index, at in enumerate((x, mate, SIDE - 1 - x, SIDE - 1 - mate)):
            copies[index].wait()
            total_ref[at] = product(hidden, held_ref[index])
        base = jnp.where(state_ref[1] == 1, rows, 0.0)
        pieces = []
        for i in range(SIDE):
            for j in range(SIDE):
                pieces.append(total_ref[j][:, i * block : (i + 1) * block])
        total = jnp.concatenate(pieces, axis=1)
        out_ref[...] = (base + total).astype(jnp.bfloat16)


def apply_quarter(state, pair, up, down):
    _, row_count, width = pair.shape
    units = down[0].shape[1]
    resident = pl.BlockSpec(memory_space=pltpu.VMEM)
    anywhere = pl.BlockSpec(memory_space=pl.ANY)
    up = [pltpu.with_memory_space_constraint(piece, pltpu.HBM) for piece in up]
    down = [pltpu.with_memory_space_constraint(piece, pltpu.HBM) for piece in down]
    return pl.pallas_call(
        quarter_layer,
        out_shape=jax.ShapeDtypeStruct((row_count, width), jnp.bfloat16),
        in_specs=[pl.BlockSpec(memory_space=pltpu.SMEM)]
        + [resident]
        + [anywhere] * 9,
        out_specs=resident,
        scratch_shapes=[
            pltpu.VMEM((3,) + up[0].shape, jnp.bfloat16),
            pltpu.VMEM((2,) + up[3].shape, jnp.bfloat16),
            pltpu.VMEM((SIDE,) + down[0].shape, jnp.bfloat16),
            pltpu.VMEM((SIDE, row_count, units // SIDE), jnp.float32),
            pltpu.VMEM((SIDE, row_count, width // SIDE), jnp.float32),
            pltpu.SemaphoreType.DMA((SIDE + 5,)),
        ],
        compiler_params=pltpu.CompilerParams(vmem_limit_bytes=32 * 2**20),
        cost_estimate=pl.CostEstimate(
            flops=4 * row_count * width * units,
            bytes_accessed=2 * width * units,
            transcendentals=row_count * units,
        ),
        name="quarter_layer",
    )(state, pair, *up, *down)


def by_halves(low, block, other):
    first = jnp.where(low == 1, block, other)
    second = jnp.where(low == 1, other, block)
    return jnp.concatenate([first, second], axis=0)


def next_plane(layer):
    route = []
    for x, across in INTER:
        for core in range(2):
            to_chip = (x if x < 2 else across) if core == 0 else (x if x >= 2 else across)
            to_core = 0 if x < 2 else 1
            source = (layer * 2 + core) * SIDE + x
            route.append((source, ((layer + 1) * 2 + to_core) * SIDE + to_chip))
    return route


def on_device(layers, patches, w_in, w_out, w_proj):
    plane, core = lax.axis_index("z"), lax.axis_index("c")
    y, x = lax.axis_index("y"), lax.axis_index("x")
    tp = ("y", "x")
    own, wide = w_out.shape[1], w_out.shape[2]
    low = (x < 2).astype(jnp.int32)

    mate = lax.ppermute(w_in[0], "x", INTRA)
    near = by_halves((lax.rem(x, 2) == 0).astype(jnp.int32), w_in[0], mate)

    columns = w_out[0].reshape(own, SIDE, 2, wide // SIDE // 2)
    left = columns[:, :, 0].reshape(own, wide // 2)
    right = columns[:, :, 1].reshape(own, wide // 2)
    both = jnp.stack(
        [jnp.where(low == 1, left, right), jnp.where(low == 1, right, left)]
    )
    below, above, head, tail = ring(both, "y", lambda t: (t[0], t[1]))
    mine = in_order((both[0], below[0], above[0], head), y)
    other = in_order((both[1], below[1], above[1], tail), y)

    flat = patches.reshape(-1, patches.shape[2])
    rows = lax.all_to_all(flat, tp, split_axis=0, concat_axis=1, tiled=True)
    rows = by_halves(low, rows, lax.ppermute(rows, "x", INTER))
    other, rows = lax.optimization_barrier((other, rows))

    across = lax.ppermute(other, "x", INTER)
    beside = lax.ppermute(mine, "x", INTRA)
    corner = lax.ppermute(across, "x", INTRA)
    down = [mine, beside, across, corner]
    near, tail = lax.optimization_barrier((near, tail))
    half = near.shape[0] // 2
    up = [near, *ring(near, "y", lambda t: (t[:half], t[half:]))]
    projection = lax.all_gather(w_proj, tp, axis=0, tiled=True)

    adds = jnp.logical_and(core == 0, low == 1)
    pair = jnp.stack([rows, jnp.zeros_like(rows)])
    for layer in range(layers):
        state = jnp.stack([plane == layer, adds, y, x]).astype(jnp.int32)
        part = apply_quarter(state, pair, up, down)
        cores = lax.all_gather(part, "c", axis=0, tiled=False)
        part = cores[0].astype(jnp.float32) + cores[1].astype(jnp.float32)
        part = part.astype(jnp.bfloat16)
        if layer < layers - 1:
            part = lax.ppermute(part, ("z", "c", "x"), next_plane(layer))
            pair = lax.all_gather(part, "c", axis=0, tiled=False)

    count = part.shape[0] // 2
    kept = jnp.where(low == 1, part[:count], part[count:])
    sent = jnp.where(low == 1, part[count:], part[:count])
    got = lax.ppermute(sent, "x", INTER)
    total = kept.astype(jnp.float32) + got.astype(jnp.float32)
    rows = jnp.where(plane == layers - 1, total, 0.0).astype(jnp.bfloat16)
    holders = [layers - 1]
    step = layers // 2
    while step:
        route = [(held, (held + step) % layers) for held in holders]
        rows = rows + lax.ppermute(rows, "z", route)
        holders += [target for _, target in route]
        step //= 2
    return jnp.dot(rows, projection, preferred_element_type=jnp.float32).astype(
        jnp.bfloat16
    )


def solution(mesh):
    sections = mesh.shape["section"]
    grid = Mesh(
        mesh.devices.reshape(sections // 2, 2, SIDE, SIDE), ("z", "c", "y", "x")
    )
    section, tp = ("z", "c"), ("y", "x")
    return jax.shard_map(
        functools.partial(on_device, sections // 2),
        mesh=grid,
        in_specs=(
            P(None, None, tp),
            P(section, tp, None),
            P(section, tp, None),
            P(tp, section),
        ),
        out_specs=P(tp, section),
        check_vma=False,
    )
```

time: 693 us -> 713 us (1.029)
  Pallas kernels: 173 us -> 23 us
  waiting for transfers between devices: 385 us -> 498 us
  starting transfers between devices: 21.8 us -> 69.9 us
  blocking collectives: 33 us -> 64.9 us
  local copies, waits for them, and re-layouts: 54.8 us -> 25.5 us
    ppermute x15 -> x29, waiting for transfers between devices: 69.9 us -> 438 us  [the longest x15 259 us: on_device(): part = lax.ppermute(part, ('z', 'c', 'x'), next_plane(layer))]
    all_gather x3 -> x1, waiting for transfers between devices: 280 us -> 31.1 us  [on_device(): projection = lax.all_gather(w_proj, tp, axis=0, tiled=True)]
    pallas_call x16, Pallas kernels: 173 us -> 23 us  [apply_quarter(): pl.pallas_call(quarter_layer, out_shape=jax.ShapeDtypeStruct((row_count,...]
    unnamed x16 -> x12, local copies, waits for them, and re-layouts: 54.6 us -> 1.53 us
    ppermute x15 -> x29, starting transfers between devices: 11.4 us -> 60.7 us  [the longest x8 28.4 us: moved(): return lax.ppermute(block, axis, route)]
    all_gather x0 -> x16, blocking collectives: none -> 33.6 us  [on_device(): cores = lax.all_gather(part, 'c', axis=0, tiled=False)]
    ppermute x4, waiting for transfers between devices: 25.8 us -> 7.64 us  [on_device(): rows = rows + lax.ppermute(rows, 'z', route)]
    all_to_all x1, waiting for transfers between devices: 7.93 us -> 20.8 us  [on_device(): rows = lax.all_to_all(flat, tp, split_axis=0, concat_axis=1, tiled=True)]
  transfers between devices with their start and end apart: 23 -> 35, of which waited for: 6 -> 10; matrix products, arithmetic and copies ran while one was open for 0% -> 2% of each run, Pallas kernels for 6% -> 0%
where the time goes in v3:
time: 713 us; the launch traced here: 704 us
  waiting for transfers between devices  498 us (70%)
  starting transfers between devices  69.9 us (10%)
  blocking collectives  64.9 us (9%)
  local copies, waits for them, and re-layouts  25.5 us (4%)
  Pallas kernels  23 us (3%)
  between operations  14.5 us (2%)
    ppermute x15, waiting for transfers between devices, on_device(): part = lax.ppermute(part, ('z', 'c', 'x'), next_plane(layer))  259 us
    ppermute x8, waiting for transfers between devices, moved(): return lax.ppermute(block, axis, route)  76.2 us
    ppermute x1, waiting for transfers between devices, on_device(): corner = lax.ppermute(across, 'x', INTRA)  52.6 us
    ppermute x1, waiting for transfers between devices, on_device(): beside = lax.ppermute(mine, 'x', INTRA)  46.4 us
    all_gather x16, blocking collectives, on_device(): cores = lax.all_gather(part, 'c', axis=0, tiled=False)  33.6 us
    all_gather x15, blocking collectives, on_device(): pair = lax.all_gather(part, 'c', axis=0, tiled=False)  31.3 us
    all_gather x1, waiting for transfers between devices, on_device(): projection = lax.all_gather(w_proj, tp, axis=0, tiled=True)  31.1 us
    ppermute x8, starting transfers between devices, moved(): return lax.ppermute(block, axis, route)  28.4 us
  transfers between devices with their start and end apart: 35, of which 10 were waited for; matrix products, arithmetic and copies ran while one was open for 2% of the time, Pallas kernels for 0%

profile of v3, /device:TPU:448, one launch (start us, length us, event | category | flops | bytes accessed | tf_op | source)
XLA Modules:
  0.0 704.2 jit_solution(102791645598906509)
XLA Ops:
  6.5 5.9 reshape_squeeze.2
  12.5 3.2 fusion.4
  15.6 2.3 broadcast_select_fusion.2
  22.3 1.8 broadcast.30
  25.2 3.5 collective-permute-start
  28.7 3.6 collective-permute-start.1
  32.3 5.9 all-to-all-start
  38.3 3.8 collective-permute-start.4
  42.1 20.8 %all-to-all-done = bf16[16,16,200]{2,1,0:T(8,128)(2,1)S(1)} async-done(((bf16[16,16,200]{2,1,0:T(8,128)(2,1)}), bf16[16,16,200]{2,1,0:T(8,128)(2,1)S(1)}, u32[]{:S(2)}, u32[]{:S(2)}) %all-to-all-start) | async-done | bytes 102432 | tf_op jit(solution)/shard_map/all_to_all | solution.py:171
  63.2 4.7 collective-permute-start.3
  67.9 2.3 slice_bitcast_fusion
  70.2 2.4 slice_dynamic-update-slice_fusion
  72.5 4.9 collective-permute-start.2
  77.5 12.8 %collective-permute-done.2 = bf16[200,1600]{1,0:T(8,128)(2,1)S(1)} collective-permute-done((bf16[200,1600]{1,0:T(8,128)(2,1)S(1)}, bf16[200,1600]{1,0:T(8,128)(2,1)S(1)}, u32[]{:S(2)}, u32[]{:S(2)}) %collective-permute-start.2) | collective-permute-done | bytes 640032 | tf_op jit(solution)/shard_map/ppermute | solution.py:18
  91.2 2.4 collective-permute-start.11
  95.3 3.1 collective-permute-start.5
  98.4 4.4 collective-permute-start.6
  102.8 1.9 collective-permute-start.9
  104.7 63.4 %collective-permute-done.9 = bf16[200,1600]{1,0:T(8,128)(2,1)S(1)} collective-permute-done((bf16[200,1600]{1,0:T(8,128)(2,1)S(1)}, bf16[200,1600]{1,0:T(8,128)(2,1)S(1)}, u32[]{:S(2)}, u32[]{:S(2)}) %collective-permute-start.9) | collective-permute-done | bytes 640032 | tf_op jit(solution)/shard_map/ppermute | solution.py:18
  168.2 2.2 collective-permute-start.10
  170.4 3.7 collective-permute-start.12
  175.3 1.9 collective-permute-start.7
  179.2 5.1 collective-permute-start.8
  184.4 46.4 %collective-permute-done.10.refs_6_ = bf16[800,1600]{1,0:T(8,128)(2,1)} collective-permute-done((bf16[800,1600]{1,0:T(8,128)(2,1)S(1)}, bf16[800,1600]{1,0:T(8,128)(2,1)}, u32[]{:S(2)}, u32[]{:S(2)}) %collective-permute-start.10) | collective-permute-done | bytes 2560032 | tf_op jit(solution)/shard_map/ppermute | solution.py:176
  230.9 52.6 %collective-permute-done.12.refs_8_ = bf16[800,1600]{1,0:T(8,128)(2,1)} collective-permute-done((bf16[800,1600]{1,0:T(8,128)(2,1)}, bf16[800,1600]{1,0:T(8,128)(2,1)}, u32[]{:S(2)}, u32[]{:S(2)}) %collective-permute-start.12) | collective-permute-done | bytes 2560032 | tf_op jit(solution)/shard_map/ppermute | solution.py:177
  284.6 2.1 all-gather
  287.6 2.1 all-gather.1
  290.3 2.1 all-gather.2
  293.2 2.1 all-gather.3
  296.0 2.1 all-gather.4
  298.9 2.1 all-gather.5
  301.8 2.1 all-gather.6
  304.7 2.1 all-gather.7
  307.5 2.1 all-gather.8
  310.4 2.1 all-gather.9
  313.1 2.1 all-gather.10
  316.1 2.1 all-gather.11
  319.0 2.1 all-gather.12
  321.9 2.1 all-gather.13
  324.7 2.1 all-gather.14
  327.6 2.1 all-gather.15
  330.3 2.1 all-gather.16
  333.3 2.1 all-gather.17
  336.4 2.1 all-gather.18
  339.3 2.1 all-gather.19
  342.1 2.1 all-gather.20
  345.0 2.1 all-gather.21
  347.8 2.1 all-gather.22
  350.7 2.1 all-gather.23
  353.6 2.1 all-gather.24
  356.5 2.1 all-gather.25
  359.3 2.1 all-gather.26
  362.8 254.3 %collective-permute-done.26 = bf16[32,3200]{1,0:T(8,128)(2,1)S(1)} collective-permute-done((bf16[32,3200]{1,0:T(8,128)(2,1)S(1)}, bf16[32,3200]{1,0:T(8,128)(2,1)S(1)}, u32[]{:S(2)}, u32[]{:S(2)}) %collective-permute-start.26) | collective-permute-done | bytes 204832 | tf_op jit(solution)/shard_map/ppermute | solution.py:193
  617.1 2.1 all-gather.27
  619.2 11.6 %quarter_layer.30 = bf16[32,3200]{1,0:T(8,128)(2,1)S(1)} custom-call(s32[4]{0:T(128)S(1)} %add_add_fusion.1.state_ref, bf16[2,32,3200]{2,1,0:T(8,128)(2,1)S(1)} %bitcast.76, bf16[400,3200]{1,0:T(8,128)(2,1)} %copy-done.1, bf16[400,3200]{1,0:T(8,128)(2,1)} %copy-done.2, bf16[400,3200]{1,0:T(8,128)(2,1)} %copy-done.3, ...), custom_call_target="tpu_custom_call" | custom-call | flops 655360000 | bytes 10240000 | tf_op jit(solution)/shard_map/quarter_layer/pallas_call | solution.py:108
  630.9 2.1 all-gather.28
  634.4 4.8 collective-permute-done.27
  639.2 2.1 all-gather.29
  642.2 2.1 all-gather.30
  644.3 4.3 collective-permute-start.28
  648.6 3.9 collective-permute-done.28
  656.0 31.1 %all-gather.33.cloned.1.call-done = bf16[3200,256]{1,0:T(8,128)(2,1)} async-done(((bf16[200,256]{1,0:T(8,128)(2,1)}), bf16[3200,256]{1,0:T(8,128)(2,1)}) %all-gather.33.cloned.1.call-update) | async-done | bytes 1638416 | tf_op jit(solution)/shard_map/all_gather | solution.py:182
  687.1 7.6 %collective-permute-done.32 = bf16[16,3200]{1,0:T(8,128)(2,1)S(1)} collective-permute-done((bf16[16,3200]{1,0:T(8,128)(2,1)S(1)}, bf16[16,3200]{1,0:T(8,128)(2,1)S(1)}, u32[]{:S(2)}, u32[]{:S(2)}) %collective-permute-start.32) | collective-permute-done | bytes 102432 | tf_op jit(solution)/shard_map/ppermute | solution.py:206
  694.8 2.4 convolution_convert_fusion
  (126 shorter events, 40.0 us)
Async XLA Ops:
  20.3 1.1 copy-start.4
  25.2 42.6 %collective-permute-start = (bf16[2,200,1600]{2,1,0:T(8,128)(2,1)}, bf16[2,200,1600]{2,1,0:T(8,128)(2,1)}, u32[]{:S(2)}, u32[]{:S(2)}) collective-permute-start(bf16[2,200,1600]{2,1,0:T(8,128)(2,1)} %get-tuple-element.25), channel_id=1, source_target_pairs={{0,4},{4,8},{8,12},{12,0},{1,5},{5,9},{9,13},{13,1},{2,6},{6,10},{... | collective-permute-start | bytes 3840008 | tf_op jit(solution)/shard_map/ppermute | solution.py:18
  28.7 41.4 %collective-permute-start.1 = (bf16[2,200,1600]{2,1,0:T(8,128)(2,1)}, bf16[2,200,1600]{2,1,0:T(8,128)(2,1)}, u32[]{:S(2)}, u32[]{:S(2)}) collective-permute-start(bf16[2,200,1600]{2,1,0:T(8,128)(2,1)} %get-tuple-element.25), channel_id=1, source_target_pairs={{0,12},{4,0},{8,4},{12,8},{1,13},{5,1},{9,5},{13,9},{2,14},{6,2},{... | collective-permute-start | bytes 3840008 | tf_op jit(solution)/shard_map/ppermute | solution.py:18
  32.3 30.6 %all-to-all-start = ((bf16[16,16,200]{2,1,0:T(8,128)(2,1)}), bf16[16,16,200]{2,1,0:T(8,128)(2,1)S(1)}, u32[]{:S(2)}, u32[]{:S(2)}) async-start(bf16[16,16,200]{2,1,0:T(8,128)(2,1)} %bitcast.22), calls=%async_computation | async-start | bytes 262144 | tf_op jit(solution)/shard_map/all_to_all | solution.py:171
  38.2 648.9 %all-gather.33.cloned.1.call-start = ((), (), s32[]{:S(2)}) async-start(), calls=%async_computation.1 | async-start | bytes 1740800 | tf_op jit(solution)/shard_map/all_gather | solution.py:182
  38.3 55.3 %collective-permute-start.4 = (bf16[200,3200]{1,0:T(8,128)(2,1)}, bf16[200,3200]{1,0:T(8,128)(2,1)}, u32[]{:S(2)}, u32[]{:S(2)}) collective-permute-start(bf16[200,3200]{1,0:T(8,128)(2,1)} %bitcast.94), channel_id=1, source_target_pairs={{0,1},{1,0},{2,3},{3,2},{4,5},{5,4},{6,7},{7,6},{8,9},{9,8},{10,11... | collective-permute-start | bytes 3840008 | tf_op jit(solution)/shard_map/ppermute | solution.py:157
  63.2 14.3 %collective-permute-start.3 = (bf16[16,3200]{1,0:T(8,128)(2,1)S(1)}, bf16[16,3200]{1,0:T(8,128)(2,1)S(1)}, u32[]{:S(2)}, u32[]{:S(2)}) collective-permute-start(bf16[16,3200]{1,0:T(8,128)(2,1)S(1)} %all_to_all.17), channel_id=1, source_target_pairs={{0,3},{3,0},{1,2},{2,1},{4,7},{7,4},{5,6},{6,5},{8,11},{11,8},{9,1... | collective-permute-start | bytes 307208 | tf_op jit(solution)/shard_map/ppermute | solution.py:172
  70.1 23.4 %copy-start.5 = (bf16[1,200,3200]{2,1,0:T(8,128)(2,1)S(1)}, bf16[1,200,3200]{2,1,0:T(8,128)(2,1)}, u32[]{:S(2)}) copy-start(bf16[1,200,3200]{2,1,0:T(8,128)(2,1)} %param.5) | copy-start | bytes 3840004
  72.5 17.7 %collective-permute-start.2 = (bf16[200,1600]{1,0:T(8,128)(2,1)S(1)}, bf16[200,1600]{1,0:T(8,128)(2,1)S(1)}, u32[]{:S(2)}, u32[]{:S(2)}) collective-permute-start(bf16[200,1600]{1,0:T(8,128)(2,1)S(1)} %get-tuple-element.21), channel_id=1, source_target_pairs={{0,12},{4,0},{8,4},{12,8},{1,13},{5,1},{9,5},{13,9},{2,14},{6,2},{... | collective-permute-start | bytes 1920008 | tf_op jit(solution)/shard_map/ppermute | solution.py:18
  91.2 79.2 %collective-permute-start.11 = (bf16[800,1600]{1,0:T(8,128)(2,1)}, bf16[800,1600]{1,0:T(8,128)(2,1)}, u32[]{:S(2)}, u32[]{:S(2)}) collective-permute-start(bf16[800,1600]{1,0:T(8,128)(2,1)} %bitcast.21), channel_id=1, source_target_pairs={{0,3},{3,0},{1,2},{2,1},{4,7},{7,4},{5,6},{6,5},{8,11},{11,8},{9,1... | collective-permute-start | bytes 7680008 | tf_op jit(solution)/shard_map/ppermute | solution.py:175
  95.3 83.3 %copy-start.1 = (bf16[400,3200]{1,0:T(8,128)(2,1)}, bf16[400,3200]{1,0:T(8,128)(2,1)S(1)}, u32[]{:S(2)}) copy-start(bf16[400,3200]{1,0:T(8,128)(2,1)S(1)} %pad_maximum_fusion.refs_0_) | copy-start | bytes 7680004
  95.3 78.8 %collective-permute-start.5 = (bf16[400,3200]{1,0:T(8,128)(2,1)S(1)}, bf16[400,3200]{1,0:T(8,128)(2,1)S(1)}, u32[]{:S(2)}, u32[]{:S(2)}) collective-permute-start(bf16[400,3200]{1,0:T(8,128)(2,1)S(1)} %pad_maximum_fusion.refs_0_), channel_id=1, source_target_pairs={{0,4},{4,8},{8,12},{12,0},{1,5},{5,9},{9,13},{13,1},{2,6},{6,10},{... | collective-permute-start | bytes 7680008 | tf_op jit(solution)/shard_map/ppermute | solution.py:18
  98.4 78.9 %collective-permute-start.6 = (bf16[400,3200]{1,0:T(8,128)(2,1)S(1)}, bf16[400,3200]{1,0:T(8,128)(2,1)S(1)}, u32[]{:S(2)}, u32[]{:S(2)}) collective-permute-start(bf16[400,3200]{1,0:T(8,128)(2,1)S(1)} %pad_maximum_fusion.refs_0_), channel_id=1, source_target_pairs={{0,12},{4,0},{8,4},{12,8},{1,13},{5,1},{9,5},{13,9},{2,14},{6,2},{... | collective-permute-start | bytes 7680008 | tf_op jit(solution)/shard_map/ppermute | solution.py:18
  102.8 65.3 %collective-permute-start.9 = (bf16[200,1600]{1,0:T(8,128)(2,1)S(1)}, bf16[200,1600]{1,0:T(8,128)(2,1)S(1)}, u32[]{:S(2)}, u32[]{:S(2)}) collective-permute-start(bf16[200,1600]{1,0:T(8,128)(2,1)S(1)} %get-tuple-element.17), channel_id=1, source_target_pairs={{0,4},{4,8},{8,12},{12,0},{1,5},{5,9},{9,13},{13,1},{2,6},{6,10},{... | collective-permute-start | bytes 1920008 | tf_op jit(solution)/shard_map/ppermute | solution.py:18
  168.2 10.4 %copy-start = (bf16[4,200,1600]{2,1,0:T(8,128)(2,1)}, bf16[4,200,1600]{2,1,0:T(8,128)(2,1)S(1)}, u32[]{:S(2)}) copy-start(bf16[4,200,1600]{2,1,0:T(8,128)(2,1)S(1)} %bitcast_dynamic-update-slice_fusion) | copy-start | bytes 7680004
  168.2 62.7 %collective-permute-start.10 = (bf16[800,1600]{1,0:T(8,128)(2,1)S(1)}, bf16[800,1600]{1,0:T(8,128)(2,1)}, u32[]{:S(2)}, u32[]{:S(2)}) collective-permute-start(bf16[800,1600]{1,0:T(8,128)(2,1)S(1)} %bitcast.77), channel_id=1, source_target_pairs={{0,1},{1,0},{2,3},{3,2},{4,5},{5,4},{6,7},{7,6},{8,9},{9,8},{10,11... | collective-permute-start | bytes 7680008 | tf_op jit(solution)/shard_map/ppermute | solution.py:176
  170.4 113.1 %collective-permute-start.12 = (bf16[800,1600]{1,0:T(8,128)(2,1)}, bf16[800,1600]{1,0:T(8,128)(2,1)}, u32[]{:S(2)}, u32[]{:S(2)}) collective-permute-start(bf16[800,1600]{1,0:T(8,128)(2,1)} %collective-permute-done.11.refs_7_), channel_id=1, source_target_pairs={{0,1},{1,0},{2,3},{3,2},{4,5},{5,4},{6,7},{7,6},{8,9},{9,8},{10,11... | collective-permute-start | bytes 7680008 | tf_op jit(solution)/shard_map/ppermute | solution.py:177
  174.1 3.2 copy-start.2
  175.3 55.5 %collective-permute-start.7 = (bf16[200,3200]{1,0:T(8,128)(2,1)}, bf16[200,3200]{1,0:T(8,128)(2,1)}, u32[]{:S(2)}, u32[]{:S(2)}) collective-permute-start(bf16[200,3200]{1,0:T(8,128)(2,1)} %slice.210), channel_id=1, source_target_pairs={{0,4},{4,8},{8,12},{12,0},{1,5},{5,9},{9,13},{13,1},{2,6},{6,10},{... | collective-permute-start | bytes 3840008 | tf_op jit(solution)/shard_map/ppermute | solution.py:18
  177.3 1.9 copy-start.3
  179.2 51.7 %collective-permute-start.8 = (bf16[200,3200]{1,0:T(8,128)(2,1)}, bf16[200,3200]{1,0:T(8,128)(2,1)}, u32[]{:S(2)}, u32[]{:S(2)}) collective-permute-start(bf16[200,3200]{1,0:T(8,128)(2,1)} %slice.211), channel_id=1, source_target_pairs={{0,12},{4,0},{8,4},{12,8},{1,13},{5,1},{9,5},{13,9},{2,14},{6,2},{... | collective-permute-start | bytes 3840008 | tf_op jit(solution)/shard_map/ppermute | solution.py:18
  286.8 0.8 collective-permute-start.13
  292.5 0.8 collective-permute-start.14
  298.1 0.8 collective-permute-start.15
  304.0 0.8 collective-permute-start.16
  309.6 0.8 collective-permute-start.17
  315.3 0.8 collective-permute-start.18
  321.2 0.8 collective-permute-start.19
  326.8 0.8 collective-permute-start.20
  332.5 0.8 collective-permute-start.21
  338.6 0.8 collective-permute-start.22
  344.2 0.8 collective-permute-start.23
  349.9 0.8 collective-permute-start.24
  355.7 0.8 collective-permute-start.25
  361.4 255.7 %collective-permute-start.26 = (bf16[32,3200]{1,0:T(8,128)(2,1)S(1)}, bf16[32,3200]{1,0:T(8,128)(2,1)S(1)}, u32[]{:S(2)}, u32[]{:S(2)}) collective-permute-start(bf16[32,3200]{1,0:T(8,128)(2,1)S(1)} %add_convert_fusion.2), channel_id=1, source_target_pairs={{416,448},{432,451},{419,464},{435,467},{417,449},{433,450},{418,4... | collective-permute-start | bytes 614408 | tf_op jit(solution)/shard_map/ppermute | solution.py:193
  633.0 6.2 collective-permute-start.27
  644.3 8.2 %collective-permute-start.28 = (bf16[16,3200]{1,0:T(8,128)(2,1)S(1)}, bf16[16,3200]{1,0:T(8,128)(2,1)S(1)}, u32[]{:S(2)}, u32[]{:S(2)}) collective-permute-start(bf16[16,3200]{1,0:T(8,128)(2,1)S(1)} %select_bitcast_fusion), channel_id=1, source_target_pairs={{0,3},{3,0},{1,2},{2,1},{4,7},{7,4},{5,6},{6,5},{8,11},{11,8},{9,1... | collective-permute-start | bytes 307208 | tf_op jit(solution)/shard_map/ppermute | solution.py:199
  652.6 0.7 collective-permute-start.29
  653.3 0.7 collective-permute-start.30
  654.0 0.7 collective-permute-start.31
  654.7 40.0 %collective-permute-start.32 = (bf16[16,3200]{1,0:T(8,128)(2,1)S(1)}, bf16[16,3200]{1,0:T(8,128)(2,1)S(1)}, u32[]{:S(2)}, u32[]{:S(2)}) collective-permute-start(bf16[16,3200]{1,0:T(8,128)(2,1)S(1)} %add.135), channel_id=1, source_target_pairs={{480,0},{224,256},{96,128},{352,384},{32,64},{288,320},{160,192},{... | collective-permute-start | bytes 307208 | tf_op jit(solution)/shard_map/ppermute | solution.py:206
Sparse Core Ops, SparseCore 0:
  634.5 52.6 all-gather.32

commit v4 on v3

v4 whole, which is shorter than its diff:
```python
import functools

import jax
import jax.numpy as jnp
from jax import lax
from jax.experimental import pallas as pl
from jax.experimental.pallas import tpu as pltpu
from jax.sharding import Mesh, PartitionSpec as P

SIDE = 4
OFFSETS = (0, 3, 1, 2)
INTRA = [(0, 1), (1, 0), (2, 3), (3, 2)]
INTER = [(0, 3), (3, 0), (1, 2), (2, 1)]


def moved(block, axis, by):
    route = [(i, (i + by) % SIDE) for i in range(SIDE)]
    return lax.ppermute(block, axis, route)


def ring(block, axis, halves):
    below = moved(block, axis, 1)
    above = moved(block, axis, -1)
    head = moved(halves(below)[0], axis, 1)
    tail = moved(halves(above)[1], axis, -1)
    return below, above, head, tail


def in_order(parts, place):
    whole = jnp.zeros((SIDE,) + parts[0].shape, parts[0].dtype)
    for part, offset in zip(parts, OFFSETS):
        at = lax.rem(place + offset, SIDE)
        whole = lax.dynamic_update_slice(whole, part[None], (at, 0, 0))
    return whole


def run_all(copies):
    for copy in copies:
        copy.start()
    for copy in copies:
        copy.wait()


def early(spots_ref, *refs):
    sources, (up_ref, down_ref, sems) = refs[:6], refs[6:]
    copies = []
    for i in range(3):
        to_up, to_down = up_ref.at[spots_ref[i]], down_ref.at[spots_ref[SIDE + i]]
        copies.append(pltpu.make_async_copy(sources[i], to_up, sems.at[i]))
        copies.append(pltpu.make_async_copy(sources[3 + i], to_down, sems.at[3 + i]))
    run_all(copies)


def late(spots_ref, head_ref, tail_ref, corner_ref, *refs):
    up_ref, down_ref, sems = refs[2:]
    cut, whole = head_ref.shape[1], up_ref.shape[2]
    far = up_ref.at[spots_ref[SIDE - 1]]
    corner = down_ref.at[spots_ref[2 * SIDE - 1]]
    copies = [
        pltpu.make_async_copy(head_ref, far.at[:, :cut], sems.at[0]),
        pltpu.make_async_copy(tail_ref, far.at[:, cut:whole], sems.at[1]),
        pltpu.make_async_copy(corner_ref, corner, sems.at[2]),
    ]
    run_all(copies)


def put_early(spots, *pieces):
    kind = pieces[0].dtype
    anywhere = pl.BlockSpec(memory_space=pl.ANY)
    return pl.pallas_call(
        early,
        out_shape=(
            jax.ShapeDtypeStruct((SIDE,) + pieces[0].shape, kind),
            jax.ShapeDtypeStruct((SIDE,) + pieces[3].shape, kind),
        ),
        in_specs=[pl.BlockSpec(memory_space=pltpu.SMEM)] + [anywhere] * 6,
        out_specs=(anywhere, anywhere),
        scratch_shapes=[pltpu.SemaphoreType.DMA((6,))],
        compiler_params=pltpu.CompilerParams(vmem_limit_bytes=2**20),
        name="put_early",
    )(spots, *pieces)


def put_late(spots, head, tail, corner, up, down):
    anywhere = pl.BlockSpec(memory_space=pl.ANY)
    return pl.pallas_call(
        late,
        out_shape=(
            jax.ShapeDtypeStruct(up.shape, up.dtype),
            jax.ShapeDtypeStruct(down.shape, down.dtype),
        ),
        in_specs=[pl.BlockSpec(memory_space=pltpu.SMEM)] + [anywhere] * 5,
        out_specs=(anywhere, anywhere),
        scratch_shapes=[pltpu.SemaphoreType.DMA((3,))],
        input_output_aliases={4: 0, 5: 1},
        compiler_params=pltpu.CompilerParams(vmem_limit_bytes=2**20),
        name="put_late",
    )(spots, head, tail, corner, up, down)


def product(left, right):
    return lax.dot_general(
        left, right, (((1,), (1,)), ((), ())), preferred_element_type=jnp.float32
    )


def quarter_layer(tick_ref, state_ref, pair_ref, up_ref, down_ref, out_ref, *scratch):
    hidden_ref, total_ref = scratch
    width = out_ref.shape[1]
    step = up_ref.shape[1]
    block = width // SIDE // SIDE
    active = tick_ref[0] == state_ref[0]

    @pl.when(jnp.logical_not(active))
    def _():
        out_ref[...] = jnp.zeros_like(out_ref)

    @pl.when(active)
    def _():
        rows = pair_ref[0].astype(jnp.float32) + pair_ref[1].astype(jnp.float32)
        scale = lax.rsqrt(jnp.mean(rows * rows, axis=1, keepdims=True) + 1e-06)
        normed = (rows * scale).astype(jnp.bfloat16)
        for i in range(SIDE):
            part = jax.nn.gelu(product(normed, up_ref[i])).astype(jnp.bfloat16)
            hidden_ref[:, i * step : (i + 1) * step] = part
        hidden = hidden_ref[...]
        for i in range(SIDE):
            total_ref[i] = product(hidden, down_ref[i])
        base = jnp.where(state_ref[1] == 1, rows, 0.0)
        pieces = []
        for i in range(SIDE):
            for j in range(SIDE):
                pieces.append(total_ref[j][:, i * block : (i + 1) * block])
        total = jnp.concatenate(pieces, axis=1)
        out_ref[...] = (base + total).astype(jnp.bfloat16)


def apply_quarter(tick, state, pair, up, down):
    _, row_count, width = pair.shape
    units = down.shape[2]
    resident = pl.BlockSpec(memory_space=pltpu.VMEM)
    scalar = pl.BlockSpec(memory_space=pltpu.SMEM)
    return pl.pallas_call(
        quarter_layer,
        out_shape=jax.ShapeDtypeStruct((row_count, width), jnp.bfloat16),
        in_specs=[scalar] * 2 + [resident] * 3,
        out_specs=resident,
        scratch_shapes=[
            pltpu.VMEM((row_count, units), jnp.bfloat16),
            pltpu.VMEM((SIDE, row_count, width // SIDE), jnp.float32),
        ],
        compiler_params=pltpu.CompilerParams(vmem_limit_bytes=10 * 2**20),
        cost_estimate=pl.CostEstimate(
            flops=4 * row_count * width * units,
            bytes_accessed=4 * row_count * width,
            transcendentals=row_count * units,
        ),
        name="quarter_layer",
    )(tick, state, pair, up, down)


def add_pair(pair_ref, out_ref):
    total = pair_ref[0].astype(jnp.float32) + pair_ref[1].astype(jnp.float32)
    out_ref[...] = total.astype(out_ref.dtype)


def added(pair):
    resident = pl.BlockSpec(memory_space=pltpu.VMEM)
    return pl.pallas_call(
        add_pair,
        out_shape=jax.ShapeDtypeStruct(pair.shape[1:], pair.dtype),
        in_specs=[resident],
        out_specs=resident,
        compiler_params=pltpu.CompilerParams(vmem_limit_bytes=2 * 2**20),
        cost_estimate=pl.CostEstimate(
            flops=pair.size, bytes_accessed=pair.size, transcendentals=0
        ),
        name="add_pair",
    )(pair)


def split_columns(low_ref, block_ref, out_ref):
    width = block_ref.shape[1] // SIDE // 2
    low = low_ref[0] == 1
    for i in range(SIDE):
        left = block_ref[:, 2 * i * width : (2 * i + 1) * width]
        right = block_ref[:, (2 * i + 1) * width : (2 * i + 2) * width]
        out_ref[0, :, i * width : (i + 1) * width] = jnp.where(low, left, right)
        out_ref[1, :, i * width : (i + 1) * width] = jnp.where(low, right, left)


def own_and_other(low, block):
    rows, width = block.shape
    resident = pl.BlockSpec(memory_space=pltpu.VMEM)
    return pl.pallas_call(
        split_columns,
        out_shape=jax.ShapeDtypeStruct((2, rows, width // 2), block.dtype),
        in_specs=[pl.BlockSpec(memory_space=pltpu.SMEM), resident],
        out_specs=resident,
        compiler_params=pltpu.CompilerParams(vmem_limit_bytes=10 * 2**20),
        name="split_columns",
    )(low.reshape(1), block)


def by_halves(low, block, other):
    first = jnp.where(low == 1, block, other)
    second = jnp.where(low == 1, other, block)
    return jnp.concatenate([first, second], axis=0)


def next_plane(layer):
    route = []
    for x, across in INTER:
        for core in range(2):
            to_chip = (x if x < 2 else across) if core == 0 else (x if x >= 2 else across)
            to_core = 0 if x < 2 else 1
            source = (layer * 2 + core) * SIDE + x
            route.append((source, ((layer + 1) * 2 + to_core) * SIDE + to_chip))
    return route


def on_device(layers, patches, w_in, w_out, w_proj):
    plane, core = lax.axis_index("z"), lax.axis_index("c")
    y, x = lax.axis_index("y"), lax.axis_index("x")
    tp = ("y", "x")
    low = (x < 2).astype(jnp.int32)

    mate = lax.ppermute(w_in[0], "x", INTRA)
    near = by_halves((lax.rem(x, 2) == 0).astype(jnp.int32), w_in[0], mate)

    both = own_and_other(low, w_out[0])
    below, above, head, tail = ring(both, "y", lambda t: (t[0], t[1]))
    mine = in_order((both[0], below[0], above[0], head), y)
    other = in_order((both[1], below[1], above[1], tail), y)

    flat = patches.reshape(-1, patches.shape[2])
    rows = lax.all_to_all(flat, tp, split_axis=0, concat_axis=1, tiled=True)
    rows = by_halves(low, rows, lax.ppermute(rows, "x", INTER))
    other, rows = lax.optimization_barrier((other, rows))

    mine = mine.reshape(-1, mine.shape[2])
    other = other.reshape(mine.shape)
    across = lax.ppermute(other, "x", INTER)
    beside = lax.ppermute(mine, "x", INTRA)
    corner = lax.ppermute(across, "x", INTRA)
    mate_x = x + 1 - 2 * lax.rem(x, 2)
    near, head, tail = lax.optimization_barrier((near, head, tail))
    cut = near.shape[1] // 256 * 128
    below, above, head, tail = ring(near, "y", lambda t: (t[:, :cut], t[:, cut:]))
    spots = [y, lax.rem(y + 3, SIDE), lax.rem(y + 1, SIDE), lax.rem(y + 2, SIDE)]
    spots += [x, mate_x, SIDE - 1 - x, SIDE - 1 - mate_x]
    spots = jnp.stack(spots).astype(jnp.int32)
    up, down = put_early(spots, near, below, above, mine, beside, across)
    up, down = put_late(spots, head, tail, corner, up, down)
    up = pltpu.with_memory_space_constraint(up, pltpu.VMEM)
    down = pltpu.with_memory_space_constraint(down, pltpu.VMEM)
    projection = lax.all_gather(w_proj, tp, axis=0, tiled=True)

    adds = jnp.logical_and(core == 0, low == 1)
    state = jnp.stack([plane, adds]).astype(jnp.int32)
    pair = jnp.stack([rows, jnp.zeros_like(rows)])
    pair, state, projection = lax.optimization_barrier((pair, state, projection))
    for layer in range(layers):
        tick = jnp.full((1,), layer, jnp.int32)
        part = apply_quarter(tick, state, pair, up, down)
        part = added(lax.all_gather(part, "c", axis=0, tiled=False))
        if layer < layers - 1:
            part = lax.ppermute(part, ("z", "c", "x"), next_plane(layer))
            pair = lax.all_gather(part, "c", axis=0, tiled=False)

    count = part.shape[0] // 2
    kept = jnp.where(low == 1, part[:count], part[count:])
    sent = jnp.where(low == 1, part[count:], part[:count])
    got = lax.ppermute(sent, "x", INTER)
    total = kept.astype(jnp.float32) + got.astype(jnp.float32)
    rows = jnp.where(plane == layers - 1, total, 0.0).astype(jnp.bfloat16)
    holders = [layers - 1]
    step = layers // 2
    while step:
        route = [(held, (held + step) % layers) for held in holders]
        rows = rows + lax.ppermute(rows, "z", route)
        holders += [target for _, target in route]
        step //= 2
    return jnp.dot(rows, projection, preferred_element_type=jnp.float32).astype(
        jnp.bfloat16
    )


def solution(mesh):
    sections = mesh.shape["section"]
    grid = Mesh(
        mesh.devices.reshape(sections // 2, 2, SIDE, SIDE), ("z", "c", "y", "x")
    )
    section, tp = ("z", "c"), ("y", "x")
    return jax.shard_map(
        functools.partial(on_device, sections // 2),
        mesh=grid,
        in_specs=(
            P(None, None, tp),
            P(section, tp, None),
            P(section, tp, None),
            P(tp, section),
        ),
        out_specs=P(tp, section),
        check_vma=False,
    )
```

time: 713 us -> 560 us (0.79)
  waiting for transfers between devices: 498 us -> 361 us
  local copies, waits for them, and re-layouts: 25.5 us -> 16.5 us
    ppermute x15, waiting for transfers between devices: 259 us -> 187 us  [on_device(): part = lax.ppermute(part, ('z', 'c', 'x'), next_plane(layer))]
    ppermute x1, waiting for transfers between devices: 0.01 us -> 47.6 us  [on_device(): across = lax.ppermute(other, 'x', INTER)]
    ppermute x1, waiting for transfers between devices: 46.4 us -> 0.06 us  [on_device(): beside = lax.ppermute(mine, 'x', INTRA)]
    ppermute x8, waiting for transfers between devices: 76.2 us -> 33.8 us  [moved(): return lax.ppermute(block, axis, route)]
    all_gather x1, waiting for transfers between devices: 31.1 us -> 0.02 us  [on_device(): projection = lax.all_gather(w_proj, tp, axis=0, tiled=True)]
    ppermute x4, waiting for transfers between devices: 7.64 us -> 33.3 us  [on_device(): rows = rows + lax.ppermute(rows, 'z', route)]
    ppermute x1, waiting for transfers between devices: 52.6 us -> 31.4 us  [on_device(): corner = lax.ppermute(across, 'x', INTRA)]
    pallas_call x0 -> x19, Pallas kernels: none -> 11.4 us  [the longest x1 5.43 us: put_early(): pl.pallas_call(early, out_shape=(jax.ShapeDtypeStruct((SIDE,) + pieces[0]...]
  transfers between devices with their start and end apart: 35 -> 35, of which waited for: 10 -> 11; matrix products, arithmetic and copies ran while one was open for 2% -> 3% of each run, Pallas kernels for 0% -> 1%
where the time goes in v4:
time: 560 us; the launch traced here: 553 us
  waiting for transfers between devices  361 us (64%)
  blocking collectives  65.3 us (12%)
  starting transfers between devices  63.4 us (11%)
  Pallas kernels  27.5 us (5%)
  local copies, waits for them, and re-layouts  16.5 us (3%)
  between operations  14.7 us (3%)
    ppermute x15, waiting for transfers between devices, on_device(): part = lax.ppermute(part, ('z', 'c', 'x'), next_plane(layer))  187 us
    ppermute x1, waiting for transfers between devices, on_device(): across = lax.ppermute(other, 'x', INTER)  47.6 us
    ppermute x8, waiting for transfers between devices, moved(): return lax.ppermute(block, axis, route)  33.8 us
    all_gather x16, blocking collectives, on_device(): part = added(lax.all_gather(part, 'c', axis=0, tiled=False))  33.7 us
    ppermute x4, waiting for transfers between devices, on_device(): rows = rows + lax.ppermute(rows, 'z', route)  33.3 us
    all_gather x15, blocking collectives, on_device(): pair = lax.all_gather(part, 'c', axis=0, tiled=False)  31.6 us
    ppermute x1, waiting for transfers between devices, on_device(): corner = lax.ppermute(across, 'x', INTRA)  31.4 us
    ppermute x8, starting transfers between devices, moved(): return lax.ppermute(block, axis, route)  25.1 us
  transfers between devices with their start and end apart: 35, of which 11 were waited for; matrix products, arithmetic and copies ran while one was open for 3% of the time, Pallas kernels for 1%

profile of v4, /device:TPU:448, one launch (start us, length us, event | category | flops | bytes accessed | tf_op | source)
XLA Modules:
  0.0 552.7 jit_solution(17763344383049194401)
XLA Ops:
  7.8 2.1 split_columns.1
  9.9 3.5 collective-permute-start
  13.4 3.6 collective-permute-start.1
  17.0 3.4 collective-permute-start.4
  20.4 5.5 %all-to-all-start = ((bf16[16,16,200]{2,1,0:T(8,128)(2,1)}), bf16[16,16,200]{2,1,0:T(8,128)(2,1)S(1)}, u32[]{:S(2)}, u32[]{:S(2)}) async-start(bf16[16,16,200]{2,1,0:T(8,128)(2,1)} %bitcast.98), calls=%async_computation | async-start | bytes 262144 | tf_op jit(solution)/shard_map/all_to_all | solution.py:237
  30.3 22.9 %all-to-all-done = bf16[16,16,200]{2,1,0:T(8,128)(2,1)S(1)} async-done(((bf16[16,16,200]{2,1,0:T(8,128)(2,1)}), bf16[16,16,200]{2,1,0:T(8,128)(2,1)S(1)}, u32[]{:S(2)}, u32[]{:S(2)}) %all-to-all-start) | async-done | bytes 102432 | tf_op jit(solution)/shard_map/all_to_all | solution.py:237
  53.5 2.5 collective-permute-start.3
  56.0 2.3 slice_dynamic-update-slice_fusion.4
  58.3 2.4 slice_dynamic-update-slice_fusion
  60.7 3.3 collective-permute-start.2
  64.0 2.6 collective-permute-start.5
  66.6 10.7 %collective-permute-done.2 = bf16[200,1600]{1,0:T(8,128)(2,1)S(1)} collective-permute-done((bf16[200,1600]{1,0:T(8,128)(2,1)S(1)}, bf16[200,1600]{1,0:T(8,128)(2,1)S(1)}, u32[]{:S(2)}, u32[]{:S(2)}) %collective-permute-start.2) | collective-permute-done | bytes 640032 | tf_op jit(solution)/shard_map/ppermute | solution.py:18
  78.2 4.5 collective-permute-start.10
  85.9 3.9 collective-permute-start.8
  89.9 1.9 collective-permute-start.6
  91.9 1.9 collective-permute-start.12
  93.8 47.6 %collective-permute-done.10.refs_5_ = bf16[800,1600]{1,0:T(8,128)(2,1)} collective-permute-done((bf16[800,1600]{1,0:T(8,128)(2,1)}, bf16[800,1600]{1,0:T(8,128)(2,1)}, u32[]{:S(2)}, u32[]{:S(2)}) %collective-permute-start.10) | collective-permute-done | bytes 2560032 | tf_op jit(solution)/shard_map/ppermute | solution.py:243
  141.4 1.9 collective-permute-start.11
  143.3 7.8 %collective-permute-done.8.refs_2_ = bf16[400,3200]{1,0:T(8,128)(2,1)} collective-permute-done((bf16[400,3200]{1,0:T(8,128)(2,1)}, bf16[400,3200]{1,0:T(8,128)(2,1)}, u32[]{:S(2)}, u32[]{:S(2)}) %collective-permute-start.8) | collective-permute-done | bytes 2560032 | tf_op jit(solution)/shard_map/ppermute | solution.py:18
  151.1 2.5 slice.49
  153.6 4.5 collective-permute-start.9
  158.1 2.4 slice.48
  160.6 1.9 collective-permute-start.7
  162.8 5.4 put_early.1
  168.2 15.3 %collective-permute-done.7.head_ref = bf16[400,1536]{1,0:T(8,128)(2,1)} collective-permute-done((bf16[400,1536]{1,0:T(8,128)(2,1)}, bf16[400,1536]{1,0:T(8,128)(2,1)}, u32[]{:S(2)}, u32[]{:S(2)}) %collective-permute-start.7) | collective-permute-done | bytes 1228832 | tf_op jit(solution)/shard_map/ppermute | solution.py:18
  183.5 31.4 %collective-permute-done.11.corner_ref = bf16[800,1600]{1,0:T(8,128)(2,1)} collective-permute-done((bf16[800,1600]{1,0:T(8,128)(2,1)}, bf16[800,1600]{1,0:T(8,128)(2,1)}, u32[]{:S(2)}, u32[]{:S(2)}) %collective-permute-start.11) | collective-permute-done | bytes 2560032 | tf_op jit(solution)/shard_map/ppermute | solution.py:245
  215.0 3.1 put_late.1
  218.7 2.1 all-gather
  221.5 2.1 all-gather.1
  224.4 2.1 all-gather.2
  227.2 2.1 all-gather.3
  229.9 2.1 all-gather.4
  232.8 2.1 all-gather.5
  235.4 2.1 all-gather.6
  238.3 2.1 all-gather.7
  241.3 2.1 all-gather.8
  244.2 2.1 all-gather.9
  246.9 2.1 all-gather.10
  249.7 2.1 all-gather.11
  252.4 2.1 all-gather.12
  255.2 2.1 all-gather.13
  258.1 2.1 all-gather.14
  260.9 2.1 all-gather.15
  263.6 2.1 all-gather.16
  266.4 2.1 all-gather.17
  269.1 2.1 all-gather.18
  271.9 2.1 all-gather.19
  274.8 2.1 all-gather.20
  277.7 2.1 all-gather.21
  280.3 2.1 all-gather.22
  283.2 2.1 all-gather.23
  285.9 2.1 all-gather.24
  288.7 2.1 all-gather.25
  291.6 2.1 all-gather.26
  295.1 182.3 %collective-permute-done.26 = bf16[32,3200]{1,0:T(8,128)(2,1)S(1)} collective-permute-done((bf16[32,3200]{1,0:T(8,128)(2,1)S(1)}, bf16[32,3200]{1,0:T(8,128)(2,1)S(1)}, u32[]{:S(2)}, u32[]{:S(2)}) %collective-permute-start.26) | collective-permute-done | bytes 204832 | tf_op jit(solution)/shard_map/ppermute | solution.py:268
  477.4 2.2 all-gather.27
  479.6 6.4 %quarter_layer.30 = bf16[32,3200]{1,0:T(8,128)(2,1)S(1)} custom-call(s32[1]{0:T(128)} %constant.61.clone.1.tick_ref, s32[2]{0:T(128)S(1)} %pad_add_fusion.state_ref, bf16[2,32,3200]{2,1,0:T(8,128)(2,1)S(1)} %bitcast.76, bf16[4,400,3200]{2,1,0:T(8,128)(2,1)S(1)} %get-tuple-element.22.up_ref, bf16[4,800,1600]{2,1,0:T(8,128)(2,1)S(1)} %get-tuple-element.23.down_ref), custom_call_target="tpu_custom_call" | custom-call | flops 655360000 | bytes 409600 | tf_op jit(solution)/shard_map/quarter_layer/pallas_call | solution.py:143
  486.0 2.1 all-gather.28
  489.5 5.1 collective-permute-done.27
  494.6 2.1 all-gather.29
  497.3 2.2 all-gather.30
  499.6 3.9 collective-permute-start.28
  503.5 4.1 collective-permute-done.28
  511.1 33.3 %collective-permute-done.32 = bf16[16,3200]{1,0:T(8,128)(2,1)S(1)} collective-permute-done((bf16[16,3200]{1,0:T(8,128)(2,1)S(1)}, bf16[16,3200]{1,0:T(8,128)(2,1)S(1)}, u32[]{:S(2)}, u32[]{:S(2)}) %collective-permute-start.32) | collective-permute-done | bytes 102432 | tf_op jit(solution)/shard_map/ppermute | solution.py:281
  (106 shorter events, 36.7 us)
Async XLA Ops:
  6.5 1.3 copy-start
  9.9 46.0 %collective-permute-start = (bf16[2,200,1600]{2,1,0:T(8,128)(2,1)}, bf16[2,200,1600]{2,1,0:T(8,128)(2,1)}, u32[]{:S(2)}, u32[]{:S(2)}) collective-permute-start(bf16[2,200,1600]{2,1,0:T(8,128)(2,1)} %split_columns.1), channel_id=1, source_target_pairs={{0,4},{4,8},{8,12},{12,0},{1,5},{5,9},{9,13},{13,1},{2,6},{6,10},{... | collective-permute-start | bytes 3840008 | tf_op jit(solution)/shard_map/ppermute | solution.py:18
  13.4 44.9 %collective-permute-start.1 = (bf16[2,200,1600]{2,1,0:T(8,128)(2,1)}, bf16[2,200,1600]{2,1,0:T(8,128)(2,1)}, u32[]{:S(2)}, u32[]{:S(2)}) collective-permute-start(bf16[2,200,1600]{2,1,0:T(8,128)(2,1)} %split_columns.1), channel_id=1, source_target_pairs={{0,12},{4,0},{8,4},{12,8},{1,13},{5,1},{9,5},{13,9},{2,14},{6,2},{... | collective-permute-start | bytes 3840008 | tf_op jit(solution)/shard_map/ppermute | solution.py:18
  17.0 65.7 %collective-permute-start.4 = (bf16[200,3200]{1,0:T(8,128)(2,1)}, bf16[200,3200]{1,0:T(8,128)(2,1)}, u32[]{:S(2)}, u32[]{:S(2)}) collective-permute-start(bf16[200,3200]{1,0:T(8,128)(2,1)} %bitcast.95), channel_id=1, source_target_pairs={{0,1},{1,0},{2,3},{3,2},{4,5},{5,4},{6,7},{7,6},{8,9},{9,8},{10,11... | collective-permute-start | bytes 3840008 | tf_op jit(solution)/shard_map/ppermute | solution.py:228
  20.4 32.8 %all-to-all-start = ((bf16[16,16,200]{2,1,0:T(8,128)(2,1)}), bf16[16,16,200]{2,1,0:T(8,128)(2,1)S(1)}, u32[]{:S(2)}, u32[]{:S(2)}) async-start(bf16[16,16,200]{2,1,0:T(8,128)(2,1)} %bitcast.98), calls=%async_computation | async-start | bytes 262144 | tf_op jit(solution)/shard_map/all_to_all | solution.py:237
  26.0 136.8 %all-gather.33.cloned.1.call-start = ((), (), s32[]{:S(2)}) async-start(), calls=%async_computation.1 | async-start | bytes 1740800 | tf_op jit(solution)/shard_map/all_gather | solution.py:257
  27.4 1.5 copy-start.1
  53.5 10.5 %collective-permute-start.3 = (bf16[16,3200]{1,0:T(8,128)(2,1)S(1)}, bf16[16,3200]{1,0:T(8,128)(2,1)S(1)}, u32[]{:S(2)}, u32[]{:S(2)}) collective-permute-start(bf16[16,3200]{1,0:T(8,128)(2,1)S(1)} %all_to_all.17), channel_id=1, source_target_pairs={{0,3},{3,0},{1,2},{2,1},{4,7},{7,4},{5,6},{6,5},{8,11},{11,8},{9,1... | collective-permute-start | bytes 307208 | tf_op jit(solution)/shard_map/ppermute | solution.py:238
  58.3 24.4 %copy-start.3 = (bf16[1,200,3200]{2,1,0:T(8,128)(2,1)S(1)}, bf16[1,200,3200]{2,1,0:T(8,128)(2,1)}, u32[]{:S(2)}) copy-start(bf16[1,200,3200]{2,1,0:T(8,128)(2,1)} %param.5) | copy-start | bytes 3840004
  60.7 16.6 %collective-permute-start.2 = (bf16[200,1600]{1,0:T(8,128)(2,1)S(1)}, bf16[200,1600]{1,0:T(8,128)(2,1)S(1)}, u32[]{:S(2)}, u32[]{:S(2)}) collective-permute-start(bf16[200,1600]{1,0:T(8,128)(2,1)S(1)} %get-tuple-element.28), channel_id=1, source_target_pairs={{0,12},{4,0},{8,4},{12,8},{1,13},{5,1},{9,5},{13,9},{2,14},{6,2},{... | collective-permute-start | bytes 1920008 | tf_op jit(solution)/shard_map/ppermute | solution.py:18
  64.0 21.9 %collective-permute-start.5 = (bf16[200,1600]{1,0:T(8,128)(2,1)S(1)}, bf16[200,1600]{1,0:T(8,128)(2,1)S(1)}, u32[]{:S(2)}, u32[]{:S(2)}) collective-permute-start(bf16[200,1600]{1,0:T(8,128)(2,1)S(1)} %get-tuple-element.31), channel_id=1, source_target_pairs={{0,4},{4,8},{8,12},{12,0},{1,5},{5,9},{9,13},{13,1},{2,6},{6,10},{... | collective-permute-start | bytes 1920008 | tf_op jit(solution)/shard_map/ppermute | solution.py:18
  78.2 63.2 %collective-permute-start.10 = (bf16[800,1600]{1,0:T(8,128)(2,1)}, bf16[800,1600]{1,0:T(8,128)(2,1)}, u32[]{:S(2)}, u32[]{:S(2)}) collective-permute-start(bf16[800,1600]{1,0:T(8,128)(2,1)} %bitcast.94), channel_id=1, source_target_pairs={{0,3},{3,0},{1,2},{2,1},{4,7},{7,4},{5,6},{6,5},{8,11},{11,8},{9,1... | collective-permute-start | bytes 7680008 | tf_op jit(solution)/shard_map/ppermute | solution.py:243
  85.9 65.2 %collective-permute-start.8 = (bf16[400,3200]{1,0:T(8,128)(2,1)}, bf16[400,3200]{1,0:T(8,128)(2,1)}, u32[]{:S(2)}, u32[]{:S(2)}) collective-permute-start(bf16[400,3200]{1,0:T(8,128)(2,1)} %pad_maximum_fusion.refs_0_), channel_id=1, source_target_pairs={{0,12},{4,0},{8,4},{12,8},{1,13},{5,1},{9,5},{13,9},{2,14},{6,2},{... | collective-permute-start | bytes 7680008 | tf_op jit(solution)/shard_map/ppermute | solution.py:18
  89.9 68.3 %collective-permute-start.6 = (bf16[400,3200]{1,0:T(8,128)(2,1)}, bf16[400,3200]{1,0:T(8,128)(2,1)}, u32[]{:S(2)}, u32[]{:S(2)}) collective-permute-start(bf16[400,3200]{1,0:T(8,128)(2,1)} %pad_maximum_fusion.refs_0_), channel_id=1, source_target_pairs={{0,4},{4,8},{8,12},{12,0},{1,5},{5,9},{9,13},{13,1},{2,6},{6,10},{... | collective-permute-start | bytes 7680008 | tf_op jit(solution)/shard_map/ppermute | solution.py:18
  91.9 70.9 %collective-permute-start.12 = (bf16[800,1600]{1,0:T(8,128)(2,1)S(1)}, bf16[800,1600]{1,0:T(8,128)(2,1)}, u32[]{:S(2)}, u32[]{:S(2)}) collective-permute-start(bf16[800,1600]{1,0:T(8,128)(2,1)S(1)} %bitcast.60), channel_id=1, source_target_pairs={{0,1},{1,0},{2,3},{3,2},{4,5},{5,4},{6,7},{7,6},{8,9},{9,8},{10,11... | collective-permute-start | bytes 7680008 | tf_op jit(solution)/shard_map/ppermute | solution.py:244
  141.4 73.6 %collective-permute-start.11 = (bf16[800,1600]{1,0:T(8,128)(2,1)}, bf16[800,1600]{1,0:T(8,128)(2,1)}, u32[]{:S(2)}, u32[]{:S(2)}) collective-permute-start(bf16[800,1600]{1,0:T(8,128)(2,1)} %collective-permute-done.10.refs_5_), channel_id=1, source_target_pairs={{0,1},{1,0},{2,3},{3,2},{4,5},{5,4},{6,7},{7,6},{8,9},{9,8},{10,11... | collective-permute-start | bytes 7680008 | tf_op jit(solution)/shard_map/ppermute | solution.py:245
  153.6 29.9 %collective-permute-start.9 = (bf16[400,1664]{1,0:T(8,128)(2,1)}, bf16[400,1664]{1,0:T(8,128)(2,1)}, u32[]{:S(2)}, u32[]{:S(2)}) collective-permute-start(bf16[400,1664]{1,0:T(8,128)(2,1)} %slice.49), channel_id=1, source_target_pairs={{0,12},{4,0},{8,4},{12,8},{1,13},{5,1},{9,5},{13,9},{2,14},{6,2},{... | collective-permute-start | bytes 3993608 | tf_op jit(solution)/shard_map/ppermute | solution.py:18
  160.6 23.0 %collective-permute-start.7 = (bf16[400,1536]{1,0:T(8,128)(2,1)}, bf16[400,1536]{1,0:T(8,128)(2,1)}, u32[]{:S(2)}, u32[]{:S(2)}) collective-permute-start(bf16[400,1536]{1,0:T(8,128)(2,1)} %slice.48), channel_id=1, source_target_pairs={{0,4},{4,8},{8,12},{12,0},{1,5},{5,9},{9,13},{13,1},{2,6},{6,10},{... | collective-permute-start | bytes 3686408 | tf_op jit(solution)/shard_map/ppermute | solution.py:18
  220.8 0.7 collective-permute-start.13
  226.5 0.7 collective-permute-start.14
  232.1 0.7 collective-permute-start.15
  237.6 0.7 collective-permute-start.16
  243.5 0.7 collective-permute-start.17
  249.0 0.7 collective-permute-start.18
  254.5 0.7 collective-permute-start.19
  260.2 0.7 collective-permute-start.20
  265.7 0.7 collective-permute-start.21
  271.3 0.7 collective-permute-start.22
  277.0 0.7 collective-permute-start.23
  282.5 0.7 collective-permute-start.24
  288.0 0.7 collective-permute-start.25
  293.8 183.6 %collective-permute-start.26 = (bf16[32,3200]{1,0:T(8,128)(2,1)S(1)}, bf16[32,3200]{1,0:T(8,128)(2,1)S(1)}, u32[]{:S(2)}, u32[]{:S(2)}) collective-permute-start(bf16[32,3200]{1,0:T(8,128)(2,1)S(1)} %add_pair.29), channel_id=1, source_target_pairs={{416,448},{432,451},{419,464},{435,467},{417,449},{433,450},{418,4... | collective-permute-start | bytes 614408 | tf_op jit(solution)/shard_map/ppermute | solution.py:268
  488.1 6.4 %collective-permute-start.27 = (bf16[32,3200]{1,0:T(8,128)(2,1)S(1)}, bf16[32,3200]{1,0:T(8,128)(2,1)S(1)}, u32[]{:S(2)}, u32[]{:S(2)}) collective-permute-start(bf16[32,3200]{1,0:T(8,128)(2,1)S(1)} %add_pair.30), channel_id=1, source_target_pairs={{448,480},{464,483},{451,496},{467,499},{449,481},{465,482},{450,4... | collective-permute-start | bytes 614408 | tf_op jit(solution)/shard_map/ppermute | solution.py:268
  497.2 47.2 %copy-start.2 = (bf16[3200,256]{1,0:T(8,128)(2,1)S(1)}, bf16[3200,256]{1,0:T(8,128)(2,1)}, u32[]{:S(2)}) copy-start(bf16[3200,256]{1,0:T(8,128)(2,1)} %all-gather.33.cloned.1.call-done) | copy-start | bytes 4915204
  499.6 8.0 %collective-permute-start.28 = (bf16[16,3200]{1,0:T(8,128)(2,1)S(1)}, bf16[16,3200]{1,0:T(8,128)(2,1)S(1)}, u32[]{:S(2)}, u32[]{:S(2)}) collective-permute-start(bf16[16,3200]{1,0:T(8,128)(2,1)S(1)} %broadcast_select_fusion.2), channel_id=1, source_target_pairs={{0,3},{3,0},{1,2},{2,1},{4,7},{7,4},{5,6},{6,5},{8,11},{11,8},{9,1... | collective-permute-start | bytes 307208 | tf_op jit(solution)/shard_map/ppermute | solution.py:274
  507.6 0.7 collective-permute-start.29
  508.4 0.7 collective-permute-start.30
  509.1 0.7 collective-permute-start.31
  509.8 34.6 %collective-permute-start.32 = (bf16[16,3200]{1,0:T(8,128)(2,1)S(1)}, bf16[16,3200]{1,0:T(8,128)(2,1)S(1)}, u32[]{:S(2)}, u32[]{:S(2)}) collective-permute-start(bf16[16,3200]{1,0:T(8,128)(2,1)S(1)} %add.62), channel_id=1, source_target_pairs={{480,0},{224,256},{96,128},{352,384},{32,64},{288,320},{160,192},{... | collective-permute-start | bytes 307208 | tf_op jit(solution)/shard_map/ppermute | solution.py:281
Sparse Core Ops, SparseCore 0:
  91.9 61.0 all-gather.32

commit v5 on v4

v5 whole, which is shorter than its diff:
```python
import functools

import jax
import jax.numpy as jnp
from jax import lax
from jax.experimental import pallas as pl
from jax.experimental.pallas import tpu as pltpu
from jax.sharding import Mesh, PartitionSpec as P

SIDE = 4
OFFSETS = (0, 3, 1, 2)
INTRA = [(0, 1), (1, 0), (2, 3), (3, 2)]
INTER = [(0, 3), (3, 0), (1, 2), (2, 1)]


def moved(block, axis, by):
    route = [(i, (i + by) % SIDE) for i in range(SIDE)]
    return lax.ppermute(block, axis, route)


def ring(first, second, axis):
    first_below = moved(first, axis, 1)
    second_above = moved(second, axis, -1)
    second_below = moved(second, axis, 1)
    first_above = moved(first, axis, -1)
    first_far = moved(first_below, axis, 1)
    second_far = moved(second_above, axis, -1)
    return (first_below, first_above, first_far), (second_below, second_above, second_far)


def run_all(copies):
    for copy in copies:
        copy.start()
    for copy in copies:
        copy.wait()


def put(plan, spots_ref, *refs):
    sources, targets, sems = refs[: len(plan)], refs[-5:-1], refs[-1]
    run_all(
        [
            pltpu.make_async_copy(source, targets[to].at[spots_ref[spot]], sems.at[i])
            for i, (source, (to, spot)) in enumerate(zip(sources, plan))
        ]
    )


def put_pieces(spots, plan, pieces, targets, shapes):
    anywhere = pl.BlockSpec(memory_space=pl.ANY)
    count = len(pieces)
    return pl.pallas_call(
        functools.partial(put, plan),
        out_shape=tuple(jax.ShapeDtypeStruct(s, pieces[0].dtype) for s in shapes),
        in_specs=[pl.BlockSpec(memory_space=pltpu.SMEM)]
        + [anywhere] * (count + len(targets)),
        out_specs=(anywhere,) * 4,
        scratch_shapes=[pltpu.SemaphoreType.DMA((count,))],
        input_output_aliases={1 + count + i: i for i in range(len(targets))},
        compiler_params=pltpu.CompilerParams(vmem_limit_bytes=2**20),
        name="put_pieces",
    )(spots, *pieces, *targets)


def product(left, right):
    return lax.dot_general(
        left, right, (((1,), (1,)), ((), ())), preferred_element_type=jnp.float32
    )


def quarter_layer(tick_ref, state_ref, pair_ref, *refs):
    left_ref, right_ref, own_ref, rest_ref, out_ref, hidden_ref, total_ref = refs
    step, cut = left_ref.shape[1:]
    block = own_ref.shape[1]
    active = tick_ref[0] == state_ref[0]

    @pl.when(jnp.logical_not(active))
    def _():
        out_ref[...] = jnp.zeros_like(out_ref)

    @pl.when(active)
    def _():
        rows = pair_ref[0].astype(jnp.float32) + pair_ref[1].astype(jnp.float32)
        scale = lax.rsqrt(jnp.mean(rows * rows, axis=1, keepdims=True) + 1e-06)
        normed = (rows * scale).astype(jnp.bfloat16)
        for i in range(SIDE):
            part = product(normed[:, :cut], left_ref[i])
            part = part + product(normed[:, cut:], right_ref[i])
            part = jax.nn.gelu(part).astype(jnp.bfloat16)
            hidden_ref[:, i * step : (i + 1) * step] = part
        hidden = hidden_ref[...]
        places = [lax.rem(state_ref[2] + offset, SIDE) for offset in OFFSETS]
        for i in range(SIDE):
            total_ref[i, places[0]] = product(hidden, own_ref[i])
            part = product(hidden, rest_ref[i])
            for j in range(SIDE - 1):
                total_ref[i, places[1 + j]] = part[:, j * block : (j + 1) * block]
        pieces = [total_ref[j, i] for i in range(SIDE) for j in range(SIDE)]
        total = jnp.concatenate(pieces, axis=1)
        base = jnp.where(state_ref[1] == 1, rows, 0.0)
        out_ref[...] = (base + total).astype(jnp.bfloat16)


def apply_quarter(tick, state, pair, weights):
    _, row_count, width = pair.shape
    units, block = weights[2].shape[2], weights[2].shape[1]
    resident = pl.BlockSpec(memory_space=pltpu.VMEM)
    scalar = pl.BlockSpec(memory_space=pltpu.SMEM)
    return pl.pallas_call(
        quarter_layer,
        out_shape=jax.ShapeDtypeStruct((row_count, width), jnp.bfloat16),
        in_specs=[scalar] * 2 + [resident] * 5,
        out_specs=resident,
        scratch_shapes=[
            pltpu.VMEM((row_count, units), jnp.bfloat16),
            pltpu.VMEM((SIDE, SIDE, row_count, block), jnp.float32),
        ],
        compiler_params=pltpu.CompilerParams(vmem_limit_bytes=10 * 2**20),
        cost_estimate=pl.CostEstimate(
            flops=4 * row_count * width * units,
            bytes_accessed=4 * row_count * width,
            transcendentals=row_count * units,
        ),
        name="quarter_layer",
    )(tick, state, pair, *weights)


def add_pair(pair_ref, out_ref):
    total = pair_ref[0].astype(jnp.float32) + pair_ref[1].astype(jnp.float32)
    out_ref[...] = total.astype(out_ref.dtype)


def added(pair):
    resident = pl.BlockSpec(memory_space=pltpu.VMEM)
    return pl.pallas_call(
        add_pair,
        out_shape=jax.ShapeDtypeStruct(pair.shape[1:], pair.dtype),
        in_specs=[resident],
        out_specs=resident,
        compiler_params=pltpu.CompilerParams(vmem_limit_bytes=2 * 2**20),
        cost_estimate=pl.CostEstimate(
            flops=pair.size, bytes_accessed=pair.size, transcendentals=0
        ),
        name="add_pair",
    )(pair)


def split_columns(low_ref, block_ref, own_ref, other_ref):
    width = block_ref.shape[1] // SIDE // 2
    low = low_ref[0] == 1
    for i in range(SIDE):
        left = block_ref[:, 2 * i * width : (2 * i + 1) * width]
        right = block_ref[:, (2 * i + 1) * width : (2 * i + 2) * width]
        own_ref[:, i * width : (i + 1) * width] = jnp.where(low, left, right)
        other_ref[:, i * width : (i + 1) * width] = jnp.where(low, right, left)


def own_and_other(low, block):
    rows, width = block.shape
    resident = pl.BlockSpec(memory_space=pltpu.VMEM)
    half = jax.ShapeDtypeStruct((rows, width // 2), block.dtype)
    return pl.pallas_call(
        split_columns,
        out_shape=(half, half),
        in_specs=[pl.BlockSpec(memory_space=pltpu.SMEM), resident],
        out_specs=(resident, resident),
        compiler_params=pltpu.CompilerParams(vmem_limit_bytes=10 * 2**20),
        name="split_columns",
    )(low.reshape(1), block)


def by_halves(low, block, other):
    first = jnp.where(low == 1, block, other)
    second = jnp.where(low == 1, other, block)
    return jnp.concatenate([first, second], axis=0)


def next_plane(layer):
    route = []
    for x, across in INTER:
        for core in range(2):
            to_chip = (x if x < 2 else across) if core == 0 else (x if x >= 2 else across)
            to_core = 0 if x < 2 else 1
            source = (layer * 2 + core) * SIDE + x
            route.append((source, ((layer + 1) * 2 + to_core) * SIDE + to_chip))
    return route


def on_device(layers, patches, w_in, w_out, w_proj):
    plane, core = lax.axis_index("z"), lax.axis_index("c")
    y, x = lax.axis_index("y"), lax.axis_index("x")
    tp = ("y", "x")
    low = (x < 2).astype(jnp.int32)

    own, other = own_and_other(low, w_out[0])
    mate = lax.ppermute(w_in[0], "x", INTRA)
    own_ring, other_ring = ring(own, other, "y")
    beside = lax.ppermute(own, "x", INTRA)
    across = lax.ppermute(other, "x", INTER)
    corner = lax.ppermute(across, "x", INTRA)
    held = (own_ring, other_ring, beside, across, corner)
    own_ring, other_ring, beside, across, corner = lax.optimization_barrier(held)
    own_rest = jnp.concatenate(own_ring, axis=0)
    other_rest = jnp.concatenate(other_ring, axis=0)

    even = (lax.rem(x, 2) == 0).astype(jnp.int32)
    cut = w_in.shape[2] // 256 * 128
    left = by_halves(even, w_in[0, :, :cut], mate[:, :cut])
    right = by_halves(even, w_in[0, :, cut:], mate[:, cut:])
    held = (left, right, own_rest, other_rest)
    left, right, own_rest, other_rest = lax.optimization_barrier(held)
    beside_rest = lax.ppermute(own_rest, "x", INTRA)
    across_rest = lax.ppermute(other_rest, "x", INTER)
    left_ring, right_ring = ring(left, right, "y")
    across_rest, patches = lax.optimization_barrier((across_rest, patches))
    corner_rest = lax.ppermute(across_rest, "x", INTRA)

    flat = patches.reshape(-1, patches.shape[2])
    rows = lax.all_to_all(flat, tp, split_axis=0, concat_axis=1, tiled=True)
    rows = by_halves(low, rows, lax.ppermute(rows, "x", INTER))

    mate_x = x + 1 - 2 * lax.rem(x, 2)
    spots = [lax.rem(y + offset, SIDE) for offset in OFFSETS]
    spots += [x, mate_x, SIDE - 1 - x, SIDE - 1 - mate_x]
    spots = jnp.stack(spots).astype(jnp.int32)
    projection = lax.all_gather(w_proj, tp, axis=0, tiled=True)
    adds = jnp.logical_and(core == 0, low == 1)
    state = jnp.stack([plane, adds, y]).astype(jnp.int32)
    pair = jnp.stack([rows, jnp.zeros_like(rows)])
    held = (spots, pair, state, projection)
    spots, pair, state, projection = lax.optimization_barrier(held)
    early = [(left, 0, 0), (left_ring[0], 0, 1), (left_ring[1], 0, 2)]
    early += [(right, 1, 0), (right_ring[0], 1, 1), (right_ring[1], 1, 2)]
    early += [(own, 2, 4), (beside, 2, 5), (across, 2, 6), (corner, 2, 7)]
    early += [(own_rest, 3, 4), (beside_rest, 3, 5), (across_rest, 3, 6)]
    late = [(left_ring[2], 0, 3), (right_ring[2], 1, 3), (corner_rest, 3, 7)]
    shapes = [(SIDE,) + piece.shape for piece in (left, right, own, own_rest)]
    weights = ()
    for group in (early, late):
        plan = tuple((to, spot) for _, to, spot in group)
        pieces = [piece for piece, _, _ in group]
        weights = put_pieces(spots, plan, pieces, weights, shapes)
    weights = [pltpu.with_memory_space_constraint(w, pltpu.VMEM) for w in weights]
    for layer in range(layers):
        tick = jnp.full((1,), layer, jnp.int32)
        part = apply_quarter(tick, state, pair, weights)
        part = added(lax.all_gather(part, "c", axis=0, tiled=False))
        if layer < layers - 1:
            part = lax.ppermute(part, ("z", "c", "x"), next_plane(layer))
            pair = lax.all_gather(part, "c", axis=0, tiled=False)

    count = part.shape[0] // 2
    kept = jnp.where(low == 1, part[:count], part[count:])
    sent = jnp.where(low == 1, part[count:], part[:count])
    last = (layers - 1) * SIDE
    route = [(last + here, last + there) for here, there in INTER]
    got = lax.ppermute(sent, ("z", "x"), route)
    total = kept.astype(jnp.float32) + got.astype(jnp.float32)
    rows = jnp.where(plane == layers - 1, total, 0.0).astype(jnp.bfloat16)
    holders = [layers - 1]
    step = layers // 2
    while step:
        route = [(held, (held + step) % layers) for held in holders]
        rows = rows + lax.ppermute(rows, "z", route)
        holders += [target for _, target in route]
        step //= 2
    return jnp.dot(rows, projection, preferred_element_type=jnp.float32).astype(
        jnp.bfloat16
    )


def solution(mesh):
    sections = mesh.shape["section"]
    grid = Mesh(
        mesh.devices.reshape(sections // 2, 2, SIDE, SIDE), ("z", "c", "y", "x")
    )
    section, tp = ("z", "c"), ("y", "x")
    return jax.shard_map(
        functools.partial(on_device, sections // 2),
        mesh=grid,
        in_specs=(
            P(None, None, tp),
            P(section, tp, None),
            P(section, tp, None),
            P(tp, section),
        ),
        out_specs=P(tp, section),
        check_vma=False,
    )
```

time: 560 us -> 613 us (1.095)
  waiting for transfers between devices: 361 us -> 398 us
  starting transfers between devices: 63.4 us -> 81.7 us
    ppermute x1, waiting for transfers between devices: 47.6 us -> 3.63 us  [on_device(): across = lax.ppermute(other, 'x', INTER)]
    all_to_all x1, waiting for transfers between devices: 22.9 us -> 56.6 us  [on_device(): rows = lax.all_to_all(flat, tp, split_axis=0, concat_axis=1, tiled=True)]
    ppermute x2 -> x5, waiting for transfers between devices: 4.18 us -> 33.5 us  [the longest x1 33.5 us: on_device(): across_rest = lax.ppermute(other_rest, 'x', INTER)]
    ppermute x8 -> x12, starting transfers between devices: 25.1 us -> 41.1 us  [moved(): return lax.ppermute(block, axis, route)]
    ppermute x8 -> x12, waiting for transfers between devices: 33.8 us -> 43.1 us  [moved(): return lax.ppermute(block, axis, route)]
    ppermute x4, waiting for transfers between devices: 33.3 us -> 41.4 us  [on_device(): rows = rows + lax.ppermute(rows, 'z', route)]
    dynamic_update_slice x6 -> x0, local copies, waits for them, and re-layouts: 8.04 us -> none  [in_order(): whole = lax.dynamic_update_slice(whole, part[None], (at, 0, 0))]
  transfers between devices with their start and end apart: 35 -> 42, of which waited for: 11 -> 12; matrix products, arithmetic and copies ran while one was open for 3% -> 0% of each run, Pallas kernels for 1% -> 1%
where the time goes in v5:
time: 613 us; the launch traced here: 605 us
  waiting for transfers between devices  398 us (65%)
  starting transfers between devices  81.7 us (13%)
  blocking collectives  65.2 us (11%)
  Pallas kernels  26.1 us (4%)
  between operations  14.7 us (2%)
  local copies, waits for them, and re-layouts  11.1 us (2%)
  other arithmetic  7.68 us (1%)
    ppermute x15, waiting for transfers between devices, on_device(): part = lax.ppermute(part, ('z', 'c', 'x'), next_plane(layer))  193 us
    all_to_all x1, waiting for transfers between devices, on_device(): rows = lax.all_to_all(flat, tp, split_axis=0, concat_axis=1, tiled=True)  56.6 us
    ppermute x12, waiting for transfers between devices, moved(): return lax.ppermute(block, axis, route)  43.1 us
    ppermute x4, waiting for transfers between devices, on_device(): rows = rows + lax.ppermute(rows, 'z', route)  41.4 us
    ppermute x12, starting transfers between devices, moved(): return lax.ppermute(block, axis, route)  41.1 us
    all_gather x16, blocking collectives, on_device(): part = added(lax.all_gather(part, 'c', axis=0, tiled=False))  33.7 us
    ppermute x1, waiting for transfers between devices, on_device(): across_rest = lax.ppermute(other_rest, 'x', INTER)  33.5 us
    all_gather x15, blocking collectives, on_device(): pair = lax.all_gather(part, 'c', axis=0, tiled=False)  31.5 us
  transfers between devices with their start and end apart: 42, of which 12 were waited for; matrix products, arithmetic and copies ran while one was open for 0% of the time, Pallas kernels for 1%

profile of v5, /device:TPU:448, one launch (start us, length us, event | category | flops | bytes accessed | tf_op | source)
XLA Modules:
  0.0 604.9 jit_solution(4411052116874144676)
XLA Ops:
  8.8 4.7 collective-permute-start.8
  13.5 4.9 collective-permute-start.5
  18.4 1.9 collective-permute-start.4
  20.4 2.1 collective-permute-start.7
  22.5 2.5 collective-permute-start.1
  25.0 3.6 collective-permute-done.8.refs_8_
  28.6 2.2 collective-permute-start
  32.3 5.7 collective-permute-start.2
  39.5 2.1 collective-permute-start.9
  42.5 3.6 collective-permute-start.6
  46.1 5.9 collective-permute-done.1
  54.0 26.1 %collective-permute-done.9.refs_9_ = bf16[200,1600]{1,0:T(8,128)(2,1)S(1)} collective-permute-done((bf16[200,1600]{1,0:T(8,128)(2,1)S(1)}, bf16[200,1600]{1,0:T(8,128)(2,1)S(1)}, u32[]{:S(2)}, u32[]{:S(2)}) %collective-permute-start.9) | collective-permute-done | bytes 640032 | tf_op jit(solution)/shard_map/ppermute | solution.py:199
  82.9 3.7 pad_maximum_fusion
  86.6 2.4 collective-permute-start.10
  89.1 4.9 collective-permute-start.17
  93.9 1.9 collective-permute-start.14
  95.8 3.9 collective-permute-start.12
  99.8 2.2 collective-permute-start.19
  102.0 33.5 %collective-permute-done.10.refs_12_ = bf16[600,1600]{1,0:T(8,128)(2,1)} collective-permute-done((bf16[600,1600]{1,0:T(8,128)(2,1)}, bf16[600,1600]{1,0:T(8,128)(2,1)}, u32[]{:S(2)}, u32[]{:S(2)}) %collective-permute-start.10) | collective-permute-done | bytes 1920032 | tf_op jit(solution)/shard_map/ppermute | solution.py:212
  137.4 5.5 all-to-all-start
  143.0 56.6 %all-to-all-done = bf16[16,16,200]{2,1,0:T(8,128)(2,1)S(1)} async-done(((bf16[16,16,200]{2,1,0:T(8,128)(2,1)}), bf16[16,16,200]{2,1,0:T(8,128)(2,1)S(1)}, u32[]{:S(2)}, u32[]{:S(2)}) %all-to-all-start) | async-done | bytes 102432 | tf_op jit(solution)/shard_map/all_to_all | solution.py:218
  202.0 2.2 collective-permute-start.11
  204.3 2.8 collective-permute-start.18
  207.2 3.0 collective-permute-start.13
  210.2 4.0 collective-permute-start.15
  216.0 23.7 %collective-permute-done.18.refs_4_ = bf16[400,1664]{1,0:T(8,128)(2,1)} collective-permute-done((bf16[400,1664]{1,0:T(8,128)(2,1)S(1)}, bf16[400,1664]{1,0:T(8,128)(2,1)}, u32[]{:S(2)}, u32[]{:S(2)}) %collective-permute-start.18) | collective-permute-done | bytes 1331232 | tf_op jit(solution)/shard_map/ppermute | solution.py:18
  245.3 4.9 put_pieces.2
  250.2 10.4 %collective-permute-done.13.refs_0_ = bf16[400,1536]{1,0:T(8,128)(2,1)} collective-permute-done((bf16[400,1536]{1,0:T(8,128)(2,1)}, bf16[400,1536]{1,0:T(8,128)(2,1)}, u32[]{:S(2)}, u32[]{:S(2)}) %collective-permute-start.13) | collective-permute-done | bytes 1228832 | tf_op jit(solution)/shard_map/ppermute | solution.py:18
  260.7 2.9 put_pieces.3
  264.2 2.1 all-gather
  267.0 2.1 all-gather.1
  269.9 2.1 all-gather.2
  272.8 2.1 all-gather.3
  275.4 2.1 all-gather.4
  278.3 2.1 all-gather.5
  280.9 2.1 all-gather.6
  283.8 2.1 all-gather.7
  286.9 2.1 all-gather.8
  289.7 2.1 all-gather.9
  292.4 2.1 all-gather.10
  295.2 2.1 all-gather.11
  297.9 2.1 all-gather.12
  300.7 2.1 all-gather.13
  303.6 2.1 all-gather.14
  306.4 2.1 all-gather.15
  309.1 2.1 all-gather.16
  311.9 2.1 all-gather.17
  314.6 2.1 all-gather.18
  317.5 2.1 all-gather.19
  320.3 2.1 all-gather.20
  323.2 2.1 all-gather.21
  325.9 2.1 all-gather.22
  328.7 2.1 all-gather.23
  331.4 2.1 all-gather.24
  334.2 2.1 all-gather.25
  337.1 2.1 all-gather.26
  340.6 188.4 %collective-permute-done.33 = bf16[32,3200]{1,0:T(8,128)(2,1)S(1)} collective-permute-done((bf16[32,3200]{1,0:T(8,128)(2,1)S(1)}, bf16[32,3200]{1,0:T(8,128)(2,1)S(1)}, u32[]{:S(2)}, u32[]{:S(2)}) %collective-permute-start.33) | collective-permute-done | bytes 204832 | tf_op jit(solution)/shard_map/ppermute | solution.py:248
  529.0 2.1 all-gather.27
  531.0 6.8 %quarter_layer.30 = bf16[32,3200]{1,0:T(8,128)(2,1)S(1)} custom-call(s32[1]{0:T(128)} %constant.59.clone.1.tick_ref, s32[3]{0:T(128)S(1)} %pad_add_fusion.state_ref, bf16[2,32,3200]{2,1,0:T(8,128)(2,1)S(1)} %bitcast.70, bf16[4,400,1536]{2,1,0:T(8,128)(2,1)S(1)} %get-tuple-element.58.refs_0_, bf16[4,400,1664]{2,1,0:T(8,128)(2,1)S(1)} %get-tuple-element.59.refs_1_, ...), custom_call_target="tpu_custom_call" | custom-call | flops 655360000 | bytes 409600 | tf_op jit(solution)/shard_map/quarter_layer/pallas_call | solution.py:108
  537.8 2.1 all-gather.28
  541.3 4.9 collective-permute-done.34
  546.2 2.1 all-gather.29
  548.8 2.2 all-gather.30
  555.3 41.4 %collective-permute-done.39 = bf16[16,3200]{1,0:T(8,128)(2,1)S(1)} collective-permute-done((bf16[16,3200]{1,0:T(8,128)(2,1)S(1)}, bf16[16,3200]{1,0:T(8,128)(2,1)S(1)}, u32[]{:S(2)}, u32[]{:S(2)}) %collective-permute-start.39) | collective-permute-done | bytes 102432 | tf_op jit(solution)/shard_map/ppermute | solution.py:263
  (133 shorter events, 49.8 us)
Async XLA Ops:
  6.5 209.4 %all-gather.33.cloned.1.call-start = ((), (), s32[]{:S(2)}) async-start(), calls=%async_computation.1 | async-start | bytes 1740800 | tf_op jit(solution)/shard_map/all_gather | solution.py:225
  6.5 1.3 copy-start.2
  8.8 73.9 %copy-start.3 = (bf16[200,1600]{1,0:T(8,128)(2,1)}, bf16[200,1600]{1,0:T(8,128)(2,1)S(1)}, u32[]{:S(2)}) copy-start(bf16[200,1600]{1,0:T(8,128)(2,1)S(1)} %get-tuple-element.34.refs_6_) | copy-start | bytes 1920004
  8.8 19.8 %collective-permute-start.8 = (bf16[200,1600]{1,0:T(8,128)(2,1)S(1)}, bf16[200,1600]{1,0:T(8,128)(2,1)S(1)}, u32[]{:S(2)}, u32[]{:S(2)}) collective-permute-start(bf16[200,1600]{1,0:T(8,128)(2,1)S(1)} %get-tuple-element.35), channel_id=1, source_target_pairs={{0,3},{3,0},{1,2},{2,1},{4,7},{7,4},{5,6},{6,5},{8,11},{11,8},{9,1... | collective-permute-start | bytes 1920008 | tf_op jit(solution)/shard_map/ppermute | solution.py:198
  13.5 18.8 %collective-permute-start.5 = (bf16[200,1600]{1,0:T(8,128)(2,1)S(1)}, bf16[200,1600]{1,0:T(8,128)(2,1)}, u32[]{:S(2)}, u32[]{:S(2)}) collective-permute-start(bf16[200,1600]{1,0:T(8,128)(2,1)S(1)} %get-tuple-element.35), channel_id=1, source_target_pairs={{0,12},{4,0},{8,4},{12,8},{1,13},{5,1},{9,5},{13,9},{2,14},{6,2},{... | collective-permute-start | bytes 1920008 | tf_op jit(solution)/shard_map/ppermute | solution.py:18
  18.4 21.1 %collective-permute-start.4 = (bf16[200,1600]{1,0:T(8,128)(2,1)S(1)}, bf16[200,1600]{1,0:T(8,128)(2,1)}, u32[]{:S(2)}, u32[]{:S(2)}) collective-permute-start(bf16[200,1600]{1,0:T(8,128)(2,1)S(1)} %get-tuple-element.35), channel_id=1, source_target_pairs={{0,4},{4,8},{8,12},{12,0},{1,5},{5,9},{9,13},{13,1},{2,6},{6,10},{... | collective-permute-start | bytes 1920008 | tf_op jit(solution)/shard_map/ppermute | solution.py:18
  20.4 21.3 %collective-permute-start.7 = (bf16[200,1600]{1,0:T(8,128)(2,1)S(1)}, bf16[200,1600]{1,0:T(8,128)(2,1)S(1)}, u32[]{:S(2)}, u32[]{:S(2)}) collective-permute-start(bf16[200,1600]{1,0:T(8,128)(2,1)S(1)} %get-tuple-element.34.refs_6_), channel_id=1, source_target_pairs={{0,1},{1,0},{2,3},{3,2},{4,5},{5,4},{6,7},{7,6},{8,9},{9,8},{10,11... | collective-permute-start | bytes 1920008 | tf_op jit(solution)/shard_map/ppermute | solution.py:197
  22.5 29.5 %collective-permute-start.1 = (bf16[200,1600]{1,0:T(8,128)(2,1)S(1)}, bf16[200,1600]{1,0:T(8,128)(2,1)}, u32[]{:S(2)}, u32[]{:S(2)}) collective-permute-start(bf16[200,1600]{1,0:T(8,128)(2,1)S(1)} %get-tuple-element.34.refs_6_), channel_id=1, source_target_pairs={{0,4},{4,8},{8,12},{12,0},{1,5},{5,9},{9,13},{13,1},{2,6},{6,10},{... | collective-permute-start | bytes 1920008 | tf_op jit(solution)/shard_map/ppermute | solution.py:18
  28.6 54.1 %copy-start.5 = (bf16[200,1600]{1,0:T(8,128)(2,1)}, bf16[200,1600]{1,0:T(8,128)(2,1)S(1)}, u32[]{:S(2)}) copy-start(bf16[200,1600]{1,0:T(8,128)(2,1)S(1)} %collective-permute-done.8.refs_8_) | copy-start | bytes 1920004
  28.6 51.5 %collective-permute-start = (bf16[200,3200]{1,0:T(8,128)(2,1)}, bf16[200,3200]{1,0:T(8,128)(2,1)S(1)}, u32[]{:S(2)}, u32[]{:S(2)}) collective-permute-start(bf16[200,3200]{1,0:T(8,128)(2,1)} %bitcast.88), channel_id=1, source_target_pairs={{0,1},{1,0},{2,3},{3,2},{4,5},{5,4},{6,7},{7,6},{8,9},{9,8},{10,11... | collective-permute-start | bytes 3840008 | tf_op jit(solution)/shard_map/ppermute | solution.py:195
  32.3 21.6 %collective-permute-start.2 = (bf16[200,1600]{1,0:T(8,128)(2,1)S(1)}, bf16[200,1600]{1,0:T(8,128)(2,1)}, u32[]{:S(2)}, u32[]{:S(2)}) collective-permute-start(bf16[200,1600]{1,0:T(8,128)(2,1)S(1)} %get-tuple-element.34.refs_6_), channel_id=1, source_target_pairs={{0,12},{4,0},{8,4},{12,8},{1,13},{5,1},{9,5},{13,9},{2,14},{6,2},{... | collective-permute-start | bytes 1920008 | tf_op jit(solution)/shard_map/ppermute | solution.py:18
  39.5 40.5 %collective-permute-start.9 = (bf16[200,1600]{1,0:T(8,128)(2,1)S(1)}, bf16[200,1600]{1,0:T(8,128)(2,1)S(1)}, u32[]{:S(2)}, u32[]{:S(2)}) collective-permute-start(bf16[200,1600]{1,0:T(8,128)(2,1)S(1)} %collective-permute-done.8.refs_8_), channel_id=1, source_target_pairs={{0,1},{1,0},{2,3},{3,2},{4,5},{5,4},{6,7},{7,6},{8,9},{9,8},{10,11... | collective-permute-start | bytes 1920008 | tf_op jit(solution)/shard_map/ppermute | solution.py:199
  41.7 0.9 copy-start.7
  42.5 37.6 %collective-permute-start.6 = (bf16[200,1600]{1,0:T(8,128)(2,1)}, bf16[200,1600]{1,0:T(8,128)(2,1)}, u32[]{:S(2)}, u32[]{:S(2)}) collective-permute-start(bf16[200,1600]{1,0:T(8,128)(2,1)} %collective-permute-done.5), channel_id=1, source_target_pairs={{0,12},{4,0},{8,4},{12,8},{1,13},{5,1},{9,5},{13,9},{2,14},{6,2},{... | collective-permute-start | bytes 1920008 | tf_op jit(solution)/shard_map/ppermute | solution.py:18
  52.0 28.1 %collective-permute-start.3 = (bf16[200,1600]{1,0:T(8,128)(2,1)}, bf16[200,1600]{1,0:T(8,128)(2,1)}, u32[]{:S(2)}, u32[]{:S(2)}) collective-permute-start(bf16[200,1600]{1,0:T(8,128)(2,1)} %collective-permute-done.1), channel_id=1, source_target_pairs={{0,4},{4,8},{8,12},{12,0},{1,5},{5,9},{9,13},{13,1},{2,6},{6,10},{... | collective-permute-start | bytes 1920008 | tf_op jit(solution)/shard_map/ppermute | solution.py:18
  54.0 28.7 %copy-start.12 = (bf16[1,200,3200]{2,1,0:T(8,128)(2,1)S(1)}, bf16[1,200,3200]{2,1,0:T(8,128)(2,1)}, u32[]{:S(2)}) copy-start(bf16[1,200,3200]{2,1,0:T(8,128)(2,1)} %param.5) | copy-start | bytes 3840004
  80.1 2.6 copy-start.9
  86.6 48.8 %collective-permute-start.10 = (bf16[600,1600]{1,0:T(8,128)(2,1)}, bf16[600,1600]{1,0:T(8,128)(2,1)}, u32[]{:S(2)}, u32[]{:S(2)}) collective-permute-start(bf16[600,1600]{1,0:T(8,128)(2,1)} %get-tuple-element.42), channel_id=1, source_target_pairs={{0,3},{3,0},{1,2},{2,1},{4,7},{7,4},{5,6},{6,5},{8,11},{11,8},{9,1... | collective-permute-start | bytes 5760008 | tf_op jit(solution)/shard_map/ppermute | solution.py:212
  89.1 113.0 %collective-permute-start.17 = (bf16[400,1536]{1,0:T(8,128)(2,1)}, bf16[400,1536]{1,0:T(8,128)(2,1)}, u32[]{:S(2)}, u32[]{:S(2)}) collective-permute-start(bf16[400,1536]{1,0:T(8,128)(2,1)} %pad_maximum_fusion.3.refs_0_), channel_id=1, source_target_pairs={{0,12},{4,0},{8,4},{12,8},{1,13},{5,1},{9,5},{13,9},{2,14},{6,2},{... | collective-permute-start | bytes 3686408 | tf_op jit(solution)/shard_map/ppermute | solution.py:18
  93.9 113.2 %collective-permute-start.14 = (bf16[400,1664]{1,0:T(8,128)(2,1)S(1)}, bf16[400,1664]{1,0:T(8,128)(2,1)}, u32[]{:S(2)}, u32[]{:S(2)}) collective-permute-start(bf16[400,1664]{1,0:T(8,128)(2,1)S(1)} %pad_maximum_fusion.2.refs_3_), channel_id=1, source_target_pairs={{0,12},{4,0},{8,4},{12,8},{1,13},{5,1},{9,5},{13,9},{2,14},{6,2},{... | collective-permute-start | bytes 3993608 | tf_op jit(solution)/shard_map/ppermute | solution.py:18
  95.8 108.4 %collective-permute-start.12 = (bf16[400,1536]{1,0:T(8,128)(2,1)}, bf16[400,1536]{1,0:T(8,128)(2,1)}, u32[]{:S(2)}, u32[]{:S(2)}) collective-permute-start(bf16[400,1536]{1,0:T(8,128)(2,1)} %pad_maximum_fusion.3.refs_0_), channel_id=1, source_target_pairs={{0,4},{4,8},{8,12},{12,0},{1,5},{5,9},{9,13},{13,1},{2,6},{6,10},{... | collective-permute-start | bytes 3686408 | tf_op jit(solution)/shard_map/ppermute | solution.py:18
  99.8 139.9 %collective-permute-start.19 = (bf16[600,1600]{1,0:T(8,128)(2,1)S(1)}, bf16[600,1600]{1,0:T(8,128)(2,1)}, u32[]{:S(2)}, u32[]{:S(2)}) collective-permute-start(bf16[600,1600]{1,0:T(8,128)(2,1)S(1)} %get-tuple-element.53.refs_10_), channel_id=1, source_target_pairs={{0,1},{1,0},{2,3},{3,2},{4,5},{5,4},{6,7},{7,6},{8,9},{9,8},{10,11... | collective-permute-start | bytes 5760008 | tf_op jit(solution)/shard_map/ppermute | solution.py:211
  135.4 125.2 %collective-permute-start.16 = (bf16[600,1600]{1,0:T(8,128)(2,1)}, bf16[600,1600]{1,0:T(8,128)(2,1)}, u32[]{:S(2)}, u32[]{:S(2)}) collective-permute-start(bf16[600,1600]{1,0:T(8,128)(2,1)} %collective-permute-done.10.refs_12_), channel_id=1, source_target_pairs={{0,1},{1,0},{2,3},{3,2},{4,5},{5,4},{6,7},{7,6},{8,9},{9,8},{10,11... | collective-permute-start | bytes 5760008 | tf_op jit(solution)/shard_map/ppermute | solution.py:215
  137.4 62.2 %all-to-all-start = ((bf16[16,16,200]{2,1,0:T(8,128)(2,1)}), bf16[16,16,200]{2,1,0:T(8,128)(2,1)S(1)}, u32[]{:S(2)}, u32[]{:S(2)}) async-start(bf16[16,16,200]{2,1,0:T(8,128)(2,1)} %bitcast.90), calls=%async_computation | async-start | bytes 262144 | tf_op jit(solution)/shard_map/all_to_all | solution.py:218
  199.6 0.6 copy-start.13
  202.0 8.2 %collective-permute-start.11 = (bf16[16,3200]{1,0:T(8,128)(2,1)}, bf16[16,3200]{1,0:T(8,128)(2,1)S(1)}, u32[]{:S(2)}, u32[]{:S(2)}) collective-permute-start(bf16[16,3200]{1,0:T(8,128)(2,1)} %all_to_all.17), channel_id=1, source_target_pairs={{0,3},{3,0},{1,2},{2,1},{4,7},{7,4},{5,6},{6,5},{8,11},{11,8},{9,1... | collective-permute-start | bytes 307208 | tf_op jit(solution)/shard_map/ppermute | solution.py:219
  204.3 35.4 %collective-permute-start.18 = (bf16[400,1664]{1,0:T(8,128)(2,1)S(1)}, bf16[400,1664]{1,0:T(8,128)(2,1)}, u32[]{:S(2)}, u32[]{:S(2)}) collective-permute-start(bf16[400,1664]{1,0:T(8,128)(2,1)S(1)} %pad_maximum_fusion.2.refs_3_), channel_id=1, source_target_pairs={{0,4},{4,8},{8,12},{12,0},{1,5},{5,9},{9,13},{13,1},{2,6},{6,10},{... | collective-permute-start | bytes 3993608 | tf_op jit(solution)/shard_map/ppermute | solution.py:18
  207.2 53.5 %collective-permute-start.13 = (bf16[400,1536]{1,0:T(8,128)(2,1)}, bf16[400,1536]{1,0:T(8,128)(2,1)}, u32[]{:S(2)}, u32[]{:S(2)}) collective-permute-start(bf16[400,1536]{1,0:T(8,128)(2,1)} %collective-permute-done.12.refs_1_), channel_id=1, source_target_pairs={{0,4},{4,8},{8,12},{12,0},{1,5},{5,9},{9,13},{13,1},{2,6},{6,10},{... | collective-permute-start | bytes 3686408 | tf_op jit(solution)/shard_map/ppermute | solution.py:18
  210.2 50.5 %collective-permute-start.15 = (bf16[400,1664]{1,0:T(8,128)(2,1)}, bf16[400,1664]{1,0:T(8,128)(2,1)}, u32[]{:S(2)}, u32[]{:S(2)}) collective-permute-start(bf16[400,1664]{1,0:T(8,128)(2,1)} %collective-permute-done.14.refs_5_), channel_id=1, source_target_pairs={{0,12},{4,0},{8,4},{12,8},{1,13},{5,1},{9,5},{13,9},{2,14},{6,2},{... | collective-permute-start | bytes 3993608 | tf_op jit(solution)/shard_map/ppermute | solution.py:18
  239.7 1.3 copy-start
  240.9 1.1 copy-start.4
  242.0 1.1 copy-start.6
  243.1 1.1 copy-start.8
  244.2 1.1 copy-start.10
  260.7 2.9 copy-start.1
  266.3 0.7 collective-permute-start.20
  272.1 0.7 collective-permute-start.21
  277.6 0.7 collective-permute-start.22
  283.1 0.7 collective-permute-start.23
  289.0 0.7 collective-permute-start.24
  294.5 0.7 collective-permute-start.25
  300.1 0.7 collective-permute-start.26
  305.7 0.7 collective-permute-start.27
  311.3 0.7 collective-permute-start.28
  316.8 0.7 collective-permute-start.29
  322.5 0.7 collective-permute-start.30
  328.0 0.7 collective-permute-start.31
  333.5 0.7 collective-permute-start.32
  339.3 189.7 %collective-permute-start.33 = (bf16[32,3200]{1,0:T(8,128)(2,1)S(1)}, bf16[32,3200]{1,0:T(8,128)(2,1)S(1)}, u32[]{:S(2)}, u32[]{:S(2)}) collective-permute-start(bf16[32,3200]{1,0:T(8,128)(2,1)S(1)} %add_pair.29), channel_id=1, source_target_pairs={{416,448},{432,451},{419,464},{435,467},{417,449},{433,450},{418,4... | collective-permute-start | bytes 614408 | tf_op jit(solution)/shard_map/ppermute | solution.py:248
  540.0 6.2 %collective-permute-start.34 = (bf16[32,3200]{1,0:T(8,128)(2,1)S(1)}, bf16[32,3200]{1,0:T(8,128)(2,1)S(1)}, u32[]{:S(2)}, u32[]{:S(2)}) collective-permute-start(bf16[32,3200]{1,0:T(8,128)(2,1)S(1)} %add_pair.30), channel_id=1, source_target_pairs={{448,480},{464,483},{451,496},{467,499},{449,481},{465,482},{450,4... | collective-permute-start | bytes 614408 | tf_op jit(solution)/shard_map/ppermute | solution.py:248
  548.8 47.9 %copy-start.11 = (bf16[3200,256]{1,0:T(8,128)(2,1)S(1)}, bf16[3200,256]{1,0:T(8,128)(2,1)}, u32[]{:S(2)}) copy-start(bf16[3200,256]{1,0:T(8,128)(2,1)} %all-gather.33.cloned.1.call-done) | copy-start | bytes 4915204
  551.1 0.7 collective-permute-start.35
  551.9 0.7 collective-permute-start.36
  552.6 0.7 collective-permute-start.37
  553.3 0.7 collective-permute-start.38
  554.0 42.7 %collective-permute-start.39 = (bf16[16,3200]{1,0:T(8,128)(2,1)S(1)}, bf16[16,3200]{1,0:T(8,128)(2,1)S(1)}, u32[]{:S(2)}, u32[]{:S(2)}) collective-permute-start(bf16[16,3200]{1,0:T(8,128)(2,1)S(1)} %add.36), channel_id=1, source_target_pairs={{480,0},{224,256},{96,128},{352,384},{32,64},{288,320},{160,192},{... | collective-permute-start | bytes 307208 | tf_op jit(solution)/shard_map/ppermute | solution.py:263
Sparse Core Ops, SparseCore 0:
  89.2 61.2 all-gather.32

commit v6 on v5

--- a/solution.py
+++ b/solution.py
@@ -36,13 +36,16 @@
 
 
 def put(plan, spots_ref, *refs):
-    sources, targets, sems = refs[: len(plan)], refs[-5:-1], refs[-1]
-    run_all(
-        [
-            pltpu.make_async_copy(source, targets[to].at[spots_ref[spot]], sems.at[i])
-            for i, (source, (to, spot)) in enumerate(zip(sources, plan))
-        ]
-    )
+    count = len(plan)
+    sources, targets, sems = refs[:count], refs[-4:-1], refs[-1]
+    copies = []
+    for i, (to, spot, start) in enumerate(plan):
+        place = targets[to].at[spots_ref[spot]]
+        width = sources[i].shape[1]
+        if width != targets[to].shape[2]:
+            place = place.at[:, start : start + width]
+        copies.append(pltpu.make_async_copy(sources[i], place, sems.at[i]))
+    run_all(copies)
 
 
 def put_pieces(spots, plan, pieces, targets, shapes):
@@ -53,7 +56,7 @@
         out_shape=tuple(jax.ShapeDtypeStruct(s, pieces[0].dtype) for s in shapes),
         in_specs=[pl.BlockSpec(memory_space=pltpu.SMEM)]
         + [anywhere] * (count + len(targets)),
-        out_specs=(anywhere,) * 4,
+        out_specs=(anywhere,) * 3,
         scratch_shapes=[pltpu.SemaphoreType.DMA((count,))],
         input_output_aliases={1 + count + i: i for i in range(len(targets))},
         compiler_params=pltpu.CompilerParams(vmem_limit_bytes=2**20),
@@ -68,8 +71,8 @@
 
 
 def quarter_layer(tick_ref, state_ref, pair_ref, *refs):
-    left_ref, right_ref, own_ref, rest_ref, out_ref, hidden_ref, total_ref = refs
-    step, cut = left_ref.shape[1:]
+    up_ref, own_ref, rest_ref, out_ref, hidden_ref, total_ref = refs
+    step = up_ref.shape[1]
     block = own_ref.shape[1]
     active = tick_ref[0] == state_ref[0]
 
@@ -83,9 +86,7 @@
         scale = lax.rsqrt(jnp.mean(rows * rows, axis=1, keepdims=True) + 1e-06)
         normed = (rows * scale).astype(jnp.bfloat16)
         for i in range(SIDE):
-            part = product(normed[:, :cut], left_ref[i])
-            part = part + product(normed[:, cut:], right_ref[i])
-            part = jax.nn.gelu(part).astype(jnp.bfloat16)
+            part = jax.nn.gelu(product(normed, up_ref[i])).astype(jnp.bfloat16)
             hidden_ref[:, i * step : (i + 1) * step] = part
         hidden = hidden_ref[...]
         places = [lax.rem(state_ref[2] + offset, SIDE) for offset in OFFSETS]
@@ -102,13 +103,13 @@
 
 def apply_quarter(tick, state, pair, weights):
     _, row_count, width = pair.shape
-    units, block = weights[2].shape[2], weights[2].shape[1]
+    units, block = weights[1].shape[2], weights[1].shape[1]
     resident = pl.BlockSpec(memory_space=pltpu.VMEM)
     scalar = pl.BlockSpec(memory_space=pltpu.SMEM)
     return pl.pallas_call(
         quarter_layer,
         out_shape=jax.ShapeDtypeStruct((row_count, width), jnp.bfloat16),
-        in_specs=[scalar] * 2 + [resident] * 5,
+        in_specs=[scalar] * 2 + [resident] * 4,
         out_specs=resident,
         scratch_shapes=[
             pltpu.VMEM((row_count, units), jnp.bfloat16),
@@ -197,26 +198,26 @@
     beside = lax.ppermute(own, "x", INTRA)
     across = lax.ppermute(other, "x", INTER)
     corner = lax.ppermute(across, "x", INTRA)
-    held = (own_ring, other_ring, beside, across, corner)
-    own_ring, other_ring, beside, across, corner = lax.optimization_barrier(held)
+    beside, across, patches = lax.optimization_barrier((beside, across, patches))
+    flat = patches.reshape(-1, patches.shape[2])
+    rows = lax.all_to_all(flat, tp, split_axis=0, concat_axis=1, tiled=True)
+    held = (own_ring, other_ring, beside, across, rows)
+    own_ring, other_ring, beside, across, rows = lax.optimization_barrier(held)
     own_rest = jnp.concatenate(own_ring, axis=0)
     other_rest = jnp.concatenate(other_ring, axis=0)
-
-    even = (lax.rem(x, 2) == 0).astype(jnp.int32)
-    cut = w_in.shape[2] // 256 * 128
-    left = by_halves(even, w_in[0, :, :cut], mate[:, :cut])
-    right = by_halves(even, w_in[0, :, cut:], mate[:, cut:])
-    held = (left, right, own_rest, other_rest)
-    left, right, own_rest, other_rest = lax.optimization_barrier(held)
+    rows = by_halves(low, rows, lax.ppermute(rows, "x", INTER))
+
+    near = by_halves((lax.rem(x, 2) == 0).astype(jnp.int32), w_in[0], mate)
+    held = (near, own_rest, other_rest)
+    near, own_rest, other_rest = lax.optimization_barrier(held)
     beside_rest = lax.ppermute(own_rest, "x", INTRA)
     across_rest = lax.ppermute(other_rest, "x", INTER)
-    left_ring, right_ring = ring(left, right, "y")
-    across_rest, patches = lax.optimization_barrier((across_rest, patches))
     corner_rest = lax.ppermute(across_rest, "x", INTRA)
-
-    flat = patches.reshape(-1, patches.shape[2])
-    rows = lax.all_to_all(flat, tp, split_axis=0, concat_axis=1, tiled=True)
-    rows = by_halves(low, rows, lax.ppermute(rows, "x", INTER))
+    cut = near.shape[1] // 256 * 128
+    below = moved(near, "y", 1)
+    above = moved(near, "y", -1)
+    head = moved(below[:, :cut], "y", 1)
+    tail = moved(above[:, cut:], "y", -1)
 
     mate_x = x + 1 - 2 * lax.rem(x, 2)
     spots = [lax.rem(y + offset, SIDE) for offset in OFFSETS]
@@ -228,16 +229,15 @@
     pair = jnp.stack([rows, jnp.zeros_like(rows)])
     held = (spots, pair, state, projection)
     spots, pair, state, projection = lax.optimization_barrier(held)
-    early = [(left, 0, 0), (left_ring[0], 0, 1), (left_ring[1], 0, 2)]
-    early += [(right, 1, 0), (right_ring[0], 1, 1), (right_ring[1], 1, 2)]
-    early += [(own, 2, 4), (beside, 2, 5), (across, 2, 6), (corner, 2, 7)]
-    early += [(own_rest, 3, 4), (beside_rest, 3, 5), (across_rest, 3, 6)]
-    late = [(left_ring[2], 0, 3), (right_ring[2], 1, 3), (corner_rest, 3, 7)]
-    shapes = [(SIDE,) + piece.shape for piece in (left, right, own, own_rest)]
+    early = [(near, 0, 0, 0), (below, 0, 1, 0), (above, 0, 2, 0)]
+    early += [(own, 1, 4, 0), (beside, 1, 5, 0), (across, 1, 6, 0), (corner, 1, 7, 0)]
+    early += [(own_rest, 2, 4, 0), (beside_rest, 2, 5, 0), (across_rest, 2, 6, 0)]
+    late = [(head, 0, 3, 0), (tail, 0, 3, cut), (corner_rest, 2, 7, 0)]
+    shapes = [(SIDE,) + piece.shape for piece in (near, own, own_rest)]
     weights = ()
     for group in (early, late):
-        plan = tuple((to, spot) for _, to, spot in group)
-        pieces = [piece for piece, _, _ in group]
+        plan = tuple(entry[1:] for entry in group)
+        pieces = [entry[0] for entry in group]
         weights = put_pieces(spots, plan, pieces, weights, shapes)
     weights = [pltpu.with_memory_space_constraint(w, pltpu.VMEM) for w in weights]
     for layer in range(layers):

time: 613 us -> 555 us (0.905)
  waiting for transfers between devices: 398 us -> 345 us
    ppermute x12 -> x10, waiting for transfers between devices: 43.1 us -> 5.39 us  [moved(): return lax.ppermute(block, axis, route)]
    all_to_all x1, waiting for transfers between devices: 56.6 us -> 20 us  [on_device(): rows = lax.all_to_all(flat, tp, split_axis=0, concat_axis=1, tiled=True)]
    ppermute x1, waiting for transfers between devices: 26.1 us -> 40 us  [on_device(): corner = lax.ppermute(across, 'x', INTRA)]
    ppermute x1, waiting for transfers between devices: 33.5 us -> 42.4 us  [on_device(): across_rest = lax.ppermute(other_rest, 'x', INTER)]
    ppermute x12 -> x10, starting transfers between devices: 41.1 us -> 33.4 us  [moved(): return lax.ppermute(block, axis, route)]
  transfers between devices with their start and end apart: 42 -> 40, of which waited for: 12 -> 10; matrix products, arithmetic and copies ran while one was open for 0% -> 1% of each run, Pallas kernels for 1% -> 1%
where the time goes in v6:
time: 555 us; the launch traced here: 547 us
  waiting for transfers between devices  345 us (62%)
  starting transfers between devices  78 us (14%)
  blocking collectives  65.2 us (12%)
  Pallas kernels  26.4 us (5%)
  between operations  14.7 us (3%)
  local copies, waits for them, and re-layouts  11.2 us (2%)
  other arithmetic  6.12 us (1%)
    ppermute x15, waiting for transfers between devices, on_device(): part = lax.ppermute(part, ('z', 'c', 'x'), next_plane(layer))  192 us
    ppermute x1, waiting for transfers between devices, on_device(): across_rest = lax.ppermute(other_rest, 'x', INTER)  42.4 us
    ppermute x4, waiting for transfers between devices, on_device(): rows = rows + lax.ppermute(rows, 'z', route)  41.4 us
    ppermute x1, waiting for transfers between devices, on_device(): corner = lax.ppermute(across, 'x', INTRA)  40 us
    all_gather x16, blocking collectives, on_device(): part = added(lax.all_gather(part, 'c', axis=0, tiled=False))  33.7 us
    ppermute x10, starting transfers between devices, moved(): return lax.ppermute(block, axis, route)  33.4 us
    all_gather x15, blocking collectives, on_device(): pair = lax.all_gather(part, 'c', axis=0, tiled=False)  31.5 us
    all_to_all x1, waiting for transfers between devices, on_device(): rows = lax.all_to_all(flat, tp, split_axis=0, concat_axis=1, tiled=True)  20 us
  transfers between devices with their start and end apart: 40, of which 10 were waited for; matrix products, arithmetic and copies ran while one was open for 1% of the time, Pallas kernels for 1%

profile of v6, /device:TPU:448, one launch (start us, length us, event | category | flops | bytes accessed | tf_op | source)
XLA Modules:
  0.0 547.2 jit_solution(8129752186423160594)
XLA Ops:
  8.8 4.7 collective-permute-start.7
  13.5 4.9 collective-permute-start.4
  18.4 2.1 collective-permute-start.6
  20.6 1.9 collective-permute-start
  22.5 3.7 collective-permute-start.9
  26.2 2.5 collective-permute-done.7.refs_5_
  28.7 3.5 collective-permute-start.3
  32.3 5.6 %collective-permute-start.1 = (bf16[200,1600]{1,0:T(8,128)(2,1)S(1)}, bf16[200,1600]{1,0:T(8,128)(2,1)}, u32[]{:S(2)}, u32[]{:S(2)}) collective-permute-start(bf16[200,1600]{1,0:T(8,128)(2,1)S(1)} %get-tuple-element.32.refs_3_), channel_id=1, source_target_pairs={{0,12},{4,0},{8,4},{12,8},{1,13},{5,1},{9,5},{13,9},{2,14},{6,2},{... | collective-permute-start | bytes 1920008 | tf_op jit(solution)/shard_map/ppermute | solution.py:18
  39.1 2.6 collective-permute-start.5
  41.8 3.2 collective-permute-start.2
  45.0 4.5 all-to-all-start
  49.5 20.0 %all-to-all-done = bf16[16,16,200]{2,1,0:T(8,128)(2,1)S(1)} async-done(((bf16[16,16,200]{2,1,0:T(8,128)(2,1)}), bf16[16,16,200]{2,1,0:T(8,128)(2,1)S(1)}, u32[]{:S(2)}, u32[]{:S(2)}) %all-to-all-start) | async-done | bytes 102432 | tf_op jit(solution)/shard_map/all_to_all | solution.py:203
  71.6 4.2 pad_maximum_fusion.1
  75.7 2.7 collective-permute-start.12
  78.4 3.2 collective-permute-start.10
  81.6 3.0 collective-permute-start.14
  84.6 2.6 collective-permute-start.17
  87.2 42.4 %collective-permute-done.14.refs_9_ = bf16[600,1600]{1,0:T(8,128)(2,1)} collective-permute-done((bf16[600,1600]{1,0:T(8,128)(2,1)}, bf16[600,1600]{1,0:T(8,128)(2,1)}, u32[]{:S(2)}, u32[]{:S(2)}) %collective-permute-start.14) | collective-permute-done | bytes 1920032 | tf_op jit(solution)/shard_map/ppermute | solution.py:214
  129.6 2.3 collective-permute-start.15
  132.1 2.8 collective-permute-start.8
  135.0 5.2 collective-permute-done.12.refs_2_
  140.2 3.6 collective-permute-start.16
  143.8 2.5 slice.19
  146.3 2.0 collective-permute-start.13
  148.3 2.4 slice.18
  150.7 3.8 collective-permute-start.11
  154.6 40.0 %collective-permute-done.16.refs_6_ = bf16[200,1600]{1,0:T(8,128)(2,1)} collective-permute-done((bf16[200,1600]{1,0:T(8,128)(2,1)}, bf16[200,1600]{1,0:T(8,128)(2,1)}, u32[]{:S(2)}, u32[]{:S(2)}) %collective-permute-start.16) | collective-permute-done | bytes 640032 | tf_op jit(solution)/shard_map/ppermute | solution.py:200
  198.4 5.3 put_pieces.2
  203.8 2.9 put_pieces.3
  207.3 2.1 all-gather
  210.1 2.1 all-gather.1
  213.0 2.1 all-gather.2
  215.8 2.1 all-gather.3
  218.5 2.1 all-gather.4
  221.4 2.1 all-gather.5
  224.0 2.1 all-gather.6
  226.9 2.1 all-gather.7
  230.0 2.1 all-gather.8
  232.8 2.1 all-gather.9
  235.5 2.1 all-gather.10
  238.3 2.1 all-gather.11
  241.0 2.1 all-gather.12
  243.8 2.1 all-gather.13
  246.7 2.1 all-gather.14
  249.5 2.1 all-gather.15
  252.2 2.1 all-gather.16
  255.0 2.1 all-gather.17
  257.7 2.1 all-gather.18
  260.6 2.1 all-gather.19
  263.4 2.1 all-gather.20
  266.3 2.1 all-gather.21
  269.0 2.1 all-gather.22
  271.8 2.1 all-gather.23
  274.5 2.1 all-gather.24
  277.3 2.1 all-gather.25
  280.2 2.1 all-gather.26
  283.7 187.6 %collective-permute-done.31 = bf16[32,3200]{1,0:T(8,128)(2,1)S(1)} collective-permute-done((bf16[32,3200]{1,0:T(8,128)(2,1)S(1)}, bf16[32,3200]{1,0:T(8,128)(2,1)S(1)}, u32[]{:S(2)}, u32[]{:S(2)}) %collective-permute-start.31) | collective-permute-done | bytes 204832 | tf_op jit(solution)/shard_map/ppermute | solution.py:248
  471.3 2.1 all-gather.27
  473.3 6.7 %quarter_layer.30 = bf16[32,3200]{1,0:T(8,128)(2,1)S(1)} custom-call(s32[1]{0:T(128)} %constant.59.clone.1.tick_ref, s32[3]{0:T(128)S(1)} %pad_add_fusion.state_ref, bf16[2,32,3200]{2,1,0:T(8,128)(2,1)S(1)} %bitcast.66, bf16[4,400,3200]{2,1,0:T(8,128)(2,1)S(1)} %get-tuple-element.55.refs_0_, bf16[4,200,1600]{2,1,0:T(8,128)(2,1)S(1)} %get-tuple-element.56.refs_1_, ...), custom_call_target="tpu_custom_call" | custom-call | flops 655360000 | bytes 409600 | tf_op jit(solution)/shard_map/quarter_layer/pallas_call | solution.py:109
  480.1 2.1 all-gather.28
  483.6 4.9 collective-permute-done.32
  488.4 2.1 all-gather.29
  491.1 2.2 all-gather.30
  497.6 41.4 %collective-permute-done.37 = bf16[16,3200]{1,0:T(8,128)(2,1)S(1)} collective-permute-done((bf16[16,3200]{1,0:T(8,128)(2,1)S(1)}, bf16[16,3200]{1,0:T(8,128)(2,1)S(1)}, u32[]{:S(2)}, u32[]{:S(2)}) %collective-permute-start.37) | collective-permute-done | bytes 102432 | tf_op jit(solution)/shard_map/ppermute | solution.py:263
  (117 shorter events, 36.5 us)
Async XLA Ops:
  6.5 1.3 copy-start.1
  7.8 62.0 %copy-start.7 = (bf16[1,200,3200]{2,1,0:T(8,128)(2,1)S(1)}, bf16[1,200,3200]{2,1,0:T(8,128)(2,1)}, u32[]{:S(2)}) copy-start(bf16[1,200,3200]{2,1,0:T(8,128)(2,1)} %param.5) | copy-start | bytes 3840004
  8.8 62.5 %copy-start.2 = (bf16[200,1600]{1,0:T(8,128)(2,1)}, bf16[200,1600]{1,0:T(8,128)(2,1)S(1)}, u32[]{:S(2)}) copy-start(bf16[200,1600]{1,0:T(8,128)(2,1)S(1)} %get-tuple-element.32.refs_3_) | copy-start | bytes 1920004
  8.8 19.9 %collective-permute-start.7 = (bf16[200,1600]{1,0:T(8,128)(2,1)S(1)}, bf16[200,1600]{1,0:T(8,128)(2,1)}, u32[]{:S(2)}, u32[]{:S(2)}) collective-permute-start(bf16[200,1600]{1,0:T(8,128)(2,1)S(1)} %get-tuple-element.33), channel_id=1, source_target_pairs={{0,3},{3,0},{1,2},{2,1},{4,7},{7,4},{5,6},{6,5},{8,11},{11,8},{9,1... | collective-permute-start | bytes 1920008 | tf_op jit(solution)/shard_map/ppermute | solution.py:199
  13.5 18.8 %collective-permute-start.4 = (bf16[200,1600]{1,0:T(8,128)(2,1)S(1)}, bf16[200,1600]{1,0:T(8,128)(2,1)S(1)}, u32[]{:S(2)}, u32[]{:S(2)}) collective-permute-start(bf16[200,1600]{1,0:T(8,128)(2,1)S(1)} %get-tuple-element.33), channel_id=1, source_target_pairs={{0,12},{4,0},{8,4},{12,8},{1,13},{5,1},{9,5},{13,9},{2,14},{6,2},{... | collective-permute-start | bytes 1920008 | tf_op jit(solution)/shard_map/ppermute | solution.py:18
  18.4 19.8 %collective-permute-start.6 = (bf16[200,1600]{1,0:T(8,128)(2,1)S(1)}, bf16[200,1600]{1,0:T(8,128)(2,1)S(1)}, u32[]{:S(2)}, u32[]{:S(2)}) collective-permute-start(bf16[200,1600]{1,0:T(8,128)(2,1)S(1)} %get-tuple-element.32.refs_3_), channel_id=1, source_target_pairs={{0,1},{1,0},{2,3},{3,2},{4,5},{5,4},{6,7},{7,6},{8,9},{9,8},{10,11... | collective-permute-start | bytes 1920008 | tf_op jit(solution)/shard_map/ppermute | solution.py:198
  20.6 21.2 %collective-permute-start = (bf16[200,1600]{1,0:T(8,128)(2,1)S(1)}, bf16[200,1600]{1,0:T(8,128)(2,1)}, u32[]{:S(2)}, u32[]{:S(2)}) collective-permute-start(bf16[200,1600]{1,0:T(8,128)(2,1)S(1)} %get-tuple-element.32.refs_3_), channel_id=1, source_target_pairs={{0,4},{4,8},{8,12},{12,0},{1,5},{5,9},{9,13},{13,1},{2,6},{6,10},{... | collective-permute-start | bytes 1920008 | tf_op jit(solution)/shard_map/ppermute | solution.py:18
  22.5 47.3 %collective-permute-start.9 = (bf16[200,3200]{1,0:T(8,128)(2,1)}, bf16[200,3200]{1,0:T(8,128)(2,1)}, u32[]{:S(2)}, u32[]{:S(2)}) collective-permute-start(bf16[200,3200]{1,0:T(8,128)(2,1)} %bitcast.84), channel_id=1, source_target_pairs={{0,1},{1,0},{2,3},{3,2},{4,5},{5,4},{6,7},{7,6},{8,9},{9,8},{10,11... | collective-permute-start | bytes 3840008 | tf_op jit(solution)/shard_map/ppermute | solution.py:196
  28.7 41.1 %collective-permute-start.3 = (bf16[200,1600]{1,0:T(8,128)(2,1)S(1)}, bf16[200,1600]{1,0:T(8,128)(2,1)}, u32[]{:S(2)}, u32[]{:S(2)}) collective-permute-start(bf16[200,1600]{1,0:T(8,128)(2,1)S(1)} %get-tuple-element.33), channel_id=1, source_target_pairs={{0,4},{4,8},{8,12},{12,0},{1,5},{5,9},{9,13},{13,1},{2,6},{6,10},{... | collective-permute-start | bytes 1920008 | tf_op jit(solution)/shard_map/ppermute | solution.py:18
  32.3 37.5 %collective-permute-start.1 = (bf16[200,1600]{1,0:T(8,128)(2,1)S(1)}, bf16[200,1600]{1,0:T(8,128)(2,1)}, u32[]{:S(2)}, u32[]{:S(2)}) collective-permute-start(bf16[200,1600]{1,0:T(8,128)(2,1)S(1)} %get-tuple-element.32.refs_3_), channel_id=1, source_target_pairs={{0,12},{4,0},{8,4},{12,8},{1,13},{5,1},{9,5},{13,9},{2,14},{6,2},{... | collective-permute-start | bytes 1920008 | tf_op jit(solution)/shard_map/ppermute | solution.py:18
  38.2 0.9 copy-start.4
  39.1 30.7 %collective-permute-start.5 = (bf16[200,1600]{1,0:T(8,128)(2,1)S(1)}, bf16[200,1600]{1,0:T(8,128)(2,1)}, u32[]{:S(2)}, u32[]{:S(2)}) collective-permute-start(bf16[200,1600]{1,0:T(8,128)(2,1)S(1)} %collective-permute-done.4), channel_id=1, source_target_pairs={{0,12},{4,0},{8,4},{12,8},{1,13},{5,1},{9,5},{13,9},{2,14},{6,2},{... | collective-permute-start | bytes 1920008 | tf_op jit(solution)/shard_map/ppermute | solution.py:18
  41.8 28.1 %collective-permute-start.2 = (bf16[200,1600]{1,0:T(8,128)(2,1)}, bf16[200,1600]{1,0:T(8,128)(2,1)}, u32[]{:S(2)}, u32[]{:S(2)}) collective-permute-start(bf16[200,1600]{1,0:T(8,128)(2,1)} %collective-permute-done), channel_id=1, source_target_pairs={{0,4},{4,8},{8,12},{12,0},{1,5},{5,9},{9,13},{13,1},{2,6},{6,10},{... | collective-permute-start | bytes 1920008 | tf_op jit(solution)/shard_map/ppermute | solution.py:18
  45.0 24.6 %all-to-all-start = ((bf16[16,16,200]{2,1,0:T(8,128)(2,1)}), bf16[16,16,200]{2,1,0:T(8,128)(2,1)S(1)}, u32[]{:S(2)}, u32[]{:S(2)}) async-start(bf16[16,16,200]{2,1,0:T(8,128)(2,1)} %bitcast.86), calls=%async_computation | async-start | bytes 262144 | tf_op jit(solution)/shard_map/all_to_all | solution.py:203
  49.5 105.2 %all-gather.33.cloned.1.call-start = ((), (), s32[]{:S(2)}) async-start(), calls=%async_computation.1 | async-start | bytes 1740800 | tf_op jit(solution)/shard_map/all_gather | solution.py:226
  75.7 64.5 %collective-permute-start.12 = (bf16[400,3200]{1,0:T(8,128)(2,1)S(1)}, bf16[400,3200]{1,0:T(8,128)(2,1)}, u32[]{:S(2)}, u32[]{:S(2)}) collective-permute-start(bf16[400,3200]{1,0:T(8,128)(2,1)S(1)} %pad_maximum_fusion.refs_0_), channel_id=1, source_target_pairs={{0,12},{4,0},{8,4},{12,8},{1,13},{5,1},{9,5},{13,9},{2,14},{6,2},{... | collective-permute-start | bytes 7680008 | tf_op jit(solution)/shard_map/ppermute | solution.py:18
  78.4 67.9 %collective-permute-start.10 = (bf16[400,3200]{1,0:T(8,128)(2,1)S(1)}, bf16[400,3200]{1,0:T(8,128)(2,1)}, u32[]{:S(2)}, u32[]{:S(2)}) collective-permute-start(bf16[400,3200]{1,0:T(8,128)(2,1)S(1)} %pad_maximum_fusion.refs_0_), channel_id=1, source_target_pairs={{0,4},{4,8},{8,12},{12,0},{1,5},{5,9},{9,13},{13,1},{2,6},{6,10},{... | collective-permute-start | bytes 7680008 | tf_op jit(solution)/shard_map/ppermute | solution.py:18
  81.6 48.0 %collective-permute-start.14 = (bf16[600,1600]{1,0:T(8,128)(2,1)}, bf16[600,1600]{1,0:T(8,128)(2,1)}, u32[]{:S(2)}, u32[]{:S(2)}) collective-permute-start(bf16[600,1600]{1,0:T(8,128)(2,1)} %get-tuple-element.48), channel_id=1, source_target_pairs={{0,3},{3,0},{1,2},{2,1},{4,7},{7,4},{5,6},{6,5},{8,11},{11,8},{9,1... | collective-permute-start | bytes 5760008 | tf_op jit(solution)/shard_map/ppermute | solution.py:214
  84.6 110.1 %collective-permute-start.17 = (bf16[600,1600]{1,0:T(8,128)(2,1)}, bf16[600,1600]{1,0:T(8,128)(2,1)}, u32[]{:S(2)}, u32[]{:S(2)}) collective-permute-start(bf16[600,1600]{1,0:T(8,128)(2,1)} %get-tuple-element.51.refs_7_), channel_id=1, source_target_pairs={{0,1},{1,0},{2,3},{3,2},{4,5},{5,4},{6,7},{7,6},{8,9},{9,8},{10,11... | collective-permute-start | bytes 5760008 | tf_op jit(solution)/shard_map/ppermute | solution.py:213
  129.6 74.2 %collective-permute-start.15 = (bf16[600,1600]{1,0:T(8,128)(2,1)}, bf16[600,1600]{1,0:T(8,128)(2,1)}, u32[]{:S(2)}, u32[]{:S(2)}) collective-permute-start(bf16[600,1600]{1,0:T(8,128)(2,1)} %collective-permute-done.14.refs_9_), channel_id=1, source_target_pairs={{0,1},{1,0},{2,3},{3,2},{4,5},{5,4},{6,7},{7,6},{8,9},{9,8},{10,11... | collective-permute-start | bytes 5760008 | tf_op jit(solution)/shard_map/ppermute | solution.py:215
  132.1 18.6 %collective-permute-start.8 = (bf16[16,3200]{1,0:T(8,128)(2,1)S(1)}, bf16[16,3200]{1,0:T(8,128)(2,1)S(1)}, u32[]{:S(2)}, u32[]{:S(2)}) collective-permute-start(bf16[16,3200]{1,0:T(8,128)(2,1)S(1)} %all_to_all.17), channel_id=1, source_target_pairs={{0,3},{3,0},{1,2},{2,1},{4,7},{7,4},{5,6},{6,5},{8,11},{11,8},{9,1... | collective-permute-start | bytes 307208 | tf_op jit(solution)/shard_map/ppermute | solution.py:208
  140.2 54.5 %collective-permute-start.16 = (bf16[200,1600]{1,0:T(8,128)(2,1)}, bf16[200,1600]{1,0:T(8,128)(2,1)}, u32[]{:S(2)}, u32[]{:S(2)}) collective-permute-start(bf16[200,1600]{1,0:T(8,128)(2,1)} %collective-permute-done.7.refs_5_), channel_id=1, source_target_pairs={{0,1},{1,0},{2,3},{3,2},{4,5},{5,4},{6,7},{7,6},{8,9},{9,8},{10,11... | collective-permute-start | bytes 1920008 | tf_op jit(solution)/shard_map/ppermute | solution.py:200
  146.3 57.5 %collective-permute-start.13 = (bf16[400,1664]{1,0:T(8,128)(2,1)}, bf16[400,1664]{1,0:T(8,128)(2,1)}, u32[]{:S(2)}, u32[]{:S(2)}) collective-permute-start(bf16[400,1664]{1,0:T(8,128)(2,1)} %slice.19), channel_id=1, source_target_pairs={{0,12},{4,0},{8,4},{12,8},{1,13},{5,1},{9,5},{13,9},{2,14},{6,2},{... | collective-permute-start | bytes 3993608 | tf_op jit(solution)/shard_map/ppermute | solution.py:18
  150.7 53.0 %collective-permute-start.11 = (bf16[400,1536]{1,0:T(8,128)(2,1)}, bf16[400,1536]{1,0:T(8,128)(2,1)}, u32[]{:S(2)}, u32[]{:S(2)}) collective-permute-start(bf16[400,1536]{1,0:T(8,128)(2,1)} %slice.18), channel_id=1, source_target_pairs={{0,4},{4,8},{8,12},{12,0},{1,5},{5,9},{9,13},{13,1},{2,6},{6,10},{... | collective-permute-start | bytes 3686408 | tf_op jit(solution)/shard_map/ppermute | solution.py:18
  194.7 1.6 copy-start
  196.3 1.1 copy-start.3
  197.3 1.1 copy-start.5
  209.4 0.7 collective-permute-start.18
  215.2 0.7 collective-permute-start.19
  220.7 0.7 collective-permute-start.20
  226.2 0.7 collective-permute-start.21
  232.1 0.7 collective-permute-start.22
  237.6 0.7 collective-permute-start.23
  243.1 0.7 collective-permute-start.24
  248.8 0.7 collective-permute-start.25
  254.3 0.7 collective-permute-start.26
  259.9 0.7 collective-permute-start.27
  265.6 0.7 collective-permute-start.28
  271.1 0.7 collective-permute-start.29
  276.6 0.7 collective-permute-start.30
  282.4 188.9 %collective-permute-start.31 = (bf16[32,3200]{1,0:T(8,128)(2,1)S(1)}, bf16[32,3200]{1,0:T(8,128)(2,1)S(1)}, u32[]{:S(2)}, u32[]{:S(2)}) collective-permute-start(bf16[32,3200]{1,0:T(8,128)(2,1)S(1)} %add_pair.29), channel_id=1, source_target_pairs={{416,448},{432,451},{419,464},{435,467},{417,449},{433,450},{418,4... | collective-permute-start | bytes 614408 | tf_op jit(solution)/shard_map/ppermute | solution.py:248
  482.2 6.2 %collective-permute-start.32 = (bf16[32,3200]{1,0:T(8,128)(2,1)S(1)}, bf16[32,3200]{1,0:T(8,128)(2,1)S(1)}, u32[]{:S(2)}, u32[]{:S(2)}) collective-permute-start(bf16[32,3200]{1,0:T(8,128)(2,1)S(1)} %add_pair.30), channel_id=1, source_target_pairs={{448,480},{464,483},{451,496},{467,499},{449,481},{465,482},{450,4... | collective-permute-start | bytes 614408 | tf_op jit(solution)/shard_map/ppermute | solution.py:248
  491.1 47.9 %copy-start.6 = (bf16[3200,256]{1,0:T(8,128)(2,1)S(1)}, bf16[3200,256]{1,0:T(8,128)(2,1)}, u32[]{:S(2)}) copy-start(bf16[3200,256]{1,0:T(8,128)(2,1)} %all-gather.33.cloned.1.call-done) | copy-start | bytes 4915204
  493.4 0.7 collective-permute-start.33
  494.2 0.7 collective-permute-start.34
  494.9 0.7 collective-permute-start.35
  495.6 0.7 collective-permute-start.36
  496.3 42.7 %collective-permute-start.37 = (bf16[16,3200]{1,0:T(8,128)(2,1)S(1)}, bf16[16,3200]{1,0:T(8,128)(2,1)S(1)}, u32[]{:S(2)}, u32[]{:S(2)}) collective-permute-start(bf16[16,3200]{1,0:T(8,128)(2,1)S(1)} %add.36), channel_id=1, source_target_pairs={{480,0},{224,256},{96,128},{352,384},{32,64},{288,320},{160,192},{... | collective-permute-start | bytes 307208 | tf_op jit(solution)/shard_map/ppermute | solution.py:263
Sparse Core Ops, SparseCore 0:
  84.7 60.2 all-gather.32

commit v7 on v6

--- a/solution.py
+++ b/solution.py
@@ -198,14 +198,10 @@
     beside = lax.ppermute(own, "x", INTRA)
     across = lax.ppermute(other, "x", INTER)
     corner = lax.ppermute(across, "x", INTRA)
-    beside, across, patches = lax.optimization_barrier((beside, across, patches))
-    flat = patches.reshape(-1, patches.shape[2])
-    rows = lax.all_to_all(flat, tp, split_axis=0, concat_axis=1, tiled=True)
-    held = (own_ring, other_ring, beside, across, rows)
-    own_ring, other_ring, beside, across, rows = lax.optimization_barrier(held)
+    held = (own_ring, other_ring, beside, across)
+    own_ring, other_ring, beside, across = lax.optimization_barrier(held)
     own_rest = jnp.concatenate(own_ring, axis=0)
     other_rest = jnp.concatenate(other_ring, axis=0)
-    rows = by_halves(low, rows, lax.ppermute(rows, "x", INTER))
 
     near = by_halves((lax.rem(x, 2) == 0).astype(jnp.int32), w_in[0], mate)
     held = (near, own_rest, other_rest)
@@ -223,16 +219,30 @@
     spots = [lax.rem(y + offset, SIDE) for offset in OFFSETS]
     spots += [x, mate_x, SIDE - 1 - x, SIDE - 1 - mate_x]
     spots = jnp.stack(spots).astype(jnp.int32)
-    projection = lax.all_gather(w_proj, tp, axis=0, tiled=True)
+    features, outputs = w_proj.shape
+    flat = patches.reshape(-1, features)
+    flat = jnp.pad(flat, ((0, 0), (0, outputs - features)))
+    everyone = lax.all_gather(jnp.concatenate([flat, w_proj], axis=0), tp, axis=0)
+    projection = everyone[:, flat.shape[0] :].reshape(-1, outputs)
+    count = flat.shape[0] // SIDE // SIDE
+
+    def rows_of(column):
+        at = (SIDE * y + column) * count
+        block = lax.dynamic_slice_in_dim(everyone, at, count, axis=1)
+        return block[:, :, :features].transpose(1, 0, 2).reshape(count, -1)
+
+    first = jnp.where(low == 1, x, SIDE - 1 - x)
+    rows = jnp.concatenate([rows_of(first), rows_of(SIDE - 1 - first)], axis=0)
     adds = jnp.logical_and(core == 0, low == 1)
     state = jnp.stack([plane, adds, y]).astype(jnp.int32)
     pair = jnp.stack([rows, jnp.zeros_like(rows)])
     held = (spots, pair, state, projection)
     spots, pair, state, projection = lax.optimization_barrier(held)
     early = [(near, 0, 0, 0), (below, 0, 1, 0), (above, 0, 2, 0)]
-    early += [(own, 1, 4, 0), (beside, 1, 5, 0), (across, 1, 6, 0), (corner, 1, 7, 0)]
+    early += [(own, 1, 4, 0), (beside, 1, 5, 0), (across, 1, 6, 0)]
     early += [(own_rest, 2, 4, 0), (beside_rest, 2, 5, 0), (across_rest, 2, 6, 0)]
-    late = [(head, 0, 3, 0), (tail, 0, 3, cut), (corner_rest, 2, 7, 0)]
+    late = [(head, 0, 3, 0), (tail, 0, 3, cut)]
+    late += [(corner, 1, 7, 0), (corner_rest, 2, 7, 0)]
     shapes = [(SIDE,) + piece.shape for piece in (near, own, own_rest)]
     weights = ()
     for group in (early, late):

time: 555 us -> 549 us (0.989)
  starting transfers between devices: 78 us -> 63.5 us
    ppermute x1, waiting for transfers between devices: 0.28 us -> 29 us  [on_device(): beside = lax.ppermute(own, 'x', INTRA)]
    ppermute x10, waiting for transfers between devices: 5.39 us -> 26.5 us  [moved(): return lax.ppermute(block, axis, route)]
    all_to_all x1 -> x0, waiting for transfers between devices: 20 us -> none  [on_device(): rows = lax.all_to_all(flat, tp, split_axis=0, concat_axis=1, tiled=True)]
    ppermute x1, waiting for transfers between devices: 40 us -> 23.4 us  [on_device(): corner = lax.ppermute(across, 'x', INTRA)]
    ppermute x15, waiting for transfers between devices: 192 us -> 185 us  [on_device(): part = lax.ppermute(part, ('z', 'c', 'x'), next_plane(layer))]
  transfers between devices with their start and end apart: 40 -> 38, of which waited for: 10 -> 13; matrix products, arithmetic and copies ran while one was open for 1% -> 2% of each run, Pallas kernels for 1% -> 1%
where the time goes in v7:
time: 549 us; the launch traced here: 541 us
  waiting for transfers between devices  347 us (63%)
  blocking collectives  65.2 us (12%)
  starting transfers between devices  63.5 us (12%)
  Pallas kernels  26.5 us (5%)
  local copies, waits for them, and re-layouts  15.9 us (3%)
  between operations  14.7 us (3%)
  other arithmetic  6.79 us (1%)
    ppermute x15, waiting for transfers between devices, on_device(): part = lax.ppermute(part, ('z', 'c', 'x'), next_plane(layer))  185 us
    ppermute x4, waiting for transfers between devices, on_device(): rows = rows + lax.ppermute(rows, 'z', route)  41.4 us
    ppermute x1, waiting for transfers between devices, on_device(): across_rest = lax.ppermute(other_rest, 'x', INTER)  38.3 us
    all_gather x16, blocking collectives, on_device(): part = added(lax.all_gather(part, 'c', axis=0, tiled=False))  33.7 us
    all_gather x15, blocking collectives, on_device(): pair = lax.all_gather(part, 'c', axis=0, tiled=False)  31.5 us
    ppermute x10, starting transfers between devices, moved(): return lax.ppermute(block, axis, route)  31.4 us
    ppermute x1, waiting for transfers between devices, on_device(): beside = lax.ppermute(own, 'x', INTRA)  29 us
    ppermute x10, waiting for transfers between devices, moved(): return lax.ppermute(block, axis, route)  26.5 us
  transfers between devices with their start and end apart: 38, of which 13 were waited for; matrix products, arithmetic and copies ran while one was open for 2% of the time, Pallas kernels for 1%

profile of v7, /device:TPU:448, one launch (start us, length us, event | category | flops | bytes accessed | tf_op | source)
XLA Modules:
  0.0 540.7 jit_solution(9766518281438790796)
XLA Ops:
  10.6 4.7 collective-permute-start.8
  15.2 4.9 collective-permute-start.5
  20.2 1.9 collective-permute-start.4
  22.1 2.5 collective-permute-start.1
  24.6 2.1 collective-permute-start
  26.7 3.9 collective-permute-done.8.refs_5_
  30.7 2.0 collective-permute-start.7
  32.6 3.9 collective-permute-done.5
  36.6 5.6 %collective-permute-start.2 = (bf16[200,1600]{1,0:T(8,128)(2,1)S(1)}, bf16[200,1600]{1,0:T(8,128)(2,1)}, u32[]{:S(2)}, u32[]{:S(2)}) collective-permute-start(bf16[200,1600]{1,0:T(8,128)(2,1)S(1)} %get-tuple-element.31.refs_3_), channel_id=1, source_target_pairs={{0,12},{4,0},{8,4},{12,8},{1,13},{5,1},{9,5},{13,9},{2,14},{6,2},{... | collective-permute-start | bytes 1920008 | tf_op jit(solution)/shard_map/ppermute | solution.py:18
  42.2 2.7 collective-permute-done.4
  44.9 1.9 collective-permute-start.6
  46.8 10.7 %collective-permute-done.1 = bf16[200,1600]{1,0:T(8,128)(2,1)} collective-permute-done((bf16[200,1600]{1,0:T(8,128)(2,1)S(1)}, bf16[200,1600]{1,0:T(8,128)(2,1)}, u32[]{:S(2)}, u32[]{:S(2)}) %collective-permute-start.1) | collective-permute-done | bytes 640032 | tf_op jit(solution)/shard_map/ppermute | solution.py:18
  57.5 1.9 collective-permute-start.3
  59.5 29.0 %collective-permute-done.7.refs_4_ = bf16[200,1600]{1,0:T(8,128)(2,1)S(1)} collective-permute-done((bf16[200,1600]{1,0:T(8,128)(2,1)S(1)}, bf16[200,1600]{1,0:T(8,128)(2,1)S(1)}, u32[]{:S(2)}, u32[]{:S(2)}) %collective-permute-start.7) | collective-permute-done | bytes 640032 | tf_op jit(solution)/shard_map/ppermute | solution.py:198
  90.3 3.5 pad_maximum_fusion.1
  94.3 3.2 collective-permute-start.11
  97.6 1.9 collective-permute-start.14
  99.5 3.7 collective-permute-start.9
  103.2 2.2 collective-permute-start.16
  105.4 38.3 %collective-permute-done.14.refs_8_ = bf16[600,1600]{1,0:T(8,128)(2,1)} collective-permute-done((bf16[600,1600]{1,0:T(8,128)(2,1)S(1)}, bf16[600,1600]{1,0:T(8,128)(2,1)}, u32[]{:S(2)}, u32[]{:S(2)}) %collective-permute-start.14) | collective-permute-done | bytes 1920032 | tf_op jit(solution)/shard_map/ppermute | solution.py:210
  143.7 1.9 collective-permute-start.15
  145.6 6.9 %collective-permute-done.11.refs_2_ = bf16[400,3200]{1,0:T(8,128)(2,1)S(1)} collective-permute-done((bf16[400,3200]{1,0:T(8,128)(2,1)S(1)}, bf16[400,3200]{1,0:T(8,128)(2,1)S(1)}, u32[]{:S(2)}, u32[]{:S(2)}) %collective-permute-start.11) | collective-permute-done | bytes 2560032 | tf_op jit(solution)/shard_map/ppermute | solution.py:18
  153.8 3.4 collective-permute-start.12
  160.2 2.4 collective-permute-start.10
  162.8 1.9 collective-permute-start.13
  164.8 2.7 slice.30
  176.3 5.3 put_pieces.2
  181.6 23.4 %collective-permute-done.13.refs_2_ = bf16[200,1600]{1,0:T(8,128)(2,1)S(1)} collective-permute-done((bf16[200,1600]{1,0:T(8,128)(2,1)}, bf16[200,1600]{1,0:T(8,128)(2,1)S(1)}, u32[]{:S(2)}, u32[]{:S(2)}) %collective-permute-start.13) | collective-permute-done | bytes 640032 | tf_op jit(solution)/shard_map/ppermute | solution.py:200
  204.9 3.0 put_pieces.3
  208.5 2.1 all-gather.1
  211.3 2.1 all-gather.2
  214.2 2.1 all-gather.3
  217.1 2.1 all-gather.4
  219.7 2.1 all-gather.5
  222.6 2.1 all-gather.6
  225.2 2.1 all-gather.7
  228.1 2.1 all-gather.8
  231.2 2.1 all-gather.9
  234.0 2.1 all-gather.10
  236.7 2.1 all-gather.11
  239.5 2.1 all-gather.12
  242.2 2.1 all-gather.13
  245.0 2.1 all-gather.14
  247.9 2.1 all-gather.15
  250.7 2.1 all-gather.16
  253.4 2.1 all-gather.17
  256.2 2.1 all-gather.18
  258.9 2.1 all-gather.19
  261.8 2.1 all-gather.20
  264.6 2.1 all-gather.21
  267.5 2.1 all-gather.22
  270.2 2.1 all-gather.23
  273.0 2.1 all-gather.24
  275.7 2.1 all-gather.25
  278.5 2.1 all-gather.26
  281.4 2.1 all-gather.27
  284.9 179.9 %collective-permute-done.30 = bf16[32,3200]{1,0:T(8,128)(2,1)S(1)} collective-permute-done((bf16[32,3200]{1,0:T(8,128)(2,1)S(1)}, bf16[32,3200]{1,0:T(8,128)(2,1)S(1)}, u32[]{:S(2)}, u32[]{:S(2)}) %collective-permute-start.30) | collective-permute-done | bytes 204832 | tf_op jit(solution)/shard_map/ppermute | solution.py:258
  464.8 2.1 all-gather.28
  466.8 6.7 %quarter_layer.30 = bf16[32,3200]{1,0:T(8,128)(2,1)S(1)} custom-call(s32[1]{0:T(128)} %constant.65.clone.1.tick_ref, s32[3]{0:T(128)S(1)} %pad_add_fusion.state_ref, bf16[2,32,3200]{2,1,0:T(8,128)(2,1)S(1)} %bitcast.71, bf16[4,400,3200]{2,1,0:T(8,128)(2,1)S(1)} %get-tuple-element.47.refs_0_, bf16[4,200,1600]{2,1,0:T(8,128)(2,1)S(1)} %get-tuple-element.48.refs_1_, ...), custom_call_target="tpu_custom_call" | custom-call | flops 655360000 | bytes 409600 | tf_op jit(solution)/shard_map/quarter_layer/pallas_call | solution.py:109
  473.6 2.1 all-gather.29
  477.1 4.9 collective-permute-done.31
  482.0 2.1 all-gather.30
  484.6 2.2 all-gather.31
  491.1 41.4 %collective-permute-done.36 = bf16[16,3200]{1,0:T(8,128)(2,1)S(1)} collective-permute-done((bf16[16,3200]{1,0:T(8,128)(2,1)S(1)}, bf16[16,3200]{1,0:T(8,128)(2,1)S(1)}, u32[]{:S(2)}, u32[]{:S(2)}) %collective-permute-start.36) | collective-permute-done | bytes 102432 | tf_op jit(solution)/shard_map/ppermute | solution.py:273
  (125 shorter events, 46.5 us)
Async XLA Ops:
  6.5 158.2 %all-gather.34.cloned.1.call-start = ((), (), s32[]{:S(2)}) async-start(), calls=%async_computation | async-start | bytes 3969024 | tf_op jit(solution)/shard_map/all_gather | solution.py:225
  8.3 1.3 copy-start.4
  10.5 83.3 %copy-start.5 = (bf16[200,1600]{1,0:T(8,128)(2,1)}, bf16[200,1600]{1,0:T(8,128)(2,1)S(1)}, u32[]{:S(2)}) copy-start(bf16[200,1600]{1,0:T(8,128)(2,1)S(1)} %get-tuple-element.31.refs_3_) | copy-start | bytes 1920004
  10.6 20.1 %collective-permute-start.8 = (bf16[200,1600]{1,0:T(8,128)(2,1)S(1)}, bf16[200,1600]{1,0:T(8,128)(2,1)}, u32[]{:S(2)}, u32[]{:S(2)}) collective-permute-start(bf16[200,1600]{1,0:T(8,128)(2,1)S(1)} %get-tuple-element.32), channel_id=1, source_target_pairs={{0,3},{3,0},{1,2},{2,1},{4,7},{7,4},{5,6},{6,5},{8,11},{11,8},{9,1... | collective-permute-start | bytes 1920008 | tf_op jit(solution)/shard_map/ppermute | solution.py:199
  15.2 21.3 %collective-permute-start.5 = (bf16[200,1600]{1,0:T(8,128)(2,1)S(1)}, bf16[200,1600]{1,0:T(8,128)(2,1)S(1)}, u32[]{:S(2)}, u32[]{:S(2)}) collective-permute-start(bf16[200,1600]{1,0:T(8,128)(2,1)S(1)} %get-tuple-element.32), channel_id=1, source_target_pairs={{0,12},{4,0},{8,4},{12,8},{1,13},{5,1},{9,5},{13,9},{2,14},{6,2},{... | collective-permute-start | bytes 1920008 | tf_op jit(solution)/shard_map/ppermute | solution.py:18
  20.2 24.7 %collective-permute-start.4 = (bf16[200,1600]{1,0:T(8,128)(2,1)S(1)}, bf16[200,1600]{1,0:T(8,128)(2,1)S(1)}, u32[]{:S(2)}, u32[]{:S(2)}) collective-permute-start(bf16[200,1600]{1,0:T(8,128)(2,1)S(1)} %get-tuple-element.32), channel_id=1, source_target_pairs={{0,4},{4,8},{8,12},{12,0},{1,5},{5,9},{9,13},{13,1},{2,6},{6,10},{... | collective-permute-start | bytes 1920008 | tf_op jit(solution)/shard_map/ppermute | solution.py:18
  22.1 35.4 %collective-permute-start.1 = (bf16[200,1600]{1,0:T(8,128)(2,1)S(1)}, bf16[200,1600]{1,0:T(8,128)(2,1)}, u32[]{:S(2)}, u32[]{:S(2)}) collective-permute-start(bf16[200,1600]{1,0:T(8,128)(2,1)S(1)} %get-tuple-element.31.refs_3_), channel_id=1, source_target_pairs={{0,4},{4,8},{8,12},{12,0},{1,5},{5,9},{9,13},{13,1},{2,6},{6,10},{... | collective-permute-start | bytes 1920008 | tf_op jit(solution)/shard_map/ppermute | solution.py:18
  24.6 69.2 %collective-permute-start = (bf16[200,3200]{1,0:T(8,128)(2,1)}, bf16[200,3200]{1,0:T(8,128)(2,1)S(1)}, u32[]{:S(2)}, u32[]{:S(2)}) collective-permute-start(bf16[200,3200]{1,0:T(8,128)(2,1)} %bitcast.90), channel_id=1, source_target_pairs={{0,1},{1,0},{2,3},{3,2},{4,5},{5,4},{6,7},{7,6},{8,9},{9,8},{10,11... | collective-permute-start | bytes 3840008 | tf_op jit(solution)/shard_map/ppermute | solution.py:196
  30.7 57.8 %collective-permute-start.7 = (bf16[200,1600]{1,0:T(8,128)(2,1)S(1)}, bf16[200,1600]{1,0:T(8,128)(2,1)S(1)}, u32[]{:S(2)}, u32[]{:S(2)}) collective-permute-start(bf16[200,1600]{1,0:T(8,128)(2,1)S(1)} %get-tuple-element.31.refs_3_), channel_id=1, source_target_pairs={{0,1},{1,0},{2,3},{3,2},{4,5},{5,4},{6,7},{7,6},{8,9},{9,8},{10,11... | collective-permute-start | bytes 1920008 | tf_op jit(solution)/shard_map/ppermute | solution.py:198
  36.6 51.9 %collective-permute-start.2 = (bf16[200,1600]{1,0:T(8,128)(2,1)S(1)}, bf16[200,1600]{1,0:T(8,128)(2,1)}, u32[]{:S(2)}, u32[]{:S(2)}) collective-permute-start(bf16[200,1600]{1,0:T(8,128)(2,1)S(1)} %get-tuple-element.31.refs_3_), channel_id=1, source_target_pairs={{0,12},{4,0},{8,4},{12,8},{1,13},{5,1},{9,5},{13,9},{2,14},{6,2},{... | collective-permute-start | bytes 1920008 | tf_op jit(solution)/shard_map/ppermute | solution.py:18
  44.9 12.6 %copy-start.11 = (bf16[200,1600]{1,0:T(8,128)(2,1)}, bf16[200,1600]{1,0:T(8,128)(2,1)S(1)}, u32[]{:S(2)}) copy-start(bf16[200,1600]{1,0:T(8,128)(2,1)S(1)} %collective-permute-done.4) | copy-start | bytes 1920004
  44.9 43.5 %collective-permute-start.6 = (bf16[200,1600]{1,0:T(8,128)(2,1)S(1)}, bf16[200,1600]{1,0:T(8,128)(2,1)}, u32[]{:S(2)}, u32[]{:S(2)}) collective-permute-start(bf16[200,1600]{1,0:T(8,128)(2,1)S(1)} %collective-permute-done.5), channel_id=1, source_target_pairs={{0,12},{4,0},{8,4},{12,8},{1,13},{5,1},{9,5},{13,9},{2,14},{6,2},{... | collective-permute-start | bytes 1920008 | tf_op jit(solution)/shard_map/ppermute | solution.py:18
  57.5 32.8 %collective-permute-start.3 = (bf16[200,1600]{1,0:T(8,128)(2,1)}, bf16[200,1600]{1,0:T(8,128)(2,1)}, u32[]{:S(2)}, u32[]{:S(2)}) collective-permute-start(bf16[200,1600]{1,0:T(8,128)(2,1)} %collective-permute-done.1), channel_id=1, source_target_pairs={{0,4},{4,8},{8,12},{12,0},{1,5},{5,9},{9,13},{13,1},{2,6},{6,10},{... | collective-permute-start | bytes 1920008 | tf_op jit(solution)/shard_map/ppermute | solution.py:18
  59.4 34.4 %copy-start.10 = (bf16[1,200,3200]{2,1,0:T(8,128)(2,1)S(1)}, bf16[1,200,3200]{2,1,0:T(8,128)(2,1)}, u32[]{:S(2)}) copy-start(bf16[1,200,3200]{2,1,0:T(8,128)(2,1)} %param.5) | copy-start | bytes 3840004
  88.5 5.4 copy-start.7
  94.3 58.2 %collective-permute-start.11 = (bf16[400,3200]{1,0:T(8,128)(2,1)S(1)}, bf16[400,3200]{1,0:T(8,128)(2,1)S(1)}, u32[]{:S(2)}, u32[]{:S(2)}) collective-permute-start(bf16[400,3200]{1,0:T(8,128)(2,1)S(1)} %pad_maximum_fusion.refs_0_), channel_id=1, source_target_pairs={{0,12},{4,0},{8,4},{12,8},{1,13},{5,1},{9,5},{13,9},{2,14},{6,2},{... | collective-permute-start | bytes 7680008 | tf_op jit(solution)/shard_map/ppermute | solution.py:18
  97.6 46.1 %collective-permute-start.14 = (bf16[600,1600]{1,0:T(8,128)(2,1)S(1)}, bf16[600,1600]{1,0:T(8,128)(2,1)}, u32[]{:S(2)}, u32[]{:S(2)}) collective-permute-start(bf16[600,1600]{1,0:T(8,128)(2,1)S(1)} %get-tuple-element.40), channel_id=1, source_target_pairs={{0,3},{3,0},{1,2},{2,1},{4,7},{7,4},{5,6},{6,5},{8,11},{11,8},{9,1... | collective-permute-start | bytes 5760008 | tf_op jit(solution)/shard_map/ppermute | solution.py:210
  99.5 58.1 %collective-permute-start.9 = (bf16[400,3200]{1,0:T(8,128)(2,1)S(1)}, bf16[400,3200]{1,0:T(8,128)(2,1)S(1)}, u32[]{:S(2)}, u32[]{:S(2)}) collective-permute-start(bf16[400,3200]{1,0:T(8,128)(2,1)S(1)} %pad_maximum_fusion.refs_0_), channel_id=1, source_target_pairs={{0,4},{4,8},{8,12},{12,0},{1,5},{5,9},{9,13},{13,1},{2,6},{6,10},{... | collective-permute-start | bytes 7680008 | tf_op jit(solution)/shard_map/ppermute | solution.py:18
  103.2 67.5 %collective-permute-start.16 = (bf16[600,1600]{1,0:T(8,128)(2,1)}, bf16[600,1600]{1,0:T(8,128)(2,1)}, u32[]{:S(2)}, u32[]{:S(2)}) collective-permute-start(bf16[600,1600]{1,0:T(8,128)(2,1)} %get-tuple-element.43.refs_6_), channel_id=1, source_target_pairs={{0,1},{1,0},{2,3},{3,2},{4,5},{5,4},{6,7},{7,6},{8,9},{9,8},{10,11... | collective-permute-start | bytes 5760008 | tf_op jit(solution)/shard_map/ppermute | solution.py:209
  143.7 61.3 %collective-permute-start.15 = (bf16[600,1600]{1,0:T(8,128)(2,1)}, bf16[600,1600]{1,0:T(8,128)(2,1)}, u32[]{:S(2)}, u32[]{:S(2)}) collective-permute-start(bf16[600,1600]{1,0:T(8,128)(2,1)} %collective-permute-done.14.refs_8_), channel_id=1, source_target_pairs={{0,1},{1,0},{2,3},{3,2},{4,5},{5,4},{6,7},{7,6},{8,9},{9,8},{10,11... | collective-permute-start | bytes 5760008 | tf_op jit(solution)/shard_map/ppermute | solution.py:211
  152.5 6.2 %copy-start = (bf16[400,3200]{1,0:T(8,128)(2,1)}, bf16[400,3200]{1,0:T(8,128)(2,1)S(1)}, u32[]{:S(2)}) copy-start(bf16[400,3200]{1,0:T(8,128)(2,1)S(1)} %collective-permute-done.11.refs_2_) | copy-start | bytes 7680004
  153.8 51.1 %collective-permute-start.12 = (bf16[400,1664]{1,0:T(8,128)(2,1)}, bf16[400,1664]{1,0:T(8,128)(2,1)}, u32[]{:S(2)}, u32[]{:S(2)}) collective-permute-start(bf16[400,1664]{1,0:T(8,128)(2,1)} %slice.32), channel_id=1, source_target_pairs={{0,12},{4,0},{8,4},{12,8},{1,13},{5,1},{9,5},{13,9},{2,14},{6,2},{... | collective-permute-start | bytes 3993608 | tf_op jit(solution)/shard_map/ppermute | solution.py:18
  158.7 1.5 copy-start.2
  160.2 44.7 %collective-permute-start.10 = (bf16[400,1536]{1,0:T(8,128)(2,1)}, bf16[400,1536]{1,0:T(8,128)(2,1)}, u32[]{:S(2)}, u32[]{:S(2)}) collective-permute-start(bf16[400,1536]{1,0:T(8,128)(2,1)} %slice.31), channel_id=1, source_target_pairs={{0,4},{4,8},{8,12},{12,0},{1,5},{5,9},{9,13},{13,1},{2,6},{6,10},{... | collective-permute-start | bytes 3686408 | tf_op jit(solution)/shard_map/ppermute | solution.py:18
  162.8 42.1 %collective-permute-start.13 = (bf16[200,1600]{1,0:T(8,128)(2,1)}, bf16[200,1600]{1,0:T(8,128)(2,1)S(1)}, u32[]{:S(2)}, u32[]{:S(2)}) collective-permute-start(bf16[200,1600]{1,0:T(8,128)(2,1)} %collective-permute-done.8.refs_5_), channel_id=1, source_target_pairs={{0,1},{1,0},{2,3},{3,2},{4,5},{5,4},{6,7},{7,6},{8,9},{9,8},{10,11... | collective-permute-start | bytes 1920008 | tf_op jit(solution)/shard_map/ppermute | solution.py:200
  170.6 1.7 copy-start.1
  172.3 1.7 copy-start.3
  174.1 1.1 copy-start.6
  175.2 1.1 copy-start.8
  210.6 0.7 collective-permute-start.17
  216.4 0.7 collective-permute-start.18
  221.9 0.7 collective-permute-start.19
  227.4 0.7 collective-permute-start.20
  233.3 0.7 collective-permute-start.21
  238.8 0.7 collective-permute-start.22
  244.4 0.7 collective-permute-start.23
  250.0 0.7 collective-permute-start.24
  255.6 0.7 collective-permute-start.25
  261.1 0.7 collective-permute-start.26
  266.8 0.7 collective-permute-start.27
  272.3 0.7 collective-permute-start.28
  277.8 0.7 collective-permute-start.29
  283.6 181.2 %collective-permute-start.30 = (bf16[32,3200]{1,0:T(8,128)(2,1)S(1)}, bf16[32,3200]{1,0:T(8,128)(2,1)S(1)}, u32[]{:S(2)}, u32[]{:S(2)}) collective-permute-start(bf16[32,3200]{1,0:T(8,128)(2,1)S(1)} %add_pair.29), channel_id=1, source_target_pairs={{416,448},{432,451},{419,464},{435,467},{417,449},{433,450},{418,4... | collective-permute-start | bytes 614408 | tf_op jit(solution)/shard_map/ppermute | solution.py:258
  475.8 6.2 %collective-permute-start.31 = (bf16[32,3200]{1,0:T(8,128)(2,1)S(1)}, bf16[32,3200]{1,0:T(8,128)(2,1)S(1)}, u32[]{:S(2)}, u32[]{:S(2)}) collective-permute-start(bf16[32,3200]{1,0:T(8,128)(2,1)S(1)} %add_pair.30), channel_id=1, source_target_pairs={{448,480},{464,483},{451,496},{467,499},{449,481},{465,482},{450,4... | collective-permute-start | bytes 614408 | tf_op jit(solution)/shard_map/ppermute | solution.py:258
  484.6 47.9 %copy-start.9 = (bf16[16,200,256]{2,1,0:T(8,128)(2,1)S(1)}, bf16[16,200,256]{2,1,0:T(8,128)(2,1)}, u32[]{:S(2)}) copy-start(bf16[16,200,256]{2,1,0:T(8,128)(2,1)} %slice.30) | copy-start | bytes 4915204
  486.9 0.7 collective-permute-start.32
  487.7 0.7 collective-permute-start.33
  488.4 0.7 collective-permute-start.34
  489.1 0.7 collective-permute-start.35
  489.8 42.7 %collective-permute-start.36 = (bf16[16,3200]{1,0:T(8,128)(2,1)S(1)}, bf16[16,3200]{1,0:T(8,128)(2,1)S(1)}, u32[]{:S(2)}, u32[]{:S(2)}) collective-permute-start(bf16[16,3200]{1,0:T(8,128)(2,1)S(1)} %add.54), channel_id=1, source_target_pairs={{480,0},{224,256},{96,128},{352,384},{32,64},{288,320},{160,192},{... | collective-permute-start | bytes 307208 | tf_op jit(solution)/shard_map/ppermute | solution.py:273
Sparse Core Ops, SparseCore 0:
  10.4 79.6 all-gather.33

commit v8 on v7

--- a/solution.py
+++ b/solution.py
@@ -193,19 +193,21 @@
     low = (x < 2).astype(jnp.int32)
 
     own, other = own_and_other(low, w_out[0])
-    mate = lax.ppermute(w_in[0], "x", INTRA)
     own_ring, other_ring = ring(own, other, "y")
     beside = lax.ppermute(own, "x", INTRA)
     across = lax.ppermute(other, "x", INTER)
     corner = lax.ppermute(across, "x", INTRA)
+    block, beside = lax.optimization_barrier((w_in[0], beside))
+    mate = lax.ppermute(block, "x", INTRA)
     held = (own_ring, other_ring, beside, across)
     own_ring, other_ring, beside, across = lax.optimization_barrier(held)
     own_rest = jnp.concatenate(own_ring, axis=0)
     other_rest = jnp.concatenate(other_ring, axis=0)
 
-    near = by_halves((lax.rem(x, 2) == 0).astype(jnp.int32), w_in[0], mate)
+    near = by_halves((lax.rem(x, 2) == 0).astype(jnp.int32), block, mate)
     held = (near, own_rest, other_rest)
     near, own_rest, other_rest = lax.optimization_barrier(held)
+    near, corner = lax.optimization_barrier((near, corner))
     beside_rest = lax.ppermute(own_rest, "x", INTRA)
     across_rest = lax.ppermute(other_rest, "x", INTER)
     corner_rest = lax.ppermute(across_rest, "x", INTRA)

time: 549 us -> 546 us (level)
  waiting for transfers between devices: 347 us -> 334 us
  starting transfers between devices: 63.5 us -> 71 us
    ppermute x10, waiting for transfers between devices: 26.5 us -> 55.6 us  [moved(): return lax.ppermute(block, axis, route)]
    ppermute x1, waiting for transfers between devices: 29 us -> 4.31 us  [on_device(): beside = lax.ppermute(own, 'x', INTRA)]
    ppermute x1, waiting for transfers between devices: 23.4 us -> 0.01 us  [on_device(): corner = lax.ppermute(across, 'x', INTRA)]
    ppermute x15, waiting for transfers between devices: 185 us -> 195 us  [on_device(): part = lax.ppermute(part, ('z', 'c', 'x'), next_plane(layer))]
where the time goes in v8:
time: 546 us; the launch traced here: 537 us
  waiting for transfers between devices  334 us (61%)
  starting transfers between devices  71 us (13%)
  blocking collectives  66.4 us (12%)
  Pallas kernels  26.5 us (5%)
  local copies, waits for them, and re-layouts  16.7 us (3%)
  between operations  14.7 us (3%)
  other arithmetic  7.57 us (1%)
    ppermute x15, waiting for transfers between devices, on_device(): part = lax.ppermute(part, ('z', 'c', 'x'), next_plane(layer))  195 us
    ppermute x10, waiting for transfers between devices, moved(): return lax.ppermute(block, axis, route)  55.6 us
    ppermute x4, waiting for transfers between devices, on_device(): rows = rows + lax.ppermute(rows, 'z', route)  39.7 us
    ppermute x1, waiting for transfers between devices, on_device(): across_rest = lax.ppermute(other_rest, 'x', INTER)  39.5 us
    ppermute x10, starting transfers between devices, moved(): return lax.ppermute(block, axis, route)  34.9 us
    all_gather x16, blocking collectives, on_device(): part = added(lax.all_gather(part, 'c', axis=0, tiled=False))  33.7 us
    all_gather x15, blocking collectives, on_device(): pair = lax.all_gather(part, 'c', axis=0, tiled=False)  32.7 us
    pallas_call x16, Pallas kernels, apply_quarter(): pl.pallas_call(quarter_layer, out_shape=jax.ShapeDtypeStruct((row_count,...  16.4 us
  transfers between devices with their start and end apart: 38, of which 13 were waited for; matrix products, arithmetic and copies ran while one was open for 2% of the time, Pallas kernels for 1%

profile of v8, /device:TPU:448, one launch (start us, length us, event | category | flops | bytes accessed | tf_op | source)
XLA Modules:
  0.0 537.4 jit_solution(6691318365895452319)
XLA Ops:
  10.6 3.4 collective-permute-start
  14.0 4.0 collective-permute-start.8
  18.0 4.9 collective-permute-start.6
  22.9 1.9 collective-permute-start.2
  24.8 4.3 collective-permute-done.refs_4_
  30.0 3.4 collective-permute-start.1
  33.4 3.5 collective-permute-start.5
  37.0 3.9 collective-permute-start.3
  40.9 5.6 %collective-permute-start.7 = (bf16[200,1600]{1,0:T(8,128)(2,1)S(1)}, bf16[200,1600]{1,0:T(8,128)(2,1)}, u32[]{:S(2)}, u32[]{:S(2)}) collective-permute-start(bf16[200,1600]{1,0:T(8,128)(2,1)S(1)} %collective-permute-done.6), channel_id=1, source_target_pairs={{0,12},{4,0},{8,4},{12,8},{1,13},{5,1},{9,5},{13,9},{2,14},{6,2},{... | collective-permute-start | bytes 1920008 | tf_op jit(solution)/shard_map/ppermute | solution.py:18
  47.7 1.9 collective-permute-start.4
  49.6 13.3 %collective-permute-done.5 = bf16[200,1600]{1,0:T(8,128)(2,1)S(1)} collective-permute-done((bf16[200,1600]{1,0:T(8,128)(2,1)S(1)}, bf16[200,1600]{1,0:T(8,128)(2,1)S(1)}, u32[]{:S(2)}, u32[]{:S(2)}) %collective-permute-start.5) | collective-permute-done | bytes 640032 | tf_op jit(solution)/shard_map/ppermute | solution.py:18
  62.9 1.9 collective-permute-start.9
  64.8 16.8 %collective-permute-done.7 = bf16[200,1600]{1,0:T(8,128)(2,1)} collective-permute-done((bf16[200,1600]{1,0:T(8,128)(2,1)S(1)}, bf16[200,1600]{1,0:T(8,128)(2,1)}, u32[]{:S(2)}, u32[]{:S(2)}) %collective-permute-start.7) | collective-permute-done | bytes 640032 | tf_op jit(solution)/shard_map/ppermute | solution.py:18
  81.6 7.7 %collective-permute-done.4 = bf16[200,1600]{1,0:T(8,128)(2,1)} collective-permute-done((bf16[200,1600]{1,0:T(8,128)(2,1)S(1)}, bf16[200,1600]{1,0:T(8,128)(2,1)}, u32[]{:S(2)}, u32[]{:S(2)}) %collective-permute-start.4) | collective-permute-done | bytes 640032 | tf_op jit(solution)/shard_map/ppermute | solution.py:18
  89.3 3.1 pad_maximum_fusion.1
  94.0 3.7 collective-permute-start.12
  97.7 3.8 collective-permute-start.14
  101.5 1.9 collective-permute-start.10
  103.4 2.4 collective-permute-start.16
  105.8 39.5 %collective-permute-done.14.refs_8_ = bf16[600,1600]{1,0:T(8,128)(2,1)} collective-permute-done((bf16[600,1600]{1,0:T(8,128)(2,1)S(1)}, bf16[600,1600]{1,0:T(8,128)(2,1)}, u32[]{:S(2)}, u32[]{:S(2)}) %collective-permute-start.14) | collective-permute-done | bytes 1920032 | tf_op jit(solution)/shard_map/ppermute | solution.py:212
  145.3 1.9 collective-permute-start.15
  147.2 4.7 collective-permute-done.12.refs_2_
  153.3 5.6 %collective-permute-start.13 = (bf16[400,1664]{1,0:T(8,128)(2,1)}, bf16[400,1664]{1,0:T(8,128)(2,1)}, u32[]{:S(2)}, u32[]{:S(2)}) collective-permute-start(bf16[400,1664]{1,0:T(8,128)(2,1)} %slice.32), channel_id=1, source_target_pairs={{0,12},{4,0},{8,4},{12,8},{1,13},{5,1},{9,5},{13,9},{2,14},{6,2},{... | collective-permute-start | bytes 3993608 | tf_op jit(solution)/shard_map/ppermute | solution.py:18
  162.8 1.9 collective-permute-start.11
  165.0 2.7 slice.30
  172.5 1.7 copy-done.3
  176.4 5.3 put_pieces.2
  181.7 10.6 %collective-permute-done.11.refs_0_ = bf16[400,1536]{1,0:T(8,128)(2,1)} collective-permute-done((bf16[400,1536]{1,0:T(8,128)(2,1)}, bf16[400,1536]{1,0:T(8,128)(2,1)}, u32[]{:S(2)}, u32[]{:S(2)}) %collective-permute-start.11) | collective-permute-done | bytes 1228832 | tf_op jit(solution)/shard_map/ppermute | solution.py:18
  192.4 3.0 put_pieces.3
  195.9 2.1 all-gather.1
  198.8 2.1 all-gather.2
  201.6 2.1 all-gather.3
  204.5 2.1 all-gather.4
  207.2 2.1 all-gather.5
  210.0 2.1 all-gather.6
  212.7 2.1 all-gather.7
  215.5 2.1 all-gather.8
  218.6 2.1 all-gather.9
  221.4 2.1 all-gather.10
  224.1 2.1 all-gather.11
  227.0 2.1 all-gather.12
  229.6 2.1 all-gather.13
  232.5 2.1 all-gather.14
  235.3 2.1 all-gather.15
  238.2 2.1 all-gather.16
  240.8 2.1 all-gather.17
  243.7 2.1 all-gather.18
  246.3 2.1 all-gather.19
  249.2 2.1 all-gather.20
  252.1 2.1 all-gather.21
  254.9 2.1 all-gather.22
  257.6 2.1 all-gather.23
  260.4 2.1 all-gather.24
  263.1 2.1 all-gather.25
  265.9 2.1 all-gather.26
  268.9 2.1 all-gather.27
  272.3 189.4 %collective-permute-done.30 = bf16[32,3200]{1,0:T(8,128)(2,1)S(1)} collective-permute-done((bf16[32,3200]{1,0:T(8,128)(2,1)S(1)}, bf16[32,3200]{1,0:T(8,128)(2,1)S(1)}, u32[]{:S(2)}, u32[]{:S(2)}) %collective-permute-start.30) | collective-permute-done | bytes 204832 | tf_op jit(solution)/shard_map/ppermute | solution.py:260
  461.7 3.3 all-gather.28
  465.0 6.7 %quarter_layer.30 = bf16[32,3200]{1,0:T(8,128)(2,1)S(1)} custom-call(s32[1]{0:T(128)} %constant.65.clone.1.tick_ref, s32[3]{0:T(128)S(1)} %pad_add_fusion.state_ref, bf16[2,32,3200]{2,1,0:T(8,128)(2,1)S(1)} %bitcast.69, bf16[4,400,3200]{2,1,0:T(8,128)(2,1)S(1)} %get-tuple-element.55.refs_0_, bf16[4,200,1600]{2,1,0:T(8,128)(2,1)S(1)} %get-tuple-element.56.refs_1_, ...), custom_call_target="tpu_custom_call" | custom-call | flops 655360000 | bytes 409600 | tf_op jit(solution)/shard_map/quarter_layer/pallas_call | solution.py:109
  471.8 2.1 all-gather.29
  475.2 5.1 collective-permute-done.31
  480.4 2.1 all-gather.30
  483.0 2.2 all-gather.31
  489.6 39.7 %collective-permute-done.36 = bf16[16,3200]{1,0:T(8,128)(2,1)S(1)} collective-permute-done((bf16[16,3200]{1,0:T(8,128)(2,1)S(1)}, bf16[16,3200]{1,0:T(8,128)(2,1)S(1)}, u32[]{:S(2)}, u32[]{:S(2)}) %collective-permute-start.36) | collective-permute-done | bytes 102432 | tf_op jit(solution)/shard_map/ppermute | solution.py:275
  (123 shorter events, 47.1 us)
Async XLA Ops:
  6.5 158.4 %all-gather.34.cloned.1.call-start = ((), (), s32[]{:S(2)}) async-start(), calls=%async_computation | async-start | bytes 3969024 | tf_op jit(solution)/shard_map/all_gather | solution.py:227
  8.3 1.3 copy-start.4
  10.5 81.8 %copy-start.5 = (bf16[200,1600]{1,0:T(8,128)(2,1)}, bf16[200,1600]{1,0:T(8,128)(2,1)S(1)}, u32[]{:S(2)}) copy-start(bf16[200,1600]{1,0:T(8,128)(2,1)S(1)} %get-tuple-element.35.refs_3_) | copy-start | bytes 1920004
  10.6 18.6 %collective-permute-start = (bf16[200,1600]{1,0:T(8,128)(2,1)S(1)}, bf16[200,1600]{1,0:T(8,128)(2,1)S(1)}, u32[]{:S(2)}, u32[]{:S(2)}) collective-permute-start(bf16[200,1600]{1,0:T(8,128)(2,1)S(1)} %get-tuple-element.35.refs_3_), channel_id=1, source_target_pairs={{0,1},{1,0},{2,3},{3,2},{4,5},{5,4},{6,7},{7,6},{8,9},{9,8},{10,11... | collective-permute-start | bytes 1920008 | tf_op jit(solution)/shard_map/ppermute | solution.py:197
  14.0 23.0 %collective-permute-start.8 = (bf16[200,1600]{1,0:T(8,128)(2,1)S(1)}, bf16[200,1600]{1,0:T(8,128)(2,1)}, u32[]{:S(2)}, u32[]{:S(2)}) collective-permute-start(bf16[200,1600]{1,0:T(8,128)(2,1)S(1)} %get-tuple-element.37), channel_id=1, source_target_pairs={{0,3},{3,0},{1,2},{2,1},{4,7},{7,4},{5,6},{6,5},{8,11},{11,8},{9,1... | collective-permute-start | bytes 1920008 | tf_op jit(solution)/shard_map/ppermute | solution.py:198
  18.0 23.0 %collective-permute-start.6 = (bf16[200,1600]{1,0:T(8,128)(2,1)S(1)}, bf16[200,1600]{1,0:T(8,128)(2,1)S(1)}, u32[]{:S(2)}, u32[]{:S(2)}) collective-permute-start(bf16[200,1600]{1,0:T(8,128)(2,1)S(1)} %get-tuple-element.37), channel_id=1, source_target_pairs={{0,12},{4,0},{8,4},{12,8},{1,13},{5,1},{9,5},{13,9},{2,14},{6,2},{... | collective-permute-start | bytes 1920008 | tf_op jit(solution)/shard_map/ppermute | solution.py:18
  22.9 24.7 %collective-permute-start.2 = (bf16[200,1600]{1,0:T(8,128)(2,1)S(1)}, bf16[200,1600]{1,0:T(8,128)(2,1)S(1)}, u32[]{:S(2)}, u32[]{:S(2)}) collective-permute-start(bf16[200,1600]{1,0:T(8,128)(2,1)S(1)} %get-tuple-element.35.refs_3_), channel_id=1, source_target_pairs={{0,4},{4,8},{8,12},{12,0},{1,5},{5,9},{9,13},{13,1},{2,6},{6,10},{... | collective-permute-start | bytes 1920008 | tf_op jit(solution)/shard_map/ppermute | solution.py:18
  29.1 0.9 copy-start.7
  30.0 62.3 %collective-permute-start.1 = (bf16[200,3200]{1,0:T(8,128)(2,1)}, bf16[200,3200]{1,0:T(8,128)(2,1)}, u32[]{:S(2)}, u32[]{:S(2)}) collective-permute-start(bf16[200,3200]{1,0:T(8,128)(2,1)} %bitcast.88), channel_id=1, source_target_pairs={{0,1},{1,0},{2,3},{3,2},{4,5},{5,4},{6,7},{7,6},{8,9},{9,8},{10,11... | collective-permute-start | bytes 3840008 | tf_op jit(solution)/shard_map/ppermute | solution.py:201
  33.4 29.5 %collective-permute-start.5 = (bf16[200,1600]{1,0:T(8,128)(2,1)S(1)}, bf16[200,1600]{1,0:T(8,128)(2,1)S(1)}, u32[]{:S(2)}, u32[]{:S(2)}) collective-permute-start(bf16[200,1600]{1,0:T(8,128)(2,1)S(1)} %get-tuple-element.37), channel_id=1, source_target_pairs={{0,4},{4,8},{8,12},{12,0},{1,5},{5,9},{9,13},{13,1},{2,6},{6,10},{... | collective-permute-start | bytes 1920008 | tf_op jit(solution)/shard_map/ppermute | solution.py:18
  37.0 27.8 %collective-permute-start.3 = (bf16[200,1600]{1,0:T(8,128)(2,1)S(1)}, bf16[200,1600]{1,0:T(8,128)(2,1)}, u32[]{:S(2)}, u32[]{:S(2)}) collective-permute-start(bf16[200,1600]{1,0:T(8,128)(2,1)S(1)} %get-tuple-element.35.refs_3_), channel_id=1, source_target_pairs={{0,12},{4,0},{8,4},{12,8},{1,13},{5,1},{9,5},{13,9},{2,14},{6,2},{... | collective-permute-start | bytes 1920008 | tf_op jit(solution)/shard_map/ppermute | solution.py:18
  40.9 40.7 %collective-permute-start.7 = (bf16[200,1600]{1,0:T(8,128)(2,1)S(1)}, bf16[200,1600]{1,0:T(8,128)(2,1)}, u32[]{:S(2)}, u32[]{:S(2)}) collective-permute-start(bf16[200,1600]{1,0:T(8,128)(2,1)S(1)} %collective-permute-done.6), channel_id=1, source_target_pairs={{0,12},{4,0},{8,4},{12,8},{1,13},{5,1},{9,5},{13,9},{2,14},{6,2},{... | collective-permute-start | bytes 1920008 | tf_op jit(solution)/shard_map/ppermute | solution.py:18
  47.7 41.6 %collective-permute-start.4 = (bf16[200,1600]{1,0:T(8,128)(2,1)S(1)}, bf16[200,1600]{1,0:T(8,128)(2,1)}, u32[]{:S(2)}, u32[]{:S(2)}) collective-permute-start(bf16[200,1600]{1,0:T(8,128)(2,1)S(1)} %collective-permute-done.2), channel_id=1, source_target_pairs={{0,4},{4,8},{8,12},{12,0},{1,5},{5,9},{9,13},{13,1},{2,6},{6,10},{... | collective-permute-start | bytes 1920008 | tf_op jit(solution)/shard_map/ppermute | solution.py:18
  49.6 42.8 %copy-start.10 = (bf16[1,200,3200]{2,1,0:T(8,128)(2,1)S(1)}, bf16[1,200,3200]{2,1,0:T(8,128)(2,1)}, u32[]{:S(2)}) copy-start(bf16[1,200,3200]{2,1,0:T(8,128)(2,1)} %param.5) | copy-start | bytes 3840004
  62.9 31.1 %collective-permute-start.9 = (bf16[200,1600]{1,0:T(8,128)(2,1)}, bf16[200,1600]{1,0:T(8,128)(2,1)S(1)}, u32[]{:S(2)}, u32[]{:S(2)}) collective-permute-start(bf16[200,1600]{1,0:T(8,128)(2,1)} %collective-permute-done.8.refs_5_), channel_id=1, source_target_pairs={{0,1},{1,0},{2,3},{3,2},{4,5},{5,4},{6,7},{7,6},{8,9},{9,8},{10,11... | collective-permute-start | bytes 1920008 | tf_op jit(solution)/shard_map/ppermute | solution.py:199
  94.0 57.9 %collective-permute-start.12 = (bf16[400,3200]{1,0:T(8,128)(2,1)S(1)}, bf16[400,3200]{1,0:T(8,128)(2,1)S(1)}, u32[]{:S(2)}, u32[]{:S(2)}) collective-permute-start(bf16[400,3200]{1,0:T(8,128)(2,1)S(1)} %pad_maximum_fusion.refs_0_), channel_id=1, source_target_pairs={{0,12},{4,0},{8,4},{12,8},{1,13},{5,1},{9,5},{13,9},{2,14},{6,2},{... | collective-permute-start | bytes 7680008 | tf_op jit(solution)/shard_map/ppermute | solution.py:18
  97.7 47.6 %collective-permute-start.14 = (bf16[600,1600]{1,0:T(8,128)(2,1)S(1)}, bf16[600,1600]{1,0:T(8,128)(2,1)}, u32[]{:S(2)}, u32[]{:S(2)}) collective-permute-start(bf16[600,1600]{1,0:T(8,128)(2,1)S(1)} %get-tuple-element.48), channel_id=1, source_target_pairs={{0,3},{3,0},{1,2},{2,1},{4,7},{7,4},{5,6},{6,5},{8,11},{11,8},{9,1... | collective-permute-start | bytes 5760008 | tf_op jit(solution)/shard_map/ppermute | solution.py:212
  101.5 58.7 %collective-permute-start.10 = (bf16[400,3200]{1,0:T(8,128)(2,1)S(1)}, bf16[400,3200]{1,0:T(8,128)(2,1)S(1)}, u32[]{:S(2)}, u32[]{:S(2)}) collective-permute-start(bf16[400,3200]{1,0:T(8,128)(2,1)S(1)} %pad_maximum_fusion.refs_0_), channel_id=1, source_target_pairs={{0,4},{4,8},{8,12},{12,0},{1,5},{5,9},{9,13},{13,1},{2,6},{6,10},{... | collective-permute-start | bytes 7680008 | tf_op jit(solution)/shard_map/ppermute | solution.py:18
  103.4 67.4 %collective-permute-start.16 = (bf16[600,1600]{1,0:T(8,128)(2,1)}, bf16[600,1600]{1,0:T(8,128)(2,1)}, u32[]{:S(2)}, u32[]{:S(2)}) collective-permute-start(bf16[600,1600]{1,0:T(8,128)(2,1)} %get-tuple-element.51.refs_6_), channel_id=1, source_target_pairs={{0,1},{1,0},{2,3},{3,2},{4,5},{5,4},{6,7},{7,6},{8,9},{9,8},{10,11... | collective-permute-start | bytes 5760008 | tf_op jit(solution)/shard_map/ppermute | solution.py:211
  145.3 47.0 %collective-permute-start.15 = (bf16[600,1600]{1,0:T(8,128)(2,1)}, bf16[600,1600]{1,0:T(8,128)(2,1)}, u32[]{:S(2)}, u32[]{:S(2)}) collective-permute-start(bf16[600,1600]{1,0:T(8,128)(2,1)} %collective-permute-done.14.refs_8_), channel_id=1, source_target_pairs={{0,1},{1,0},{2,3},{3,2},{4,5},{5,4},{6,7},{7,6},{8,9},{9,8},{10,11... | collective-permute-start | bytes 5760008 | tf_op jit(solution)/shard_map/ppermute | solution.py:213
  152.0 9.3 %copy-start = (bf16[400,3200]{1,0:T(8,128)(2,1)}, bf16[400,3200]{1,0:T(8,128)(2,1)S(1)}, u32[]{:S(2)}) copy-start(bf16[400,3200]{1,0:T(8,128)(2,1)S(1)} %collective-permute-done.12.refs_2_) | copy-start | bytes 7680004
  153.3 39.1 %collective-permute-start.13 = (bf16[400,1664]{1,0:T(8,128)(2,1)}, bf16[400,1664]{1,0:T(8,128)(2,1)}, u32[]{:S(2)}, u32[]{:S(2)}) collective-permute-start(bf16[400,1664]{1,0:T(8,128)(2,1)} %slice.32), channel_id=1, source_target_pairs={{0,12},{4,0},{8,4},{12,8},{1,13},{5,1},{9,5},{13,9},{2,14},{6,2},{... | collective-permute-start | bytes 3993608 | tf_op jit(solution)/shard_map/ppermute | solution.py:18
  161.3 1.5 copy-start.2
  162.8 29.5 %collective-permute-start.11 = (bf16[400,1536]{1,0:T(8,128)(2,1)}, bf16[400,1536]{1,0:T(8,128)(2,1)}, u32[]{:S(2)}, u32[]{:S(2)}) collective-permute-start(bf16[400,1536]{1,0:T(8,128)(2,1)} %slice.31), channel_id=1, source_target_pairs={{0,4},{4,8},{8,12},{12,0},{1,5},{5,9},{9,13},{13,1},{2,6},{6,10},{... | collective-permute-start | bytes 3686408 | tf_op jit(solution)/shard_map/ppermute | solution.py:18
  170.8 1.7 copy-start.1
  172.5 1.7 copy-start.3
  174.3 1.1 copy-start.6
  175.3 1.1 copy-start.8
  198.1 0.7 collective-permute-start.17
  203.8 0.7 collective-permute-start.18
  209.3 0.7 collective-permute-start.19
  214.8 0.7 collective-permute-start.20
  220.7 0.7 collective-permute-start.21
  226.3 0.7 collective-permute-start.22
  231.8 0.7 collective-permute-start.23
  237.5 0.7 collective-permute-start.24
  243.0 0.7 collective-permute-start.25
  248.5 0.7 collective-permute-start.26
  254.2 0.7 collective-permute-start.27
  259.7 0.7 collective-permute-start.28
  265.3 0.7 collective-permute-start.29
  271.0 190.7 %collective-permute-start.30 = (bf16[32,3200]{1,0:T(8,128)(2,1)S(1)}, bf16[32,3200]{1,0:T(8,128)(2,1)S(1)}, u32[]{:S(2)}, u32[]{:S(2)}) collective-permute-start(bf16[32,3200]{1,0:T(8,128)(2,1)S(1)} %add_pair.29), channel_id=1, source_target_pairs={{416,448},{432,451},{419,464},{435,467},{417,449},{433,450},{418,4... | collective-permute-start | bytes 614408 | tf_op jit(solution)/shard_map/ppermute | solution.py:260
  473.9 6.4 %collective-permute-start.31 = (bf16[32,3200]{1,0:T(8,128)(2,1)S(1)}, bf16[32,3200]{1,0:T(8,128)(2,1)S(1)}, u32[]{:S(2)}, u32[]{:S(2)}) collective-permute-start(bf16[32,3200]{1,0:T(8,128)(2,1)S(1)} %add_pair.30), channel_id=1, source_target_pairs={{448,480},{464,483},{451,496},{467,499},{449,481},{465,482},{450,4... | collective-permute-start | bytes 614408 | tf_op jit(solution)/shard_map/ppermute | solution.py:260
  483.0 46.2 %copy-start.9 = (bf16[16,200,256]{2,1,0:T(8,128)(2,1)S(1)}, bf16[16,200,256]{2,1,0:T(8,128)(2,1)}, u32[]{:S(2)}) copy-start(bf16[16,200,256]{2,1,0:T(8,128)(2,1)} %slice.30) | copy-start | bytes 4915204
  485.3 0.7 collective-permute-start.32
  486.1 0.7 collective-permute-start.33
  486.8 0.7 collective-permute-start.34
  487.5 0.7 collective-permute-start.35
  488.3 41.0 %collective-permute-start.36 = (bf16[16,3200]{1,0:T(8,128)(2,1)S(1)}, bf16[16,3200]{1,0:T(8,128)(2,1)S(1)}, u32[]{:S(2)}, u32[]{:S(2)}) collective-permute-start(bf16[16,3200]{1,0:T(8,128)(2,1)S(1)} %add.54), channel_id=1, source_target_pairs={{480,0},{224,256},{96,128},{352,384},{32,64},{288,320},{160,192},{... | collective-permute-start | bytes 307208 | tf_op jit(solution)/shard_map/ppermute | solution.py:275
Sparse Core Ops, SparseCore 0:
  10.4 79.7 all-gather.33

commit v9 on v8

--- a/solution.py
+++ b/solution.py
@@ -263,13 +263,19 @@
     count = part.shape[0] // 2
     kept = jnp.where(low == 1, part[:count], part[count:])
     sent = jnp.where(low == 1, part[count:], part[:count])
-    last = (layers - 1) * SIDE
-    route = [(last + here, last + there) for here, there in INTER]
-    got = lax.ppermute(sent, ("z", "x"), route)
-    total = kept.astype(jnp.float32) + got.astype(jnp.float32)
-    rows = jnp.where(plane == layers - 1, total, 0.0).astype(jnp.bfloat16)
-    holders = [layers - 1]
-    step = layers // 2
+    last, half = layers - 1, layers // 2
+
+    def crossed(target):
+        route = [(last * SIDE + i, target * SIDE + j) for i, j in INTER]
+        return lax.ppermute(sent, ("z", "x"), route)
+
+    first = (last + half) % layers
+    got = crossed(last) + crossed(first)
+    ahead = lax.ppermute(kept, "z", [(last, first)])
+    kept = jnp.where(plane == last, kept, jnp.zeros_like(kept)) + ahead
+    rows = (kept.astype(jnp.float32) + got.astype(jnp.float32)).astype(jnp.bfloat16)
+    holders = [last, first]
+    step = half // 2
     while step:
         route = [(held, (held + step) % layers) for held in holders]
         rows = rows + lax.ppermute(rows, "z", route)

time: 546 us -> 541 us (level)
  waiting for transfers between devices: 334 us -> 328 us
    ppermute x4 -> x3, waiting for transfers between devices: 39.7 us -> 34.5 us  [on_device(): rows = rows + lax.ppermute(rows, 'z', route)]
  transfers between devices with their start and end apart: 38 -> 39, of which waited for: 13 -> 13; matrix products, arithmetic and copies ran while one was open for 2% -> 2% of each run, Pallas kernels for 1% -> 1%
where the time goes in v9:
time: 541 us; the launch traced here: 533 us
  waiting for transfers between devices  328 us (61%)
  starting transfers between devices  71.6 us (13%)
  blocking collectives  66.4 us (12%)
  Pallas kernels  26.5 us (5%)
  local copies, waits for them, and re-layouts  16.7 us (3%)
  between operations  14.7 us (3%)
  other arithmetic  7.57 us (1%)
    ppermute x15, waiting for transfers between devices, on_device(): part = lax.ppermute(part, ('z', 'c', 'x'), next_plane(layer))  194 us
    ppermute x10, waiting for transfers between devices, moved(): return lax.ppermute(block, axis, route)  55.6 us
    ppermute x1, waiting for transfers between devices, on_device(): across_rest = lax.ppermute(other_rest, 'x', INTER)  39.5 us
    ppermute x10, starting transfers between devices, moved(): return lax.ppermute(block, axis, route)  34.9 us
    ppermute x3, waiting for transfers between devices, on_device(): rows = rows + lax.ppermute(rows, 'z', route)  34.5 us
    all_gather x16, blocking collectives, on_device(): part = added(lax.all_gather(part, 'c', axis=0, tiled=False))  33.7 us
    all_gather x15, blocking collectives, on_device(): pair = lax.all_gather(part, 'c', axis=0, tiled=False)  32.7 us
    pallas_call x16, Pallas kernels, apply_quarter(): pl.pallas_call(quarter_layer, out_shape=jax.ShapeDtypeStruct((row_count,...  16.4 us
  transfers between devices with their start and end apart: 39, of which 13 were waited for; matrix products, arithmetic and copies ran while one was open for 2% of the time, Pallas kernels for 1%

profile of v9, /device:TPU:448, one launch (start us, length us, event | category | flops | bytes accessed | tf_op | source)
XLA Modules:
  0.0 532.9 jit_solution(13269958900719629926)
XLA Ops:
  10.6 3.4 collective-permute-start
  14.0 4.0 collective-permute-start.8
  18.0 4.9 collective-permute-start.6
  22.9 1.9 collective-permute-start.2
  24.8 4.3 collective-permute-done.refs_4_
  30.0 3.4 collective-permute-start.1
  33.4 3.5 collective-permute-start.5
  37.0 3.9 collective-permute-start.3
  40.9 5.6 %collective-permute-start.7 = (bf16[200,1600]{1,0:T(8,128)(2,1)S(1)}, bf16[200,1600]{1,0:T(8,128)(2,1)}, u32[]{:S(2)}, u32[]{:S(2)}) collective-permute-start(bf16[200,1600]{1,0:T(8,128)(2,1)S(1)} %collective-permute-done.6), channel_id=1, source_target_pairs={{0,12},{4,0},{8,4},{12,8},{1,13},{5,1},{9,5},{13,9},{2,14},{6,2},{... | collective-permute-start | bytes 1920008 | tf_op jit(solution)/shard_map/ppermute | solution.py:18
  47.7 1.9 collective-permute-start.4
  49.6 13.3 %collective-permute-done.5 = bf16[200,1600]{1,0:T(8,128)(2,1)S(1)} collective-permute-done((bf16[200,1600]{1,0:T(8,128)(2,1)S(1)}, bf16[200,1600]{1,0:T(8,128)(2,1)S(1)}, u32[]{:S(2)}, u32[]{:S(2)}) %collective-permute-start.5) | collective-permute-done | bytes 640032 | tf_op jit(solution)/shard_map/ppermute | solution.py:18
  62.9 1.9 collective-permute-start.9
  64.8 16.8 %collective-permute-done.7 = bf16[200,1600]{1,0:T(8,128)(2,1)} collective-permute-done((bf16[200,1600]{1,0:T(8,128)(2,1)S(1)}, bf16[200,1600]{1,0:T(8,128)(2,1)}, u32[]{:S(2)}, u32[]{:S(2)}) %collective-permute-start.7) | collective-permute-done | bytes 640032 | tf_op jit(solution)/shard_map/ppermute | solution.py:18
  81.6 7.7 %collective-permute-done.4 = bf16[200,1600]{1,0:T(8,128)(2,1)} collective-permute-done((bf16[200,1600]{1,0:T(8,128)(2,1)S(1)}, bf16[200,1600]{1,0:T(8,128)(2,1)}, u32[]{:S(2)}, u32[]{:S(2)}) %collective-permute-start.4) | collective-permute-done | bytes 640032 | tf_op jit(solution)/shard_map/ppermute | solution.py:18
  89.3 3.1 pad_maximum_fusion.1
  94.0 3.7 collective-permute-start.12
  97.7 3.8 collective-permute-start.14
  101.5 1.9 collective-permute-start.10
  103.4 2.4 collective-permute-start.16
  105.8 39.5 %collective-permute-done.14.refs_8_ = bf16[600,1600]{1,0:T(8,128)(2,1)} collective-permute-done((bf16[600,1600]{1,0:T(8,128)(2,1)S(1)}, bf16[600,1600]{1,0:T(8,128)(2,1)}, u32[]{:S(2)}, u32[]{:S(2)}) %collective-permute-start.14) | collective-permute-done | bytes 1920032 | tf_op jit(solution)/shard_map/ppermute | solution.py:212
  145.3 1.9 collective-permute-start.15
  147.2 4.7 collective-permute-done.12.refs_2_
  153.2 5.6 %collective-permute-start.13 = (bf16[400,1664]{1,0:T(8,128)(2,1)}, bf16[400,1664]{1,0:T(8,128)(2,1)}, u32[]{:S(2)}, u32[]{:S(2)}) collective-permute-start(bf16[400,1664]{1,0:T(8,128)(2,1)} %slice.32), channel_id=1, source_target_pairs={{0,12},{4,0},{8,4},{12,8},{1,13},{5,1},{9,5},{13,9},{2,14},{6,2},{... | collective-permute-start | bytes 3993608 | tf_op jit(solution)/shard_map/ppermute | solution.py:18
  162.8 1.9 collective-permute-start.11
  165.0 2.7 slice.30
  172.5 1.7 copy-done.3
  176.4 5.3 put_pieces.2
  181.7 10.6 %collective-permute-done.11.refs_0_ = bf16[400,1536]{1,0:T(8,128)(2,1)} collective-permute-done((bf16[400,1536]{1,0:T(8,128)(2,1)}, bf16[400,1536]{1,0:T(8,128)(2,1)}, u32[]{:S(2)}, u32[]{:S(2)}) %collective-permute-start.11) | collective-permute-done | bytes 1228832 | tf_op jit(solution)/shard_map/ppermute | solution.py:18
  192.4 3.0 put_pieces.3
  195.9 2.1 all-gather.1
  198.8 2.1 all-gather.2
  201.6 2.1 all-gather.3
  204.5 2.1 all-gather.4
  207.2 2.1 all-gather.5
  210.0 2.1 all-gather.6
  212.7 2.1 all-gather.7
  215.5 2.1 all-gather.8
  218.6 2.1 all-gather.9
  221.4 2.1 all-gather.10
  224.1 2.1 all-gather.11
  227.0 2.1 all-gather.12
  229.6 2.1 all-gather.13
  232.5 2.1 all-gather.14
  235.3 2.1 all-gather.15
  238.2 2.1 all-gather.16
  240.8 2.1 all-gather.17
  243.7 2.1 all-gather.18
  246.3 2.1 all-gather.19
  249.2 2.1 all-gather.20
  252.1 2.1 all-gather.21
  254.9 2.1 all-gather.22
  257.6 2.1 all-gather.23
  260.4 2.1 all-gather.24
  263.1 2.1 all-gather.25
  266.0 2.1 all-gather.26
  268.9 2.1 all-gather.27
  272.3 189.3 %collective-permute-done.30 = bf16[32,3200]{1,0:T(8,128)(2,1)S(1)} collective-permute-done((bf16[32,3200]{1,0:T(8,128)(2,1)S(1)}, bf16[32,3200]{1,0:T(8,128)(2,1)S(1)}, u32[]{:S(2)}, u32[]{:S(2)}) %collective-permute-start.30) | collective-permute-done | bytes 204832 | tf_op jit(solution)/shard_map/ppermute | solution.py:260
  461.7 3.3 all-gather.28
  465.0 6.7 %quarter_layer.30 = bf16[32,3200]{1,0:T(8,128)(2,1)S(1)} custom-call(s32[1]{0:T(128)} %constant.65.clone.1.tick_ref, s32[3]{0:T(128)S(1)} %pad_add_fusion.state_ref, bf16[2,32,3200]{2,1,0:T(8,128)(2,1)S(1)} %bitcast.69, bf16[4,400,3200]{2,1,0:T(8,128)(2,1)S(1)} %get-tuple-element.55.refs_0_, bf16[4,200,1600]{2,1,0:T(8,128)(2,1)S(1)} %get-tuple-element.56.refs_1_, ...), custom_call_target="tpu_custom_call" | custom-call | flops 655360000 | bytes 409600 | tf_op jit(solution)/shard_map/quarter_layer/pallas_call | solution.py:109
  471.7 2.1 all-gather.29
  475.2 5.1 collective-permute-done.31
  480.3 2.1 all-gather.30
  483.0 2.2 all-gather.31
  490.2 34.5 %collective-permute-done.37 = bf16[16,3200]{1,0:T(8,128)(2,1)S(1)} collective-permute-done((bf16[16,3200]{1,0:T(8,128)(2,1)S(1)}, bf16[16,3200]{1,0:T(8,128)(2,1)S(1)}, u32[]{:S(2)}, u32[]{:S(2)}) %collective-permute-start.37) | collective-permute-done | bytes 102432 | tf_op jit(solution)/shard_map/ppermute | solution.py:281
  (124 shorter events, 47.8 us)
Async XLA Ops:
  6.5 158.4 %all-gather.34.cloned.1.call-start = ((), (), s32[]{:S(2)}) async-start(), calls=%async_computation | async-start | bytes 3969024 | tf_op jit(solution)/shard_map/all_gather | solution.py:227
  8.3 1.3 copy-start.4
  10.5 81.8 %copy-start.5 = (bf16[200,1600]{1,0:T(8,128)(2,1)}, bf16[200,1600]{1,0:T(8,128)(2,1)S(1)}, u32[]{:S(2)}) copy-start(bf16[200,1600]{1,0:T(8,128)(2,1)S(1)} %get-tuple-element.35.refs_3_) | copy-start | bytes 1920004
  10.6 18.6 %collective-permute-start = (bf16[200,1600]{1,0:T(8,128)(2,1)S(1)}, bf16[200,1600]{1,0:T(8,128)(2,1)S(1)}, u32[]{:S(2)}, u32[]{:S(2)}) collective-permute-start(bf16[200,1600]{1,0:T(8,128)(2,1)S(1)} %get-tuple-element.35.refs_3_), channel_id=1, source_target_pairs={{0,1},{1,0},{2,3},{3,2},{4,5},{5,4},{6,7},{7,6},{8,9},{9,8},{10,11... | collective-permute-start | bytes 1920008 | tf_op jit(solution)/shard_map/ppermute | solution.py:197
  14.0 23.0 %collective-permute-start.8 = (bf16[200,1600]{1,0:T(8,128)(2,1)S(1)}, bf16[200,1600]{1,0:T(8,128)(2,1)}, u32[]{:S(2)}, u32[]{:S(2)}) collective-permute-start(bf16[200,1600]{1,0:T(8,128)(2,1)S(1)} %get-tuple-element.37), channel_id=1, source_target_pairs={{0,3},{3,0},{1,2},{2,1},{4,7},{7,4},{5,6},{6,5},{8,11},{11,8},{9,1... | collective-permute-start | bytes 1920008 | tf_op jit(solution)/shard_map/ppermute | solution.py:198
  18.0 23.0 %collective-permute-start.6 = (bf16[200,1600]{1,0:T(8,128)(2,1)S(1)}, bf16[200,1600]{1,0:T(8,128)(2,1)S(1)}, u32[]{:S(2)}, u32[]{:S(2)}) collective-permute-start(bf16[200,1600]{1,0:T(8,128)(2,1)S(1)} %get-tuple-element.37), channel_id=1, source_target_pairs={{0,12},{4,0},{8,4},{12,8},{1,13},{5,1},{9,5},{13,9},{2,14},{6,2},{... | collective-permute-start | bytes 1920008 | tf_op jit(solution)/shard_map/ppermute | solution.py:18
  22.9 24.7 %collective-permute-start.2 = (bf16[200,1600]{1,0:T(8,128)(2,1)S(1)}, bf16[200,1600]{1,0:T(8,128)(2,1)S(1)}, u32[]{:S(2)}, u32[]{:S(2)}) collective-permute-start(bf16[200,1600]{1,0:T(8,128)(2,1)S(1)} %get-tuple-element.35.refs_3_), channel_id=1, source_target_pairs={{0,4},{4,8},{8,12},{12,0},{1,5},{5,9},{9,13},{13,1},{2,6},{6,10},{... | collective-permute-start | bytes 1920008 | tf_op jit(solution)/shard_map/ppermute | solution.py:18
  29.1 0.9 copy-start.7
  30.0 62.3 %collective-permute-start.1 = (bf16[200,3200]{1,0:T(8,128)(2,1)}, bf16[200,3200]{1,0:T(8,128)(2,1)}, u32[]{:S(2)}, u32[]{:S(2)}) collective-permute-start(bf16[200,3200]{1,0:T(8,128)(2,1)} %bitcast.88), channel_id=1, source_target_pairs={{0,1},{1,0},{2,3},{3,2},{4,5},{5,4},{6,7},{7,6},{8,9},{9,8},{10,11... | collective-permute-start | bytes 3840008 | tf_op jit(solution)/shard_map/ppermute | solution.py:201
  33.4 29.5 %collective-permute-start.5 = (bf16[200,1600]{1,0:T(8,128)(2,1)S(1)}, bf16[200,1600]{1,0:T(8,128)(2,1)S(1)}, u32[]{:S(2)}, u32[]{:S(2)}) collective-permute-start(bf16[200,1600]{1,0:T(8,128)(2,1)S(1)} %get-tuple-element.37), channel_id=1, source_target_pairs={{0,4},{4,8},{8,12},{12,0},{1,5},{5,9},{9,13},{13,1},{2,6},{6,10},{... | collective-permute-start | bytes 1920008 | tf_op jit(solution)/shard_map/ppermute | solution.py:18
  37.0 27.8 %collective-permute-start.3 = (bf16[200,1600]{1,0:T(8,128)(2,1)S(1)}, bf16[200,1600]{1,0:T(8,128)(2,1)}, u32[]{:S(2)}, u32[]{:S(2)}) collective-permute-start(bf16[200,1600]{1,0:T(8,128)(2,1)S(1)} %get-tuple-element.35.refs_3_), channel_id=1, source_target_pairs={{0,12},{4,0},{8,4},{12,8},{1,13},{5,1},{9,5},{13,9},{2,14},{6,2},{... | collective-permute-start | bytes 1920008 | tf_op jit(solution)/shard_map/ppermute | solution.py:18
  40.9 40.6 %collective-permute-start.7 = (bf16[200,1600]{1,0:T(8,128)(2,1)S(1)}, bf16[200,1600]{1,0:T(8,128)(2,1)}, u32[]{:S(2)}, u32[]{:S(2)}) collective-permute-start(bf16[200,1600]{1,0:T(8,128)(2,1)S(1)} %collective-permute-done.6), channel_id=1, source_target_pairs={{0,12},{4,0},{8,4},{12,8},{1,13},{5,1},{9,5},{13,9},{2,14},{6,2},{... | collective-permute-start | bytes 1920008 | tf_op jit(solution)/shard_map/ppermute | solution.py:18
  47.7 41.6 %collective-permute-start.4 = (bf16[200,1600]{1,0:T(8,128)(2,1)S(1)}, bf16[200,1600]{1,0:T(8,128)(2,1)}, u32[]{:S(2)}, u32[]{:S(2)}) collective-permute-start(bf16[200,1600]{1,0:T(8,128)(2,1)S(1)} %collective-permute-done.2), channel_id=1, source_target_pairs={{0,4},{4,8},{8,12},{12,0},{1,5},{5,9},{9,13},{13,1},{2,6},{6,10},{... | collective-permute-start | bytes 1920008 | tf_op jit(solution)/shard_map/ppermute | solution.py:18
  49.6 42.8 %copy-start.10 = (bf16[1,200,3200]{2,1,0:T(8,128)(2,1)S(1)}, bf16[1,200,3200]{2,1,0:T(8,128)(2,1)}, u32[]{:S(2)}) copy-start(bf16[1,200,3200]{2,1,0:T(8,128)(2,1)} %param.5) | copy-start | bytes 3840004
  62.9 31.1 %collective-permute-start.9 = (bf16[200,1600]{1,0:T(8,128)(2,1)}, bf16[200,1600]{1,0:T(8,128)(2,1)S(1)}, u32[]{:S(2)}, u32[]{:S(2)}) collective-permute-start(bf16[200,1600]{1,0:T(8,128)(2,1)} %collective-permute-done.8.refs_5_), channel_id=1, source_target_pairs={{0,1},{1,0},{2,3},{3,2},{4,5},{5,4},{6,7},{7,6},{8,9},{9,8},{10,11... | collective-permute-start | bytes 1920008 | tf_op jit(solution)/shard_map/ppermute | solution.py:199
  94.0 57.9 %collective-permute-start.12 = (bf16[400,3200]{1,0:T(8,128)(2,1)S(1)}, bf16[400,3200]{1,0:T(8,128)(2,1)S(1)}, u32[]{:S(2)}, u32[]{:S(2)}) collective-permute-start(bf16[400,3200]{1,0:T(8,128)(2,1)S(1)} %pad_maximum_fusion.refs_0_), channel_id=1, source_target_pairs={{0,12},{4,0},{8,4},{12,8},{1,13},{5,1},{9,5},{13,9},{2,14},{6,2},{... | collective-permute-start | bytes 7680008 | tf_op jit(solution)/shard_map/ppermute | solution.py:18
  97.7 47.6 %collective-permute-start.14 = (bf16[600,1600]{1,0:T(8,128)(2,1)S(1)}, bf16[600,1600]{1,0:T(8,128)(2,1)}, u32[]{:S(2)}, u32[]{:S(2)}) collective-permute-start(bf16[600,1600]{1,0:T(8,128)(2,1)S(1)} %get-tuple-element.48), channel_id=1, source_target_pairs={{0,3},{3,0},{1,2},{2,1},{4,7},{7,4},{5,6},{6,5},{8,11},{11,8},{9,1... | collective-permute-start | bytes 5760008 | tf_op jit(solution)/shard_map/ppermute | solution.py:212
  101.5 58.7 %collective-permute-start.10 = (bf16[400,3200]{1,0:T(8,128)(2,1)S(1)}, bf16[400,3200]{1,0:T(8,128)(2,1)S(1)}, u32[]{:S(2)}, u32[]{:S(2)}) collective-permute-start(bf16[400,3200]{1,0:T(8,128)(2,1)S(1)} %pad_maximum_fusion.refs_0_), channel_id=1, source_target_pairs={{0,4},{4,8},{8,12},{12,0},{1,5},{5,9},{9,13},{13,1},{2,6},{6,10},{... | collective-permute-start | bytes 7680008 | tf_op jit(solution)/shard_map/ppermute | solution.py:18
  103.4 67.4 %collective-permute-start.16 = (bf16[600,1600]{1,0:T(8,128)(2,1)}, bf16[600,1600]{1,0:T(8,128)(2,1)}, u32[]{:S(2)}, u32[]{:S(2)}) collective-permute-start(bf16[600,1600]{1,0:T(8,128)(2,1)} %get-tuple-element.51.refs_6_), channel_id=1, source_target_pairs={{0,1},{1,0},{2,3},{3,2},{4,5},{5,4},{6,7},{7,6},{8,9},{9,8},{10,11... | collective-permute-start | bytes 5760008 | tf_op jit(solution)/shard_map/ppermute | solution.py:211
  145.3 47.0 %collective-permute-start.15 = (bf16[600,1600]{1,0:T(8,128)(2,1)}, bf16[600,1600]{1,0:T(8,128)(2,1)}, u32[]{:S(2)}, u32[]{:S(2)}) collective-permute-start(bf16[600,1600]{1,0:T(8,128)(2,1)} %collective-permute-done.14.refs_8_), channel_id=1, source_target_pairs={{0,1},{1,0},{2,3},{3,2},{4,5},{5,4},{6,7},{7,6},{8,9},{9,8},{10,11... | collective-permute-start | bytes 5760008 | tf_op jit(solution)/shard_map/ppermute | solution.py:213
  151.9 9.4 %copy-start = (bf16[400,3200]{1,0:T(8,128)(2,1)}, bf16[400,3200]{1,0:T(8,128)(2,1)S(1)}, u32[]{:S(2)}) copy-start(bf16[400,3200]{1,0:T(8,128)(2,1)S(1)} %collective-permute-done.12.refs_2_) | copy-start | bytes 7680004
  153.2 39.1 %collective-permute-start.13 = (bf16[400,1664]{1,0:T(8,128)(2,1)}, bf16[400,1664]{1,0:T(8,128)(2,1)}, u32[]{:S(2)}, u32[]{:S(2)}) collective-permute-start(bf16[400,1664]{1,0:T(8,128)(2,1)} %slice.32), channel_id=1, source_target_pairs={{0,12},{4,0},{8,4},{12,8},{1,13},{5,1},{9,5},{13,9},{2,14},{6,2},{... | collective-permute-start | bytes 3993608 | tf_op jit(solution)/shard_map/ppermute | solution.py:18
  161.3 1.5 copy-start.2
  162.8 29.5 %collective-permute-start.11 = (bf16[400,1536]{1,0:T(8,128)(2,1)}, bf16[400,1536]{1,0:T(8,128)(2,1)}, u32[]{:S(2)}, u32[]{:S(2)}) collective-permute-start(bf16[400,1536]{1,0:T(8,128)(2,1)} %slice.31), channel_id=1, source_target_pairs={{0,4},{4,8},{8,12},{12,0},{1,5},{5,9},{9,13},{13,1},{2,6},{6,10},{... | collective-permute-start | bytes 3686408 | tf_op jit(solution)/shard_map/ppermute | solution.py:18
  170.8 1.7 copy-start.1
  172.5 1.7 copy-start.3
  174.2 1.1 copy-start.6
  175.3 1.1 copy-start.8
  198.1 0.7 collective-permute-start.17
  203.8 0.7 collective-permute-start.18
  209.3 0.7 collective-permute-start.19
  214.8 0.7 collective-permute-start.20
  220.7 0.7 collective-permute-start.21
  226.3 0.7 collective-permute-start.22
  231.8 0.7 collective-permute-start.23
  237.5 0.7 collective-permute-start.24
  243.0 0.7 collective-permute-start.25
  248.5 0.7 collective-permute-start.26
  254.2 0.7 collective-permute-start.27
  259.7 0.7 collective-permute-start.28
  265.3 0.7 collective-permute-start.29
  271.0 190.6 %collective-permute-start.30 = (bf16[32,3200]{1,0:T(8,128)(2,1)S(1)}, bf16[32,3200]{1,0:T(8,128)(2,1)S(1)}, u32[]{:S(2)}, u32[]{:S(2)}) collective-permute-start(bf16[32,3200]{1,0:T(8,128)(2,1)S(1)} %add_pair.29), channel_id=1, source_target_pairs={{416,448},{432,451},{419,464},{435,467},{417,449},{433,450},{418,4... | collective-permute-start | bytes 614408 | tf_op jit(solution)/shard_map/ppermute | solution.py:260
  473.9 6.4 %collective-permute-start.31 = (bf16[32,3200]{1,0:T(8,128)(2,1)S(1)}, bf16[32,3200]{1,0:T(8,128)(2,1)S(1)}, u32[]{:S(2)}, u32[]{:S(2)}) collective-permute-start(bf16[32,3200]{1,0:T(8,128)(2,1)S(1)} %add_pair.30), channel_id=1, source_target_pairs={{448,480},{464,483},{451,496},{467,499},{449,481},{465,482},{450,4... | collective-permute-start | bytes 614408 | tf_op jit(solution)/shard_map/ppermute | solution.py:260
  483.0 41.8 %copy-start.9 = (bf16[16,200,256]{2,1,0:T(8,128)(2,1)S(1)}, bf16[16,200,256]{2,1,0:T(8,128)(2,1)}, u32[]{:S(2)}) copy-start(bf16[16,200,256]{2,1,0:T(8,128)(2,1)} %slice.30) | copy-start | bytes 4915204
  485.3 2.0 collective-permute-start.32
  486.0 1.4 collective-permute-start.34
  486.7 0.7 collective-permute-start.33
  487.4 0.7 collective-permute-start.35
  488.2 0.7 collective-permute-start.36
  488.9 35.8 %collective-permute-start.37 = (bf16[16,3200]{1,0:T(8,128)(2,1)S(1)}, bf16[16,3200]{1,0:T(8,128)(2,1)S(1)}, u32[]{:S(2)}, u32[]{:S(2)}) collective-permute-start(bf16[16,3200]{1,0:T(8,128)(2,1)S(1)} %add.58), channel_id=1, source_target_pairs={{480,0},{224,256},{96,128},{352,384},{32,64},{288,320},{160,192},{... | collective-permute-start | bytes 307208 | tf_op jit(solution)/shard_map/ppermute | solution.py:281
Sparse Core Ops, SparseCore 0:
  10.4 79.7 all-gather.33

commit v10 on v9

--- a/solution.py
+++ b/solution.py
@@ -221,17 +221,16 @@
     spots = [lax.rem(y + offset, SIDE) for offset in OFFSETS]
     spots += [x, mate_x, SIDE - 1 - x, SIDE - 1 - mate_x]
     spots = jnp.stack(spots).astype(jnp.int32)
-    features, outputs = w_proj.shape
-    flat = patches.reshape(-1, features)
-    flat = jnp.pad(flat, ((0, 0), (0, outputs - features)))
+    features = w_proj.shape[0]
+    flat = patches.reshape(-1, features).T
     everyone = lax.all_gather(jnp.concatenate([flat, w_proj], axis=0), tp, axis=0)
-    projection = everyone[:, flat.shape[0] :].reshape(-1, outputs)
-    count = flat.shape[0] // SIDE // SIDE
+    projection = everyone[:, features:].reshape(-1, w_proj.shape[1])
+    count = flat.shape[1] // SIDE // SIDE
 
     def rows_of(column):
         at = (SIDE * y + column) * count
-        block = lax.dynamic_slice_in_dim(everyone, at, count, axis=1)
-        return block[:, :, :features].transpose(1, 0, 2).reshape(count, -1)
+        block = lax.dynamic_slice_in_dim(everyone[:, :features], at, count, axis=2)
+        return block.reshape(-1, count).T
 
     first = jnp.where(low == 1, x, SIDE - 1 - x)
     rows = jnp.concatenate([rows_of(first), rows_of(SIDE - 1 - first)], axis=0)
@@ -241,10 +240,9 @@
     held = (spots, pair, state, projection)
     spots, pair, state, projection = lax.optimization_barrier(held)
     early = [(near, 0, 0, 0), (below, 0, 1, 0), (above, 0, 2, 0)]
-    early += [(own, 1, 4, 0), (beside, 1, 5, 0), (across, 1, 6, 0)]
+    early += [(own, 1, 4, 0), (beside, 1, 5, 0), (across, 1, 6, 0), (corner, 1, 7, 0)]
     early += [(own_rest, 2, 4, 0), (beside_rest, 2, 5, 0), (across_rest, 2, 6, 0)]
-    late = [(head, 0, 3, 0), (tail, 0, 3, cut)]
-    late += [(corner, 1, 7, 0), (corner_rest, 2, 7, 0)]
+    late = [(head, 0, 3, 0), (tail, 0, 3, cut), (corner_rest, 2, 7, 0)]
     shapes = [(SIDE,) + piece.shape for piece in (near, own, own_rest)]
     weights = ()
     for group in (early, late):

time: 541 us -> 533 us (0.985)
  the two profiles are of different devices: /device:TPU:448 before, /device:TPU:64 now
where the time goes in v10:
time: 533 us; the launch traced here: 525 us
  waiting for transfers between devices  321 us (60%)
  starting transfers between devices  68.5 us (13%)
  blocking collectives  65.2 us (12%)
  Pallas kernels  26.5 us (5%)
  local copies, waits for them, and re-layouts  21.3 us (4%)
  between operations  14.7 us (3%)
  other arithmetic  6.92 us (1%)
    ppermute x3, waiting for transfers between devices, on_device(): rows = rows + lax.ppermute(rows, 'z', route)  198 us
    ppermute x1, waiting for transfers between devices, on_device(): across_rest = lax.ppermute(other_rest, 'x', INTER)  46.5 us
    ppermute x10, waiting for transfers between devices, moved(): return lax.ppermute(block, axis, route)  44.3 us
    all_gather x16, blocking collectives, on_device(): part = added(lax.all_gather(part, 'c', axis=0, tiled=False))  33.7 us
    all_gather x15, blocking collectives, on_device(): pair = lax.all_gather(part, 'c', axis=0, tiled=False)  31.5 us
    ppermute x15, waiting for transfers between devices, on_device(): part = lax.ppermute(part, ('z', 'c', 'x'), next_plane(layer))  31.3 us
    ppermute x10, starting transfers between devices, moved(): return lax.ppermute(block, axis, route)  30.5 us
    pallas_call x16, Pallas kernels, apply_quarter(): pl.pallas_call(quarter_layer, out_shape=jax.ShapeDtypeStruct((row_count,...  16.4 us
  transfers between devices with their start and end apart: 39, of which 11 were waited for; matrix products, arithmetic and copies ran while one was open for 4% of the time, Pallas kernels for 1%

profile of v10, /device:TPU:64, one launch (start us, length us, event | category | flops | bytes accessed | tf_op | source)
XLA Modules:
  0.0 524.8 jit_solution(14120636019566936556)
XLA Ops:
  8.8 3.4 collective-permute-start
  12.2 4.0 collective-permute-start.8
  16.2 4.9 collective-permute-start.6
  21.2 1.9 collective-permute-start.2
  27.4 3.4 collective-permute-start.1
  30.8 3.5 collective-permute-start.5
  34.3 3.6 collective-permute-start.3
  37.9 3.7 collective-permute-start.7
  42.3 1.9 collective-permute-start.4
  44.2 15.1 %collective-permute-done.5 = bf16[200,1600]{1,0:T(8,128)(2,1)} collective-permute-done((bf16[200,1600]{1,0:T(8,128)(2,1)S(1)}, bf16[200,1600]{1,0:T(8,128)(2,1)}, u32[]{:S(2)}, u32[]{:S(2)}) %collective-permute-start.5) | collective-permute-done | bytes 640032 | tf_op jit(solution)/shard_map/ppermute | solution.py:18
  59.3 2.3 collective-permute-start.9
  61.7 7.6 %collective-permute-done.7 = bf16[200,1600]{1,0:T(8,128)(2,1)} collective-permute-done((bf16[200,1600]{1,0:T(8,128)(2,1)}, bf16[200,1600]{1,0:T(8,128)(2,1)}, u32[]{:S(2)}, u32[]{:S(2)}) %collective-permute-start.7) | collective-permute-done | bytes 640032 | tf_op jit(solution)/shard_map/ppermute | solution.py:18
  69.2 2.8 collective-permute-done.4
  72.1 3.7 pad_maximum_fusion.1
  75.7 1.7 broadcast_select_fusion.1
  77.7 3.2 collective-permute-start.12
  80.9 4.7 collective-permute-start.14
  85.5 1.9 collective-permute-start.10
  87.5 2.1 collective-permute-start.16
  89.6 46.5 %collective-permute-done.14.refs_9_ = bf16[600,1600]{1,0:T(8,128)(2,1)} collective-permute-done((bf16[600,1600]{1,0:T(8,128)(2,1)S(1)}, bf16[600,1600]{1,0:T(8,128)(2,1)}, u32[]{:S(2)}, u32[]{:S(2)}) %collective-permute-start.14) | collective-permute-done | bytes 1920032 | tf_op jit(solution)/shard_map/ppermute | solution.py:212
  136.1 2.2 collective-permute-start.15
  138.3 8.2 %collective-permute-done.12.refs_2_ = bf16[400,3200]{1,0:T(8,128)(2,1)S(1)} collective-permute-done((bf16[400,3200]{1,0:T(8,128)(2,1)S(1)}, bf16[400,3200]{1,0:T(8,128)(2,1)S(1)}, u32[]{:S(2)}, u32[]{:S(2)}) %collective-permute-start.12) | collective-permute-done | bytes 2560032 | tf_op jit(solution)/shard_map/ppermute | solution.py:18
  147.8 3.6 collective-permute-start.13
  154.1 2.2 collective-permute-start.11
  156.5 3.3 fusion.1
  166.2 1.7 copy-done.3
  170.1 5.3 %put_pieces.2 = (bf16[4,400,3200]{2,1,0:T(8,128)(2,1)S(1)}, bf16[4,200,1600]{2,1,0:T(8,128)(2,1)S(1)}, bf16[4,600,1600]{2,1,0:T(8,128)(2,1)S(1)}) custom-call(s32[8]{0:T(128)S(1)} %stack.56.spots_ref, bf16[400,3200]{1,0:T(8,128)(2,1)S(1)} %pad_maximum_fusion.refs_0_, bf16[400,3200]{1,0:T(8,128)(2,1)S(1)} %copy-done.3, bf16[400,3200]{1,0:T(8,128)(2,1)S(1)} %copy-done.1, ...), custom_call_target="tpu_custom_call" | custom-call | tf_op jit(solution)/shard_map/put_pieces/pallas_call | solution.py:54
  175.5 9.9 %collective-permute-done.11.refs_0_ = bf16[400,1536]{1,0:T(8,128)(2,1)} collective-permute-done((bf16[400,1536]{1,0:T(8,128)(2,1)}, bf16[400,1536]{1,0:T(8,128)(2,1)}, u32[]{:S(2)}, u32[]{:S(2)}) %collective-permute-start.11) | collective-permute-done | bytes 1228832 | tf_op jit(solution)/shard_map/ppermute | solution.py:18
  185.3 2.9 put_pieces.3
  188.8 2.1 all-gather.1
  191.7 2.1 all-gather.2
  194.5 2.1 all-gather.3
  198.0 26.4 %collective-permute-done.18 = bf16[32,3200]{1,0:T(8,128)(2,1)S(1)} collective-permute-done((bf16[32,3200]{1,0:T(8,128)(2,1)S(1)}, bf16[32,3200]{1,0:T(8,128)(2,1)S(1)}, u32[]{:S(2)}, u32[]{:S(2)}) %collective-permute-start.18) | collective-permute-done | bytes 204832 | tf_op jit(solution)/shard_map/ppermute | solution.py:258
  224.4 2.1 all-gather.4
  226.5 6.7 %quarter_layer.18 = bf16[32,3200]{1,0:T(8,128)(2,1)S(1)} custom-call(s32[1]{0:T(128)} %constant.76.clone.1.tick_ref, s32[3]{0:T(128)S(1)} %pad_add_fusion.state_ref, bf16[2,32,3200]{2,1,0:T(8,128)(2,1)S(1)} %bitcast.59, bf16[4,400,3200]{2,1,0:T(8,128)(2,1)S(1)} %get-tuple-element.55.refs_0_, bf16[4,200,1600]{2,1,0:T(8,128)(2,1)S(1)} %get-tuple-element.56.refs_1_, ...), custom_call_target="tpu_custom_call" | custom-call | flops 655360000 | bytes 409600 | tf_op jit(solution)/shard_map/quarter_layer/pallas_call | solution.py:109
  233.3 2.1 all-gather.5
  236.7 4.9 collective-permute-done.19
  241.6 2.1 all-gather.6
  244.3 2.1 all-gather.7
  247.1 2.1 all-gather.8
  250.2 2.1 all-gather.9
  253.0 2.1 all-gather.10
  255.7 2.1 all-gather.11
  258.5 2.1 all-gather.12
  261.2 2.1 all-gather.13
  264.1 2.1 all-gather.14
  266.9 2.1 all-gather.15
  269.8 2.1 all-gather.16
  272.4 2.1 all-gather.17
  275.3 2.1 all-gather.18
  277.9 2.1 all-gather.19
  280.8 2.1 all-gather.20
  283.7 2.1 all-gather.21
  286.5 2.1 all-gather.22
  289.2 2.1 all-gather.23
  292.0 2.1 all-gather.24
  294.7 2.1 all-gather.25
  297.5 2.1 all-gather.26
  300.5 2.1 all-gather.27
  303.3 2.1 all-gather.28
  306.0 2.1 all-gather.29
  308.8 2.1 all-gather.30
  311.5 2.2 all-gather.31
  318.7 197.8 %collective-permute-done.37 = bf16[16,3200]{1,0:T(8,128)(2,1)S(1)} collective-permute-done((bf16[16,3200]{1,0:T(8,128)(2,1)S(1)}, bf16[16,3200]{1,0:T(8,128)(2,1)S(1)}, u32[]{:S(2)}, u32[]{:S(2)}) %collective-permute-start.37) | collective-permute-done | bytes 102432 | tf_op jit(solution)/shard_map/ppermute | solution.py:279
  (124 shorter events, 47.6 us)
Async XLA Ops:
  6.5 149.9 %all-gather.34.cloned.1.call-start = ((), (), s32[]{:S(2)}) async-start(), calls=%async_computation | async-start | bytes 3481600 | tf_op jit(solution)/shard_map/all_gather | solution.py:226
  6.5 1.3 copy-start.4
  7.8 19.6 %copy-start.10 = (bf16[1,200,3200]{2,1,0:T(8,128)(2,1)S(1)}, bf16[1,200,3200]{2,1,0:T(8,128)(2,1)}, u32[]{:S(2)}) copy-start(bf16[1,200,3200]{2,1,0:T(8,128)(2,1)} %param.5) | copy-start | bytes 3840004
  8.8 18.6 %collective-permute-start = (bf16[200,1600]{1,0:T(8,128)(2,1)S(1)}, bf16[200,1600]{1,0:T(8,128)(2,1)S(1)}, u32[]{:S(2)}, u32[]{:S(2)}) collective-permute-start(bf16[200,1600]{1,0:T(8,128)(2,1)S(1)} %get-tuple-element.35.refs_3_), channel_id=1, source_target_pairs={{0,1},{1,0},{2,3},{3,2},{4,5},{5,4},{6,7},{7,6},{8,9},{9,8},{10,11... | collective-permute-start | bytes 1920008 | tf_op jit(solution)/shard_map/ppermute | solution.py:197
  12.2 22.1 %collective-permute-start.8 = (bf16[200,1600]{1,0:T(8,128)(2,1)S(1)}, bf16[200,1600]{1,0:T(8,128)(2,1)}, u32[]{:S(2)}, u32[]{:S(2)}) collective-permute-start(bf16[200,1600]{1,0:T(8,128)(2,1)S(1)} %get-tuple-element.37), channel_id=1, source_target_pairs={{0,3},{3,0},{1,2},{2,1},{4,7},{7,4},{5,6},{6,5},{8,11},{11,8},{9,1... | collective-permute-start | bytes 1920008 | tf_op jit(solution)/shard_map/ppermute | solution.py:198
  16.2 21.7 %collective-permute-start.6 = (bf16[200,1600]{1,0:T(8,128)(2,1)S(1)}, bf16[200,1600]{1,0:T(8,128)(2,1)}, u32[]{:S(2)}, u32[]{:S(2)}) collective-permute-start(bf16[200,1600]{1,0:T(8,128)(2,1)S(1)} %get-tuple-element.37), channel_id=1, source_target_pairs={{0,12},{4,0},{8,4},{12,8},{1,13},{5,1},{9,5},{13,9},{2,14},{6,2},{... | collective-permute-start | bytes 1920008 | tf_op jit(solution)/shard_map/ppermute | solution.py:18
  21.2 21.1 %collective-permute-start.2 = (bf16[200,1600]{1,0:T(8,128)(2,1)S(1)}, bf16[200,1600]{1,0:T(8,128)(2,1)}, u32[]{:S(2)}, u32[]{:S(2)}) collective-permute-start(bf16[200,1600]{1,0:T(8,128)(2,1)S(1)} %get-tuple-element.35.refs_3_), channel_id=1, source_target_pairs={{0,4},{4,8},{8,12},{12,0},{1,5},{5,9},{9,13},{13,1},{2,6},{6,10},{... | collective-permute-start | bytes 1920008 | tf_op jit(solution)/shard_map/ppermute | solution.py:18
  27.4 48.3 %copy-start.5 = (bf16[200,1600]{1,0:T(8,128)(2,1)}, bf16[200,1600]{1,0:T(8,128)(2,1)S(1)}, u32[]{:S(2)}) copy-start(bf16[200,1600]{1,0:T(8,128)(2,1)S(1)} %collective-permute-done.refs_4_) | copy-start | bytes 1920004
  27.4 48.3 %collective-permute-start.1 = (bf16[200,3200]{1,0:T(8,128)(2,1)S(1)}, bf16[200,3200]{1,0:T(8,128)(2,1)}, u32[]{:S(2)}, u32[]{:S(2)}) collective-permute-start(bf16[200,3200]{1,0:T(8,128)(2,1)S(1)} %bitcast.93), channel_id=1, source_target_pairs={{0,1},{1,0},{2,3},{3,2},{4,5},{5,4},{6,7},{7,6},{8,9},{9,8},{10,11... | collective-permute-start | bytes 3840008 | tf_op jit(solution)/shard_map/ppermute | solution.py:201
  30.8 28.5 %collective-permute-start.5 = (bf16[200,1600]{1,0:T(8,128)(2,1)S(1)}, bf16[200,1600]{1,0:T(8,128)(2,1)}, u32[]{:S(2)}, u32[]{:S(2)}) collective-permute-start(bf16[200,1600]{1,0:T(8,128)(2,1)S(1)} %get-tuple-element.37), channel_id=1, source_target_pairs={{0,4},{4,8},{8,12},{12,0},{1,5},{5,9},{9,13},{13,1},{2,6},{6,10},{... | collective-permute-start | bytes 1920008 | tf_op jit(solution)/shard_map/ppermute | solution.py:18
  34.3 27.3 %collective-permute-start.3 = (bf16[200,1600]{1,0:T(8,128)(2,1)S(1)}, bf16[200,1600]{1,0:T(8,128)(2,1)}, u32[]{:S(2)}, u32[]{:S(2)}) collective-permute-start(bf16[200,1600]{1,0:T(8,128)(2,1)S(1)} %get-tuple-element.35.refs_3_), channel_id=1, source_target_pairs={{0,12},{4,0},{8,4},{12,8},{1,13},{5,1},{9,5},{13,9},{2,14},{6,2},{... | collective-permute-start | bytes 1920008 | tf_op jit(solution)/shard_map/ppermute | solution.py:18
  37.9 31.3 %collective-permute-start.7 = (bf16[200,1600]{1,0:T(8,128)(2,1)}, bf16[200,1600]{1,0:T(8,128)(2,1)}, u32[]{:S(2)}, u32[]{:S(2)}) collective-permute-start(bf16[200,1600]{1,0:T(8,128)(2,1)} %collective-permute-done.6), channel_id=1, source_target_pairs={{0,12},{4,0},{8,4},{12,8},{1,13},{5,1},{9,5},{13,9},{2,14},{6,2},{... | collective-permute-start | bytes 1920008 | tf_op jit(solution)/shard_map/ppermute | solution.py:18
  42.3 29.8 %collective-permute-start.4 = (bf16[200,1600]{1,0:T(8,128)(2,1)}, bf16[200,1600]{1,0:T(8,128)(2,1)}, u32[]{:S(2)}, u32[]{:S(2)}) collective-permute-start(bf16[200,1600]{1,0:T(8,128)(2,1)} %collective-permute-done.2), channel_id=1, source_target_pairs={{0,4},{4,8},{8,12},{12,0},{1,5},{5,9},{9,13},{13,1},{2,6},{6,10},{... | collective-permute-start | bytes 1920008 | tf_op jit(solution)/shard_map/ppermute | solution.py:18
  59.3 18.3 %collective-permute-start.9 = (bf16[200,1600]{1,0:T(8,128)(2,1)}, bf16[200,1600]{1,0:T(8,128)(2,1)S(1)}, u32[]{:S(2)}, u32[]{:S(2)}) collective-permute-start(bf16[200,1600]{1,0:T(8,128)(2,1)} %collective-permute-done.8.refs_5_), channel_id=1, source_target_pairs={{0,1},{1,0},{2,3},{3,2},{4,5},{5,4},{6,7},{7,6},{8,9},{9,8},{10,11... | collective-permute-start | bytes 1920008 | tf_op jit(solution)/shard_map/ppermute | solution.py:199
  77.7 74.9 %copy-start.7 = (bf16[200,1600]{1,0:T(8,128)(2,1)}, bf16[200,1600]{1,0:T(8,128)(2,1)S(1)}, u32[]{:S(2)}) copy-start(bf16[200,1600]{1,0:T(8,128)(2,1)S(1)} %collective-permute-done.9.refs_6_) | copy-start | bytes 1920004
  77.7 68.8 %collective-permute-start.12 = (bf16[400,3200]{1,0:T(8,128)(2,1)S(1)}, bf16[400,3200]{1,0:T(8,128)(2,1)S(1)}, u32[]{:S(2)}, u32[]{:S(2)}) collective-permute-start(bf16[400,3200]{1,0:T(8,128)(2,1)S(1)} %pad_maximum_fusion.refs_0_), channel_id=1, source_target_pairs={{0,12},{4,0},{8,4},{12,8},{1,13},{5,1},{9,5},{13,9},{2,14},{6,2},{... | collective-permute-start | bytes 7680008 | tf_op jit(solution)/shard_map/ppermute | solution.py:18
  80.9 55.2 %collective-permute-start.14 = (bf16[600,1600]{1,0:T(8,128)(2,1)S(1)}, bf16[600,1600]{1,0:T(8,128)(2,1)}, u32[]{:S(2)}, u32[]{:S(2)}) collective-permute-start(bf16[600,1600]{1,0:T(8,128)(2,1)S(1)} %get-tuple-element.47), channel_id=1, source_target_pairs={{0,3},{3,0},{1,2},{2,1},{4,7},{7,4},{5,6},{6,5},{8,11},{11,8},{9,1... | collective-permute-start | bytes 5760008 | tf_op jit(solution)/shard_map/ppermute | solution.py:212
  85.5 65.9 %collective-permute-start.10 = (bf16[400,3200]{1,0:T(8,128)(2,1)S(1)}, bf16[400,3200]{1,0:T(8,128)(2,1)S(1)}, u32[]{:S(2)}, u32[]{:S(2)}) collective-permute-start(bf16[400,3200]{1,0:T(8,128)(2,1)S(1)} %pad_maximum_fusion.refs_0_), channel_id=1, source_target_pairs={{0,4},{4,8},{8,12},{12,0},{1,5},{5,9},{9,13},{13,1},{2,6},{6,10},{... | collective-permute-start | bytes 7680008 | tf_op jit(solution)/shard_map/ppermute | solution.py:18
  87.5 77.0 %collective-permute-start.16 = (bf16[600,1600]{1,0:T(8,128)(2,1)}, bf16[600,1600]{1,0:T(8,128)(2,1)}, u32[]{:S(2)}, u32[]{:S(2)}) collective-permute-start(bf16[600,1600]{1,0:T(8,128)(2,1)} %get-tuple-element.51.refs_7_), channel_id=1, source_target_pairs={{0,1},{1,0},{2,3},{3,2},{4,5},{5,4},{6,7},{7,6},{8,9},{9,8},{10,11... | collective-permute-start | bytes 5760008 | tf_op jit(solution)/shard_map/ppermute | solution.py:211
  136.1 49.2 %collective-permute-start.15 = (bf16[600,1600]{1,0:T(8,128)(2,1)}, bf16[600,1600]{1,0:T(8,128)(2,1)}, u32[]{:S(2)}, u32[]{:S(2)}) collective-permute-start(bf16[600,1600]{1,0:T(8,128)(2,1)} %collective-permute-done.14.refs_9_), channel_id=1, source_target_pairs={{0,1},{1,0},{2,3},{3,2},{4,5},{5,4},{6,7},{7,6},{8,9},{9,8},{10,11... | collective-permute-start | bytes 5760008 | tf_op jit(solution)/shard_map/ppermute | solution.py:213
  146.5 6.1 %copy-start = (bf16[400,3200]{1,0:T(8,128)(2,1)}, bf16[400,3200]{1,0:T(8,128)(2,1)S(1)}, u32[]{:S(2)}) copy-start(bf16[400,3200]{1,0:T(8,128)(2,1)S(1)} %collective-permute-done.12.refs_2_) | copy-start | bytes 7680004
  147.8 37.6 %collective-permute-start.13 = (bf16[400,1664]{1,0:T(8,128)(2,1)}, bf16[400,1664]{1,0:T(8,128)(2,1)}, u32[]{:S(2)}, u32[]{:S(2)}) collective-permute-start(bf16[400,1664]{1,0:T(8,128)(2,1)} %slice.30), channel_id=1, source_target_pairs={{0,12},{4,0},{8,4},{12,8},{1,13},{5,1},{9,5},{13,9},{2,14},{6,2},{... | collective-permute-start | bytes 3993608 | tf_op jit(solution)/shard_map/ppermute | solution.py:18
  152.6 1.5 copy-start.2
  154.1 31.2 %collective-permute-start.11 = (bf16[400,1536]{1,0:T(8,128)(2,1)}, bf16[400,1536]{1,0:T(8,128)(2,1)}, u32[]{:S(2)}, u32[]{:S(2)}) collective-permute-start(bf16[400,1536]{1,0:T(8,128)(2,1)} %slice.29), channel_id=1, source_target_pairs={{0,4},{4,8},{8,12},{12,0},{1,5},{5,9},{9,13},{13,1},{2,6},{6,10},{... | collective-permute-start | bytes 3686408 | tf_op jit(solution)/shard_map/ppermute | solution.py:18
  164.5 1.7 copy-start.1
  166.2 1.7 copy-start.3
  167.9 1.1 copy-start.6
  169.0 1.1 copy-start.8
  191.0 0.7 collective-permute-start.17
  196.7 27.7 %collective-permute-start.18 = (bf16[32,3200]{1,0:T(8,128)(2,1)S(1)}, bf16[32,3200]{1,0:T(8,128)(2,1)S(1)}, u32[]{:S(2)}, u32[]{:S(2)}) collective-permute-start(bf16[32,3200]{1,0:T(8,128)(2,1)S(1)} %add_pair.17), channel_id=1, source_target_pairs={{32,64},{48,67},{35,80},{51,83},{33,65},{49,66},{34,81},{50,82},{3... | collective-permute-start | bytes 614408 | tf_op jit(solution)/shard_map/ppermute | solution.py:258
  235.4 6.2 %collective-permute-start.19 = (bf16[32,3200]{1,0:T(8,128)(2,1)S(1)}, bf16[32,3200]{1,0:T(8,128)(2,1)S(1)}, u32[]{:S(2)}, u32[]{:S(2)}) collective-permute-start(bf16[32,3200]{1,0:T(8,128)(2,1)S(1)} %add_pair.18), channel_id=1, source_target_pairs={{64,96},{80,99},{67,112},{83,115},{65,97},{81,98},{66,113},{82,114... | collective-permute-start | bytes 614408 | tf_op jit(solution)/shard_map/ppermute | solution.py:258
  246.4 0.7 collective-permute-start.20
  252.3 0.7 collective-permute-start.21
  257.9 0.7 collective-permute-start.22
  263.4 0.7 collective-permute-start.23
  269.1 0.7 collective-permute-start.24
  274.6 0.7 collective-permute-start.25
  280.1 0.7 collective-permute-start.26
  285.8 0.7 collective-permute-start.27
  291.3 0.7 collective-permute-start.28
  296.9 0.7 collective-permute-start.29
  302.6 0.7 collective-permute-start.30
  308.1 0.7 collective-permute-start.31
  311.5 205.0 %copy-start.9 = (bf16[16,200,256]{2,1,0:T(8,128)(2,1)S(1)}, bf16[16,200,256]{2,1,0:T(8,128)(2,1)}, u32[]{:S(2)}) copy-start(bf16[16,200,256]{2,1,0:T(8,128)(2,1)} %get-tuple-element.59) | copy-start | bytes 4915204
  313.8 2.0 collective-permute-start.32
  314.5 1.4 collective-permute-start.34
  315.2 0.7 collective-permute-start.33
  316.0 0.7 collective-permute-start.35
  316.7 0.7 collective-permute-start.36
  317.4 199.1 %collective-permute-start.37 = (bf16[16,3200]{1,0:T(8,128)(2,1)S(1)}, bf16[16,3200]{1,0:T(8,128)(2,1)S(1)}, u32[]{:S(2)}, u32[]{:S(2)}) collective-permute-start(bf16[16,3200]{1,0:T(8,128)(2,1)S(1)} %add.56), channel_id=1, source_target_pairs={{480,0},{224,256},{96,128},{352,384},{32,64},{288,320},{160,192},{... | collective-permute-start | bytes 307208 | tf_op jit(solution)/shard_map/ppermute | solution.py:279
Sparse Core Ops, SparseCore 0:
  26.8 76.1 all-gather.33
